TPU v7x, 32 devices: a whole 2x2x4 slice. The times are simulated.
32 devices in a mesh: section: 2 (over x), dp: 16 (over z, y, core).
Axes of the slice: x: 2, y: 2, z: 4, core: 2. Of those that a mesh axis runs over, the one named last changes fastest.
Arguments:
- tokens: bfloat16 [2, 8192, 768], P(None, 'dp'), may hold values from -6 to 6
- segments: int32 [2, 8192], P(None, 'dp'), may hold values from 0 to 31, never falling along the last dimension, each value on 1 to 512 neighbouring positions
- cotangent: float32 [2, 8192, 768], P(None, 'dp'), may hold values from -6 to 6
- ln1_gain: bfloat16 [2, 768], P('section', 'dp'), may hold values from 0.099609375 to 1.8984375
- ln1_bias: bfloat16 [2, 768], P('section', 'dp'), may hold values from -3 to 3
- ln2_gain: bfloat16 [2, 768], P('section', 'dp'), may hold values from 0.099609375 to 1.8984375
- ln2_bias: bfloat16 [2, 768], P('section', 'dp'), may hold values from -3 to 3
- qkv_weight: bfloat16 [2, 768, 2304], P('section', 'dp'), may hold values from -0.21875 to 0.21875
- qkv_bias: bfloat16 [2, 2304], P('section', 'dp'), may hold values from -3 to 3
- out_weight: bfloat16 [2, 768, 768], P('section', 'dp'), may hold values from -0.875 to 0.875
- out_bias: bfloat16 [2, 768], P('section', 'dp'), may hold values from -3 to 3
- up_weight: bfloat16 [2, 768, 3072], P('section', 'dp'), may hold values from -0.21875 to 0.21875
- up_bias: bfloat16 [2, 3072], P('section', 'dp'), may hold values from -3 to 3
- down_weight: bfloat16 [2, 3072, 768], P('section', 'dp'), may hold values from -0.15625 to 0.15625
- down_bias: bfloat16 [2, 768], P('section', 'dp'), may hold values from -3 to 3
Outputs:
- section_outputs: bfloat16 [2, 2, 8192, 768], P('section', None, 'dp')
- input_grads: float32 [2, 2, 8192, 768], P('section', None, 'dp')
- ln1_gain_grad: float32 [2, 768], P('section', 'dp')
- ln1_bias_grad: float32 [2, 768], P('section', 'dp')
- ln2_gain_grad: float32 [2, 768], P('section', 'dp')
- ln2_bias_grad: float32 [2, 768], P('section', 'dp')
- qkv_weight_grad: float32 [2, 768, 2304], P('section', 'dp')
- qkv_bias_grad: float32 [2, 2304], P('section', 'dp')
- out_weight_grad: float32 [2, 768, 768], P('section', 'dp')
- out_bias_grad: float32 [2, 768], P('section', 'dp')
- up_weight_grad: float32 [2, 768, 3072], P('section', 'dp')
- up_bias_grad: float32 [2, 3072], P('section', 'dp')
- down_weight_grad: float32 [2, 3072, 768], P('section', 'dp')
- down_bias_grad: float32 [2, 768], P('section', 'dp')
Inputs may be any that keep to these rules, and one draw needn't show every extreme that they name: `segments`: along each micro-batch row the segment number never falls; each document covers 1 to 512 consecutive positions, one exactly 512, and every number of 0 to 31 occurs.
All inputs are finite; a program needn't handle non-finite values.
Results may differ from a plain program's by a relative error of at most 0.014.
Values may be sent and summed in bfloat16 or wider, within the bound.
No kernel may reach another device: no remote copies, remote signals or barrier semaphores. Data moves between devices by JAX's collectives and lax.ppermute only.
A program may use at most 320 MiB of HBM per device.

v0:
```python
from functools import partial

import jax
import jax.numpy as jnp
from jax import lax
from jax.sharding import PartitionSpec as P

D = 768
HEADS = 12
HEAD_DIM = 64
FF = 3072
ROT = 16


def passed_along(block, axis, distance):
    devices = range(lax.axis_size(axis))
    route = [(i - distance, i) for i in devices if i - distance in devices]
    return lax.ppermute(block, axis, route)


def layer_norm(values, norm_gain, norm_shift):
    center = values - jnp.mean(values, axis=-1, keepdims=True)
    spread = jnp.mean(center * center, axis=-1, keepdims=True)
    return center * lax.rsqrt(spread + 1e-05) * norm_gain + norm_shift


def positions(seg_row):
    index_row = jnp.arange(seg_row.shape[0], dtype=jnp.int32)
    starts = jnp.concatenate([jnp.ones((1,), dtype=jnp.bool_), seg_row[1:] != seg_row[:-1]])
    begin_at = lax.cummax(jnp.where(starts, index_row, jnp.zeros_like(index_row)), axis=0)
    return index_row - begin_at


def rotate(heads_in, pos_row):
    half_rot = ROT // 2
    frequency = 10000.0 ** (-2.0 * jnp.arange(half_rot, dtype=jnp.float32) / ROT)
    angles = pos_row.astype(jnp.float32)[:, None] * frequency[None, :]
    cosine = jnp.cos(angles)[:, None, :]
    sine_part = jnp.sin(angles)[:, None, :]
    front_half = heads_in[..., :half_rot]
    back_part = heads_in[..., half_rot:ROT]
    return jnp.concatenate(
        [
            front_half * cosine - back_part * sine_part,
            back_part * cosine + front_half * sine_part,
            heads_in[..., ROT:],
        ],
        axis=-1,
    )


def attend_forward(queries, key_heads, values, seg_row):
    length = queries.shape[0]
    block_rows = min(512, length)
    index_row = jnp.arange(length, dtype=jnp.int32)
    score_scale = HEAD_DIM ** (-0.5)

    def one_block(block_index):
        start_row = block_index * block_rows
        rows_at = start_row + jnp.arange(block_rows, dtype=jnp.int32)
        allowed = (rows_at[:, None] >= index_row[None, :]) & (seg_row[:, None] == seg_row[None, :])
        raw_score = (
            jnp.einsum("qhd,khd->hqk", queries, key_heads, preferred_element_type=jnp.float32)
            * score_scale
        )
        masked_score = jnp.where(allowed[None], raw_score, -1e30)
        row_peak = jnp.max(masked_score, axis=-1)
        shifted = jnp.exp(masked_score - row_peak[..., None])
        row_total = jnp.sum(shifted, axis=-1)
        attn_prob = (shifted / row_total[..., None]).astype(jnp.bfloat16)
        context = jnp.einsum("hqk,khd->qhd", attn_prob, values, preferred_element_type=jnp.float32)
        return (context, row_peak + jnp.log(row_total))

    context, log_total = lax.map(one_block, jnp.arange(length // block_rows, dtype=jnp.int32))
    return (context.reshape(length, D), log_total)


def attend_backward(queries, key_heads, values, seg_row, log_total, grad_context):
    length = queries.shape[0]
    block_rows = min(512, length)
    index_row = jnp.arange(length, dtype=jnp.int32)
    score_scale = HEAD_DIM ** (-0.5)

    def one_block(carried, pieces):
        grad_keys, grad_values = carried
        block_index, block_total = pieces
        start_row = block_index * block_rows
        rows_at = start_row + jnp.arange(block_rows, dtype=jnp.int32)
        allowed = (rows_at[:, None] >= index_row[None, :]) & (seg_row[:, None] == seg_row[None, :])
        raw_score = (
            jnp.einsum("qhd,khd->hqk", queries, key_heads, preferred_element_type=jnp.float32)
            * score_scale
        )
        attn_prob = jnp.exp(jnp.where(allowed[None], raw_score - block_total[..., None], -1e30))
        prob_low = attn_prob.astype(jnp.bfloat16)
        grad_values = grad_values + jnp.einsum(
            "hqk,qhd->khd", prob_low, grad_context, preferred_element_type=jnp.float32
        )
        grad_prob = jnp.einsum(
            "qhd,khd->hqk", grad_context, values, preferred_element_type=jnp.float32
        )
        inner_sum = jnp.sum(attn_prob * grad_prob, axis=-1, keepdims=True)
        grad_score = (attn_prob * (grad_prob - inner_sum)).astype(jnp.bfloat16)
        grad_query = (
            jnp.einsum("hqk,khd->qhd", grad_score, key_heads, preferred_element_type=jnp.float32)
            * score_scale
        )
        grad_keys = (
            grad_keys
            + jnp.einsum("hqk,qhd->khd", grad_score, queries, preferred_element_type=jnp.float32)
            * score_scale
        )
        return ((grad_keys, grad_values), grad_query)

    zero_heads = jnp.zeros(key_heads.shape, jnp.float32)
    (grad_keys, grad_values), grad_query = lax.scan(
        one_block,
        (zero_heads, zero_heads),
        (jnp.arange(length // block_rows, dtype=jnp.int32), log_total),
    )
    return (grad_query.reshape(key_heads.shape), grad_keys, grad_values)


def blank_saved(length):
    block_rows = min(512, length)
    flat_zero = jnp.zeros((length, D), jnp.bfloat16)
    head_zero = jnp.zeros((length, HEADS, HEAD_DIM), jnp.bfloat16)
    return (
        flat_zero,
        flat_zero,
        flat_zero,
        head_zero,
        head_zero,
        head_zero,
        flat_zero,
        jnp.zeros((length // block_rows, HEADS, block_rows), jnp.float32),
        jnp.zeros((length, FF), jnp.float32),
    )


def run_forward(source, seg_row, weights):
    (
        gain_one,
        shift_one,
        gain_two,
        shift_two,
        w_qkv,
        b_qkv,
        w_out,
        b_out,
        w_up,
        b_up,
        w_down,
        b_down,
    ) = weights
    length = source.shape[0]
    rows_in = source.astype(jnp.float32)
    normed = layer_norm(
        rows_in, gain_one.astype(jnp.float32), shift_one.astype(jnp.float32)
    ).astype(jnp.bfloat16)
    joined_qkv = jnp.dot(normed, w_qkv, preferred_element_type=jnp.float32) + b_qkv.astype(
        jnp.float32
    )
    pos_row = positions(seg_row)
    queries = rotate(joined_qkv[:, :D].reshape(length, HEADS, HEAD_DIM), pos_row).astype(
        jnp.bfloat16
    )
    key_heads = rotate(joined_qkv[:, D : 2 * D].reshape(length, HEADS, HEAD_DIM), pos_row).astype(
        jnp.bfloat16
    )
    values = joined_qkv[:, 2 * D :].reshape(length, HEADS, HEAD_DIM).astype(jnp.bfloat16)
    context, log_total = attend_forward(queries, key_heads, values, seg_row)
    context = context.astype(jnp.bfloat16)
    second = layer_norm(
        rows_in, gain_two.astype(jnp.float32), shift_two.astype(jnp.float32)
    ).astype(jnp.bfloat16)
    upward = jnp.dot(second, w_up, preferred_element_type=jnp.float32) + b_up.astype(jnp.float32)
    middle = jax.nn.gelu(upward, approximate=False).astype(jnp.bfloat16)
    branch = (
        jnp.dot(context, w_out, preferred_element_type=jnp.float32)
        + b_out.astype(jnp.float32)
        + jnp.dot(middle, w_down, preferred_element_type=jnp.float32)
        + b_down.astype(jnp.float32)
    )
    return (
        rows_in + branch,
        (source, normed, second, queries, key_heads, values, context, log_total, upward),
    )


def skip_forward(source, seg_row, weights):
    return (jnp.zeros(source.shape, jnp.float32), blank_saved(source.shape[0]))


def run_backward(saved, seg_row, incoming, weights):
    (
        gain_one,
        shift_one,
        gain_two,
        shift_two,
        w_qkv,
        b_qkv,
        w_out,
        b_out,
        w_up,
        b_up,
        w_down,
        b_down,
    ) = weights
    source, normed, second, queries, key_heads, values, context, log_total, upward = saved
    length = source.shape[0]
    rows_in = source.astype(jnp.float32)
    grad_low = incoming.astype(jnp.bfloat16)
    bias_grad = jnp.sum(grad_low.astype(jnp.float32), axis=0)
    out_grad = jnp.einsum("ti,tj->ij", context, grad_low, preferred_element_type=jnp.float32)
    middle, gelu_back = jax.vjp(partial(jax.nn.gelu, approximate=False), upward)
    middle_low = middle.astype(jnp.bfloat16)
    down_grad = jnp.einsum("ti,tj->ij", middle_low, grad_low, preferred_element_type=jnp.float32)
    grad_middle = jnp.einsum("tj,ij->ti", grad_low, w_down, preferred_element_type=jnp.float32)
    grad_up = gelu_back(grad_middle)[0].astype(jnp.bfloat16)
    up_bias_grad = jnp.sum(grad_up.astype(jnp.float32), axis=0)
    up_grad = jnp.einsum("ti,tj->ij", second, grad_up, preferred_element_type=jnp.float32)
    grad_second = jnp.einsum("tj,ij->ti", grad_up, w_up, preferred_element_type=jnp.float32)
    grad_context = (
        jnp.einsum("tj,ij->ti", grad_low, w_out, preferred_element_type=jnp.float32)
        .astype(jnp.bfloat16)
        .reshape(length, HEADS, HEAD_DIM)
    )
    grad_query, grad_key, grad_value = attend_backward(
        queries, key_heads, values, seg_row, log_total, grad_context
    )
    pos_row = positions(seg_row)
    _, turn_back = jax.vjp(
        lambda heads_in: rotate(heads_in, pos_row), jnp.zeros(queries.shape, jnp.float32)
    )
    grad_joined = jnp.concatenate(
        [
            turn_back(grad_query)[0].reshape(length, D),
            turn_back(grad_key)[0].reshape(length, D),
            grad_value.reshape(length, D),
        ],
        axis=1,
    ).astype(jnp.bfloat16)
    joined_bias_grad = jnp.sum(grad_joined.astype(jnp.float32), axis=0)
    joined_grad = jnp.einsum("ti,tj->ij", normed, grad_joined, preferred_element_type=jnp.float32)
    grad_normed = jnp.einsum("tj,ij->ti", grad_joined, w_qkv, preferred_element_type=jnp.float32)
    _, norm_back_one = jax.vjp(
        layer_norm, rows_in, gain_one.astype(jnp.float32), shift_one.astype(jnp.float32)
    )
    grad_rows_one, gain_one_grad, shift_one_grad = norm_back_one(grad_normed)
    _, norm_back_two = jax.vjp(
        layer_norm, rows_in, gain_two.astype(jnp.float32), shift_two.astype(jnp.float32)
    )
    grad_rows_two, gain_two_grad, shift_two_grad = norm_back_two(grad_second)
    grad_in = incoming + grad_rows_one + grad_rows_two
    grads_all = (
        gain_one_grad,
        shift_one_grad,
        gain_two_grad,
        shift_two_grad,
        joined_grad,
        joined_bias_grad,
        out_grad,
        bias_grad,
        up_grad,
        up_bias_grad,
        down_grad,
        bias_grad,
    )
    return (grad_in, grads_all)


def skip_backward(saved, seg_row, incoming, weights):
    return (
        jnp.zeros(incoming.shape, jnp.float32),
        tuple((jnp.zeros(member.shape, jnp.float32) for member in weights)),
    )


def gather_forward(shards):
    (
        gain_one,
        shift_one,
        gain_two,
        shift_two,
        w_qkv,
        b_qkv,
        w_out,
        b_out,
        w_up,
        b_up,
        w_down,
        b_down,
    ) = shards
    gathered = (
        lax.all_gather(gain_one, "dp", axis=1, tiled=True),
        lax.all_gather(shift_one, "dp", axis=1, tiled=True),
        lax.all_gather(gain_two, "dp", axis=1, tiled=True),
        lax.all_gather(shift_two, "dp", axis=1, tiled=True),
        lax.all_gather(w_qkv, "dp", axis=1, tiled=True),
        lax.all_gather(b_qkv, "dp", axis=1, tiled=True),
        lax.all_gather(w_out, "dp", axis=1, tiled=True),
        lax.all_gather(b_out, "dp", axis=1, tiled=True),
        lax.all_gather(w_up, "dp", axis=1, tiled=True),
        lax.all_gather(b_up, "dp", axis=1, tiled=True),
        lax.all_gather(w_down, "dp", axis=1, tiled=True),
        lax.all_gather(b_down, "dp", axis=1, tiled=True),
    )
    return tuple((member[0] for member in gathered))


def gather_backward(shards):
    (
        gain_one,
        shift_one,
        gain_two,
        shift_two,
        w_qkv,
        b_qkv,
        w_out,
        b_out,
        w_up,
        b_up,
        w_down,
        b_down,
    ) = shards
    gathered = (
        lax.all_gather(gain_one, "dp", axis=1, tiled=True),
        lax.all_gather(shift_one, "dp", axis=1, tiled=True),
        lax.all_gather(gain_two, "dp", axis=1, tiled=True),
        lax.all_gather(shift_two, "dp", axis=1, tiled=True),
        lax.all_gather(w_qkv, "dp", axis=1, tiled=True),
        lax.all_gather(b_qkv, "dp", axis=1, tiled=True),
        lax.all_gather(w_out, "dp", axis=1, tiled=True),
        lax.all_gather(b_out, "dp", axis=1, tiled=True),
        lax.all_gather(w_up, "dp", axis=1, tiled=True),
        lax.all_gather(b_up, "dp", axis=1, tiled=True),
        lax.all_gather(w_down, "dp", axis=1, tiled=True),
        lax.all_gather(b_down, "dp", axis=1, tiled=True),
    )
    return tuple((member[0] for member in gathered))


def scatter_final(grads_all):
    (
        g_one,
        g_two,
        g_three,
        g_four,
        g_five,
        g_six,
        g_seven,
        g_eight,
        g_nine,
        g_ten,
        g_eleven,
        g_twelve,
    ) = grads_all
    return (
        lax.psum_scatter(g_one[None], "dp", scatter_dimension=1, tiled=True),
        lax.psum_scatter(g_two[None], "dp", scatter_dimension=1, tiled=True),
        lax.psum_scatter(g_three[None], "dp", scatter_dimension=1, tiled=True),
        lax.psum_scatter(g_four[None], "dp", scatter_dimension=1, tiled=True),
        lax.psum_scatter(g_five[None], "dp", scatter_dimension=1, tiled=True),
        lax.psum_scatter(g_six[None], "dp", scatter_dimension=1, tiled=True),
        lax.psum_scatter(g_seven[None], "dp", scatter_dimension=1, tiled=True),
        lax.psum_scatter(g_eight[None], "dp", scatter_dimension=1, tiled=True),
        lax.psum_scatter(g_nine[None], "dp", scatter_dimension=1, tiled=True),
        lax.psum_scatter(g_ten[None], "dp", scatter_dimension=1, tiled=True),
        lax.psum_scatter(g_eleven[None], "dp", scatter_dimension=1, tiled=True),
        lax.psum_scatter(g_twelve[None], "dp", scatter_dimension=1, tiled=True),
    )


def store_slot(buffer, value, slot_index, active):
    previous = lax.dynamic_index_in_dim(buffer, slot_index, 0, keepdims=False)
    return lax.dynamic_update_index_in_dim(
        buffer, jnp.where(active, value, previous), slot_index, 0
    )


def body(
    tokens,
    segments,
    cotangent,
    ln1_gain,
    ln1_bias,
    ln2_gain,
    ln2_bias,
    qkv_weight,
    qkv_bias,
    out_weight,
    out_bias,
    up_weight,
    up_bias,
    down_weight,
    down_bias,
):
    shards = (
        ln1_gain,
        ln1_bias,
        ln2_gain,
        ln2_bias,
        qkv_weight,
        qkv_bias,
        out_weight,
        out_bias,
        up_weight,
        up_bias,
        down_weight,
        down_bias,
    )
    section_index = lax.axis_index("section")
    is_first = section_index == 0
    micro_count = tokens.shape[0]
    length = tokens.shape[1]
    group_size = lax.axis_size("dp")
    buffers = tuple(
        (jnp.zeros((micro_count,) + member.shape, member.dtype) for member in blank_saved(length))
    )
    outputs = jnp.zeros((micro_count, length, D), jnp.bfloat16)
    in_grads = jnp.zeros((micro_count, length, D), jnp.float32)
    totals = tuple(
        (
            jnp.zeros((member.shape[1] * group_size,) + member.shape[2:], jnp.float32)
            for member in shards
        )
    )
    shares = tuple((jnp.zeros(member.shape, jnp.float32) for member in shards))
    arrived = jnp.zeros((length, D), jnp.bfloat16)
    returned = jnp.zeros((length, D), jnp.bfloat16)
    for moment in range(micro_count + 2):
        if moment <= micro_count:
            weights = gather_forward(shards)
            active = jnp.where(is_first, moment < micro_count, moment >= 1)
            slot_index = jnp.clip(moment - section_index, 0, micro_count - 1)
            source = jnp.where(is_first, tokens[min(moment, micro_count - 1)], arrived)
            seg_row = lax.dynamic_index_in_dim(segments, slot_index, 0, keepdims=False)
            result, saved = lax.cond(active, run_forward, skip_forward, source, seg_row, weights)
            buffers = tuple(
                (
                    store_slot(buffer, value, slot_index, active)
                    for buffer, value in zip(buffers, saved)
                )
            )
            sent_rows = result.astype(jnp.bfloat16)
            outputs = store_slot(outputs, sent_rows, slot_index, active)
            if moment < micro_count:
                arrived = passed_along(sent_rows, "section", 1)
        if moment >= 1:
            weights = gather_backward(shards)
            active = jnp.where(is_first, moment >= 2, moment <= micro_count)
            slot_index = jnp.clip(moment - 2 + section_index, 0, micro_count - 1)
            seg_row = lax.dynamic_index_in_dim(segments, slot_index, 0, keepdims=False)
            incoming = jnp.where(
                is_first,
                returned.astype(jnp.float32),
                lax.dynamic_index_in_dim(cotangent, slot_index, 0, keepdims=False),
            )
            saved = tuple(
                (
                    lax.dynamic_index_in_dim(buffer, slot_index, 0, keepdims=False)
                    for buffer in buffers
                )
            )
            grad_in, grads_all = lax.cond(
                active, run_backward, skip_backward, saved, seg_row, incoming, weights
            )
            in_grads = store_slot(in_grads, grad_in, slot_index, active)
            totals = tuple((total_sum + piece for total_sum, piece in zip(totals, grads_all)))
            if moment <= micro_count:
                returned = passed_along(grad_in.astype(jnp.bfloat16), "section", -1)
    shares = scatter_final(totals)
    return (outputs[None], in_grads[None]) + tuple(shares)


def solution(mesh):
    placed = (
        P(None, "dp", None),
        P(None, "dp"),
        P(None, "dp", None),
        P("section", "dp"),
        P("section", "dp"),
        P("section", "dp"),
        P("section", "dp"),
        P("section", "dp", None),
        P("section", "dp"),
        P("section", "dp", None),
        P("section", "dp"),
        P("section", "dp", None),
        P("section", "dp"),
        P("section", "dp", None),
        P("section", "dp"),
    )
    return jax.shard_map(
        body,
        mesh=mesh,
        in_specs=placed,
        out_specs=(
            P("section", None, "dp", None),
            P("section", None, "dp", None),
            P("section", "dp"),
            P("section", "dp"),
            P("section", "dp"),
            P("section", "dp"),
            P("section", "dp", None),
            P("section", "dp"),
            P("section", "dp", None),
            P("section", "dp"),
            P("section", "dp", None),
            P("section", "dp"),
            P("section", "dp", None),
            P("section", "dp"),
        ),
        check_vma=False,
    )
```

profile of v0, /device:TPU:1, one launch (start us, length us, event | category | flops | bytes accessed | tf_op | source)
XLA Modules:
  0.0 1604.6 jit_solution(11363951553600605048)
XLA Ops:
  20.1 58.3 %all-reduce.26 = (bf16[768]{0:T(1024)(128)(2,1)S(1)}, bf16[768]{0:T(1024)(128)(2,1)S(1)}, bf16[768]{0:T(1024)(128)(2,1)S(1)}, bf16[768]{0:T(1024)(128)(2,1)S(1)}...) all-reduce(bf16[768]{0:T(1024)(128)(2,1)S(1)} %dynamic-update-slice, ...), channel_id=1, replica_groups=mesh['section'=2,'dp'=16] {'dp'}, use_global_device_ids=true, to_apply=%add.18 | all-reduce | flops 9984 | bytes 39936 | tf_op jit(solution)/shard_map/squeeze | solution.py:309
  88.3 11.4 all-gather.5.cloned.1.call-done
  99.8 54.7 %all-gather.7.cloned.1.call-done = bf16[1,768,3072]{2,1,0:T(8,128)(2,1)} async-done(((bf16[1,48,3072]{2,1,0:T(8,128)(2,1)}), bf16[1,768,3072]{2,1,0:T(8,128)(2,1)}) %all-gather.7.cloned.1.call-update) | async-done | bytes 4718608 | tf_op jit(solution)/shard_map/all_gather | solution.py:304
  154.5 54.1 %all-gather.11.cloned.1.call-done = bf16[1,3072,768]{2,1,0:T(8,128)(2,1)} async-done(((bf16[1,192,768]{2,1,0:T(8,128)(2,1)}), bf16[1,3072,768]{2,1,0:T(8,128)(2,1)}) %all-gather.11.cloned.1.call-update) | async-done | bytes 4718608 | tf_op jit(solution)/shard_map/all_gather | solution.py:306
  208.8 64.7 %conditional.4 = (bf16[512,768]{1,0:T(8,128)(2,1)}, bf16[512,768]{1,0:T(8,128)(2,1)}, bf16[512,768]{1,0:T(8,128)(2,1)}, bf16[512,12,64]{0,2,1:T(8,128)(2,1)S(1)}...) conditional(s32[]{:T(128)} %convert_element_type.568, () %tuple.87, ...), branch_computations={%region_0.1_spmd, %region_1.8_spmd} | conditional | flops 8211214336 | bytes 153318576 | solution.py:439
  245.4 19.0 %fusion.13 = f32[512,768]{1,0:T(8,128)S(1)} fusion(bf16[3072,768]{1,0:T(8,128)(2,1)} %get-tuple-element.903, f32[512,3072]{1,0:T(8,128)} %convolution_add_fusion.1), kind=kOutput, calls=%fused_computation.27 | convolution fusion | flops 2518155264 | bytes 12582912 | tf_op jit(solution)/shard_map/cond/branch_1_fun/dot_general | solution.py:182
  357.3 27.1 %conditional.6 = (f32[512,768]{1,0:T(8,128)}, f32[768]{0:T(1024)S(1)}, f32[768]{0:T(1024)S(1)}, f32[768]{0:T(1024)}, f32[768]{0:T(1024)}, /*index=5*/f32[768,230...) conditional(s32[]{:T(128)} %convert_element_type.589, () %tuple.91, ...), branch_computations={%region_22.23_spmd, %region_23.40_spmd} | conditional | flops 16725800960 | bytes 410042400 | solution.py:466
  387.6 19.4 %fusion.329 = f32[512,768]{1,0:T(8,128)S(1)} fusion(f32[512,3072]{1,0:T(8,128)} %get-tuple-element.1286, f32[3072]{0:T(1024)} %convert_element_type.585, bf16[1,3072,768]{2,1,0:T(8,128)(2,1)} %all-gather.11.cloned.1.call-done), kind=kOutput, calls=%fused_computation.527 | convolution fusion | flops 2519728128 | bytes 12595200 | tf_op jit(solution)/shard_map/cond/branch_1_fun/dot_general | solution.py:182
  412.2 75.7 %collective-permute-start.1 = (bf16[512,768]{1,0:T(8,128)(2,1)}, bf16[512,768]{1,0:T(8,128)(2,1)S(1)}, u32[]{:S(2)}, u32[]{:S(2)}) collective-permute-start(bf16[512,768]{1,0:T(8,128)(2,1)} %get-tuple-element.1284), channel_id=1, source_target_pairs={{0,16},{1,17},{2,18},{3,19},{4,20},{5,21},{6,22},{7,23},{8,24},{9,... | collective-permute-start | bytes 2359304 | tf_op jit(solution)/shard_map/ppermute | solution.py:18
  505.2 14.4 conditional.5
  556.5 14.2 fusion.294
  608.1 84.9 %collective-permute-done.3 = bf16[512,768]{1,0:T(8,128)(2,1)S(1)} collective-permute-done((bf16[512,768]{1,0:T(8,128)(2,1)S(1)}, bf16[512,768]{1,0:T(8,128)(2,1)S(1)}, u32[]{:S(2)}, u32[]{:S(2)}) %collective-permute-start.3) | collective-permute-done | bytes 786464 | tf_op jit(solution)/shard_map/ppermute | solution.py:18
  693.2 98.6 %conditional.7 = (f32[512,768]{1,0:T(8,128)}, f32[768]{0:T(1024)}, f32[768]{0:T(1024)}, f32[768]{0:T(1024)}, f32[768]{0:T(1024)}, /*index=5*/f32[768,2304]{1,0:T...) conditional(s32[]{:T(128)} %convert_element_type.568, () %tuple.93, ...), branch_computations={%region_49.50_spmd, %region_50.67_spmd} | conditional | flops 16725800960 | bytes 460337120 | solution.py:466
  697.6 18.9 %convert_reduce_fusion.6 = (f32[3072]{0:T(1024)}, bf16[512,3072]{1,0:T(8,128)(2,1)S(1)}, f32[512,3072]{1,0:T(8,128)}) fusion(f32[2,512,3072]{2,1,0:T(8,128)S(1)} %get-tuple-element.955, s32[]{:T(128)} %get-tuple-element.945, bf16[512,768]{1,0:T(8,128)(2,1)S(1)} %get-tuple-element.1182, bf16[3072,768]{1,0:T(8,128)(2,1)S(1)} %get-tuple-element.956), kind=kOutput, calls=%fused_computation.346 | convolution fusion | flops 2532307968 | bytes 21245956 | tf_op jit(solution)/shard_map/cond/branch_1_fun/tj,ij->ti/dot_general | solution.py:219
  870.9 34.1 %reduce-scatter.36.cloned.1.call-done = f32[48,1]{1,0:T(8,128)} async-done(((f32[768,1]{1,0:T(8,128)}), f32[48,1]{1,0:T(8,128)}) %reduce-scatter.36.cloned.1.call-update) | async-done | bytes 208
  906.3 56.8 %reduce-scatter.38.cloned.1.call-done = f32[48,1]{1,0:T(8,128)} async-done(((f32[768,1]{1,0:T(8,128)}), f32[48,1]{1,0:T(8,128)}) %reduce-scatter.38.cloned.1.call-update) | async-done | bytes 208
  964.5 57.2 %reduce-scatter.40.cloned.1.call-done = f32[48,1]{1,0:T(8,128)} async-done(((f32[768,1]{1,0:T(8,128)}), f32[48,1]{1,0:T(8,128)}) %reduce-scatter.40.cloned.1.call-update) | async-done | bytes 208
  1022.9 56.8 %reduce-scatter.44.cloned.1.call-done = f32[48,1]{1,0:T(8,128)} async-done(((f32[768,1]{1,0:T(8,128)}), f32[48,1]{1,0:T(8,128)}) %reduce-scatter.44.cloned.1.call-update) | async-done | bytes 208
  1080.6 60.2 %reduce-scatter.42.cloned.1.call-done = f32[144,1]{1,0:T(8,128)} async-done(((f32[2304,1]{1,0:T(8,128)}), f32[144,1]{1,0:T(8,128)}) %reduce-scatter.42.cloned.1.call-update) | async-done | bytes 592
  1142.3 61.3 %reduce-scatter.46.cloned.1.call-done = f32[192,1]{1,0:T(8,128)} async-done(((f32[3072,1]{1,0:T(8,128)}), f32[192,1]{1,0:T(8,128)}) %reduce-scatter.46.cloned.1.call-update) | async-done | bytes 784
  1205.2 64.8 %reduce-scatter.28.cloned.1.call-done = f32[1,48,768]{2,1,0:T(8,128)} async-done(((f32[1,768,768]{2,1,0:T(8,128)}), f32[1,48,768]{2,1,0:T(8,128)}) %reduce-scatter.28.cloned.1.call-update) | async-done | bytes 147472 | tf_op jit(solution)/shard_map/reduce_scatter | solution.py:366
  1270.0 95.4 %reduce-scatter.26.cloned.1.call-done = f32[1,48,2304]{2,1,0:T(8,128)} async-done(((f32[1,768,2304]{2,1,0:T(8,128)}), f32[1,48,2304]{2,1,0:T(8,128)}) %reduce-scatter.26.cloned.1.call-update) | async-done | bytes 442384 | tf_op jit(solution)/shard_map/reduce_scatter | solution.py:364
  1365.4 115.7 %reduce-scatter.30.cloned.1.call-done = f32[1,48,3072]{2,1,0:T(8,128)} async-done(((f32[1,768,3072]{2,1,0:T(8,128)}), f32[1,48,3072]{2,1,0:T(8,128)}) %reduce-scatter.30.cloned.1.call-update) | async-done | bytes 589840 | tf_op jit(solution)/shard_map/reduce_scatter | solution.py:368
  1481.1 116.2 %reduce-scatter.32.cloned.1.call-done = f32[1,192,768]{2,1,0:T(8,128)} async-done(((f32[1,3072,768]{2,1,0:T(8,128)}), f32[1,192,768]{2,1,0:T(8,128)}) %reduce-scatter.32.cloned.1.call-update) | async-done | bytes 589840 | tf_op jit(solution)/shard_map/reduce_scatter | solution.py:370
  (632 shorter events, 444.3 us)
Async XLA Ops:
  7.2 81.2 %all-gather.9.cloned.1.call-start = ((), (), s32[]{:S(2)}) async-start(), calls=%async_computation.13 | async-start | bytes 1253376 | tf_op jit(solution)/shard_map/all_gather | solution.py:302
  7.9 91.9 %all-gather.5.cloned.1.call-start = ((), (), s32[]{:S(2)}) async-start(), calls=%async_computation.11 | async-start | bytes 3760128 | tf_op jit(solution)/shard_map/all_gather | solution.py:300
  8.7 145.8 %all-gather.7.cloned.1.call-start = ((), (), s32[]{:S(2)}) async-start(), calls=%async_computation.12 | async-start | bytes 5013504 | tf_op jit(solution)/shard_map/all_gather | solution.py:304
  9.4 199.2 %all-gather.11.cloned.1.call-start = ((), (), s32[]{:S(2)}) async-start(), calls=%async_computation.14 | async-start | bytes 5013504 | tf_op jit(solution)/shard_map/all_gather | solution.py:306
  10.0 859.6 %reduce-scatter.34.cloned.1.call-start = ((), (), s32[]{:S(2)}) async-start(), calls=%async_computation.19 | async-start | bytes 417792
  78.4 130.4 %copy-start.121 = (bf16[768]{0:T(1024)(128)(2,1)}, bf16[768]{0:T(1024)(128)(2,1)S(1)}, u32[]{:S(2)}) copy-start(bf16[768]{0:T(1024)(128)(2,1)S(1)} %get-tuple-element.1162) | copy-start | bytes 4612
  82.6 214.5 %copy-start.106 = (f32[768]{0:T(1024)}, f32[768]{0:T(1024)S(1)}, u32[]{:S(2)}) copy-start(f32[768]{0:T(1024)S(1)} %convert_element_type.570) | copy-start | bytes 9220
  273.5 21.6 %collective-permute-start = (bf16[512,768]{1,0:T(8,128)(2,1)}, bf16[512,768]{1,0:T(8,128)(2,1)S(1)}, u32[]{:S(2)}, u32[]{:S(2)}) collective-permute-start(bf16[512,768]{1,0:T(8,128)(2,1)} %get-tuple-element.1020), channel_id=1, source_target_pairs={{0,16},{1,17},{2,18},{3,19},{4,20},{5,21},{6,22},{7,23},{8,24},{9,... | collective-permute-start | bytes 2359304 | tf_op jit(solution)/shard_map/ppermute | solution.py:18
  386.1 109.0 %collective-permute-start.2 = (bf16[512,768]{1,0:T(8,128)(2,1)S(1)}, bf16[512,768]{1,0:T(8,128)(2,1)S(1)}, u32[]{:S(2)}, u32[]{:S(2)}) collective-permute-start(bf16[512,768]{1,0:T(8,128)(2,1)S(1)} %convert_element_type.592), channel_id=1, source_target_pairs={{16,0},{17,1},{18,2},{19,3},{20,4},{21,5},{22,6},{23,7},{24,8},{25... | collective-permute-start | bytes 2359304 | tf_op jit(solution)/shard_map/ppermute | solution.py:18
  412.2 92.1 %collective-permute-start.1 = (bf16[512,768]{1,0:T(8,128)(2,1)}, bf16[512,768]{1,0:T(8,128)(2,1)S(1)}, u32[]{:S(2)}, u32[]{:S(2)}) collective-permute-start(bf16[512,768]{1,0:T(8,128)(2,1)} %get-tuple-element.1284), channel_id=1, source_target_pairs={{0,16},{1,17},{2,18},{3,19},{4,20},{5,21},{6,22},{7,23},{8,24},{9,... | collective-permute-start | bytes 2359304 | tf_op jit(solution)/shard_map/ppermute | solution.py:18
  556.5 136.7 %copy-start.1 = (f32[2,512,3072]{2,1,0:T(8,128)}, f32[2,512,3072]{2,1,0:T(8,128)S(1)}, u32[]{:S(2)}) copy-start(f32[2,512,3072]{2,1,0:T(8,128)S(1)} %bitcast_dynamic-update-slice_fusion) | copy-start | bytes 37748740
  598.7 94.3 %collective-permute-start.3 = (bf16[512,768]{1,0:T(8,128)(2,1)S(1)}, bf16[512,768]{1,0:T(8,128)(2,1)S(1)}, u32[]{:S(2)}, u32[]{:S(2)}) collective-permute-start(bf16[512,768]{1,0:T(8,128)(2,1)S(1)} %get-tuple-element.1185), channel_id=1, source_target_pairs={{16,0},{17,1},{18,2},{19,3},{20,4},{21,5},{22,6},{23,7},{24,8},{25... | collective-permute-start | bytes 2359304 | tf_op jit(solution)/shard_map/ppermute | solution.py:18
  793.6 111.4 %reduce-scatter.36.cloned.1.call-start = ((), (), s32[]{:S(2)}) async-start(), calls=%async_computation.20 | async-start | bytes 417792
  795.3 167.8 %reduce-scatter.38.cloned.1.call-start = ((), (), s32[]{:S(2)}) async-start(), calls=%async_computation.21 | async-start | bytes 417792
  797.0 224.6 %reduce-scatter.40.cloned.1.call-start = ((), (), s32[]{:S(2)}) async-start(), calls=%async_computation.22 | async-start | bytes 417792
  798.7 281.1 %reduce-scatter.44.cloned.1.call-start = ((), (), s32[]{:S(2)}) async-start(), calls=%async_computation.24 | async-start | bytes 417792
  800.4 340.4 %reduce-scatter.42.cloned.1.call-start = ((), (), s32[]{:S(2)}) async-start(), calls=%async_computation.23 | async-start | bytes 1253376
  802.6 401.0 %reduce-scatter.46.cloned.1.call-start = ((), (), s32[]{:S(2)}) async-start(), calls=%async_computation.25 | async-start | bytes 1671168
  805.1 464.9 %reduce-scatter.28.cloned.1.call-start = ((), (), s32[]{:S(2)}) async-start(), calls=%async_computation.16 | async-start | bytes 2506752 | tf_op jit(solution)/shard_map/reduce_scatter | solution.py:366
  809.6 555.9 %reduce-scatter.26.cloned.1.call-start = ((), (), s32[]{:S(2)}) async-start(), calls=%async_computation.15 | async-start | bytes 7520256 | tf_op jit(solution)/shard_map/reduce_scatter | solution.py:364
  827.4 653.8 %reduce-scatter.30.cloned.1.call-start = ((), (), s32[]{:S(2)}) async-start(), calls=%async_computation.17 | async-start | bytes 10027008 | tf_op jit(solution)/shard_map/reduce_scatter | solution.py:368
  843.9 753.4 %reduce-scatter.32.cloned.1.call-start = ((), (), s32[]{:S(2)}) async-start(), calls=%async_computation.18 | async-start | bytes 10027008 | tf_op jit(solution)/shard_map/reduce_scatter | solution.py:370
  866.3 731.6 %copy-start.85 = (bf16[1,2,512,768]{3,2,1,0:T(8,128)(2,1)}, bf16[1,2,512,768]{3,2,1,0:T(8,128)(2,1)S(1)}, u32[]{:S(2)}) copy-start(bf16[1,2,512,768]{3,2,1,0:T(8,128)(2,1)S(1)} %bitcast_dynamic-update-slice_fusion.23) | copy-start | bytes 4718596
  1080.6 517.3 %copy-start.148 = (f32[1,48]{1,0:T(1,128)}, f32[1,48]{1,0:T(1,128)S(1)}, u32[]{:S(2)}) copy-start(f32[1,48]{1,0:T(1,128)S(1)} %copy.161) | copy-start | bytes 580
  (149 other events, 2788.4 us)
Sparse Core Ops, SparseCore 0:
  10.3 41.0 all-gather.8
  53.7 46.0 all-gather.4
  102.1 52.3 all-gather.6
  156.6 51.9 all-gather.10
  793.7 52.9 reduce-scatter.33
  850.5 54.4 reduce-scatter.35
  908.5 54.5 reduce-scatter.37
  967.0 54.5 reduce-scatter.39
  1025.1 54.6 reduce-scatter.43
  1083.7 57.0 reduce-scatter.41
  1144.9 58.6 reduce-scatter.45
  1207.8 62.0 reduce-scatter.27
  1275.1 90.2 reduce-scatter.25
  1370.0 111.1 reduce-scatter.29
  1486.2 111.0 reduce-scatter.31
where the time goes:
time: 1610 us; the launch traced here: 1600 us
  waiting for transfers between devices  930 us (58%)
  matrix products  208 us (13%)
  other arithmetic  162 us (10%)
  local copies, waits for them, and re-layouts  135 us (8%)
  starting transfers between devices  80.7 us (5%)
  blocking collectives  58.3 us (4%)
  between operations  17.8 us (1%)
    unnamed x22, waiting for transfers between devices  329 us
    reduce_scatter x1, waiting for transfers between devices, scatter_final(): lax.psum_scatter(g_eleven[None], 'dp', scatter_dimension=1, tiled=True)  116 us
    reduce_scatter x1, waiting for transfers between devices, scatter_final(): lax.psum_scatter(g_nine[None], 'dp', scatter_dimension=1, tiled=True)  116 us
    reduce_scatter x1, waiting for transfers between devices, scatter_final(): lax.psum_scatter(g_five[None], 'dp', scatter_dimension=1, tiled=True)  95.4 us
    ppermute x4, waiting for transfers between devices, passed_along(): return lax.ppermute(block, axis, route)  88 us
    ppermute x4, starting transfers between devices, passed_along(): return lax.ppermute(block, axis, route)  79.9 us
    reduce_scatter x1, waiting for transfers between devices, scatter_final(): lax.psum_scatter(g_seven[None], 'dp', scatter_dimension=1, tiled=True)  64.8 us
    squeeze x1, blocking collectives, gather_forward(): return tuple((member[0] for member in gathered))  58.3 us
  transfers between devices with their start and end apart: 19, of which 15 were waited for; matrix products, arithmetic and copies ran while one was open for 10% of the time, Pallas kernels for 0%

commit v1 on v0

v1 whole, which is shorter than its diff:
```python
import jax
import jax.numpy as jnp
import numpy as np
from jax import lax
from jax.experimental import pallas as pl
from jax.experimental.pallas import tpu as pltpu
from jax.sharding import PartitionSpec as P

D = 768
HEADS = 12
HEAD_DIM = 64
FF = 3072
ROT = 16
HALF = D // 2
PAIR = 2 * HEAD_DIM
PAIRS = HALF // PAIR
FFH = FF // 2
LANES = 2 * D
QKVH = 3 * HALF
PAD = 16
SCALE = HEAD_DIM**-0.5
F32 = jnp.float32
BF16 = jnp.bfloat16

SMALL = (1, 1, 1, 1, 3, 1, 4, 1)


def pick(is_zero, first, second):
    return jnp.where(is_zero, first, second)


def swap_core(block):
    n = lax.axis_size("dp")
    return lax.ppermute(block, "dp", [(i, i ^ 1) for i in range(n)])


def swap_section(block):
    return lax.ppermute(block, "section", [(0, 1), (1, 0)])


def ring_order(chips):
    rows = chips // 2
    return [2 * z for z in range(rows)] + [2 * z + 1 for z in reversed(range(rows))]


class Ring:
    def __init__(self, n):
        self.chips = n // 2
        self.order = ring_order(self.chips)
        place = [0] * self.chips
        for position, chip in enumerate(self.order):
            place[chip] = position
        chip = lax.axis_index("dp") // 2
        self.position = jnp.asarray(place, jnp.int32)[chip]
        self.table = jnp.asarray(self.order, jnp.int32)
        self.right = self.route(1)
        self.left = self.route(-1)

    def route(self, step):
        k = len(self.order)
        pairs = []
        for i in range(k):
            source, target = self.order[i], self.order[(i + step) % k]
            pairs += [(2 * source, 2 * target), (2 * source + 1, 2 * target + 1)]
        return pairs

    def chip_at(self, offset):
        return self.table[lax.rem(self.position + offset + self.chips, self.chips)]

    def gather(self, own):
        (own,) = yield [own]
        found = [(self.chip_at(0), own)]
        reach = self.chips // 2
        ahead = back = own
        for k in range(1, reach):
            ahead = lax.ppermute(ahead, "dp", self.right)
            back = lax.ppermute(back, "dp", self.left)
            ahead, back = yield [ahead, back]
            found += [(self.chip_at(-k), ahead), (self.chip_at(k), back)]
        cut = own.shape[0] // 32 * 16
        ahead = lax.ppermute(ahead[:cut], "dp", self.right)
        back = lax.ppermute(back[cut:], "dp", self.left)
        ahead, back = yield [ahead, back]
        found.append((self.chip_at(reach), jnp.concatenate([ahead, back])))
        return found

    def scatter(self, block_of, rows):
        reach = self.chips // 2
        cut = rows // 32 * 16
        far = block_of(self.chip_at(reach))
        ahead, back = yield [far[:cut], far[cut:]]
        ahead = lax.ppermute(ahead, "dp", self.right)
        back = lax.ppermute(back, "dp", self.left)
        ahead, back = yield [ahead, back]
        own = block_of(self.chip_at(reach - 1))
        ahead = jnp.concatenate([add_low(ahead, own[:cut]), own[cut:]])
        own = block_of(self.chip_at(1 - reach))
        back = jnp.concatenate([own[:cut], add_low(back, own[cut:])])
        for k in range(reach - 2, -1, -1):
            ahead = lax.ppermute(ahead, "dp", self.right)
            back = lax.ppermute(back, "dp", self.left)
            ahead, back = yield [ahead, back]
            if k:
                ahead = add_low(ahead, block_of(self.chip_at(k)))
                back = add_low(back, block_of(self.chip_at(-k)))
        own = block_of(self.chip_at(0))
        return own.astype(F32) + ahead.astype(F32) + back.astype(F32)


class Track:
    def __init__(self):
        self.waiting, self.active, self.held = [], None, []
        self.done = {}

    def push(self, name, steps):
        self.waiting.append((name, steps))

    def step(self, values=()):
        if self.active is None:
            if not self.waiting:
                return values
            self.active = self.waiting.pop(0)
            self.held = next(self.active[1])
        self.held, values = lax.optimization_barrier((self.held, values))
        while True:
            try:
                self.held = self.active[1].send(self.held)
                return values
            except StopIteration as end:
                self.done[self.active[0]] = end.value
                last, self.active = self.held, None
                if not self.waiting:
                    return values
                self.active = self.waiting.pop(0)
                self.held, last = lax.optimization_barrier((next(self.active[1]), last))

    def finish(self, name):
        while name not in self.done:
            self.step()
        return self.done[name]


def add_low(one, two):
    return (one.astype(F32) + two.astype(F32)).astype(BF16)


def same_core(n):
    return [[c + 2 * i for i in range(n // 2)] for c in (0, 1)]


def rotary_tables(segs):
    length = segs.shape[1]
    begin = jnp.sum((segs[:, None, :] < segs[:, :, None]).astype(jnp.int32), axis=2)
    place = (jnp.arange(length, dtype=jnp.int32)[None] - begin).reshape(-1).astype(F32)[:, None]
    half = ROT // 2
    freq = 10000.0 ** (-2.0 * jnp.arange(half, dtype=F32) / ROT)
    rest = jnp.zeros(HEAD_DIM - ROT, F32)
    freq = jnp.tile(jnp.concatenate([freq, freq, rest]), 2)[None]
    first = np.tile(np.arange(HEAD_DIM) < half, 2)[None]
    angle = place * freq
    sin = jnp.sin(angle)
    return jnp.concatenate([jnp.cos(angle), jnp.where(first, -sin, sin)], axis=1), begin.reshape(-1)[:, None]


def turned(x, table, sign):
    lane = lax.rem(lax.broadcasted_iota(jnp.int32, x.shape, 1), HEAD_DIM)
    partner = jnp.where(lane < ROT // 2, pltpu.roll(x, PAIR - ROT // 2, 1), pltpu.roll(x, ROT // 2, 1))
    moved = partner * table[:, PAIR:]
    return x * table[:, :PAIR] + moved if sign > 0 else x * table[:, :PAIR] - moved


def dot_nt(a, b):
    return lax.dot_general(a, b, (((1,), (1,)), ((), ())), preferred_element_type=F32)


def dot_tn(a, b):
    return lax.dot_general(a, b, (((0,), (0,)), ((), ())), preferred_element_type=F32)


def kept(begin, row0, rows, keys):
    key = lax.broadcasted_iota(jnp.int32, (rows, keys), 1)
    row = lax.broadcasted_iota(jnp.int32, (rows, keys), 0) + row0
    return (key <= row) & (key >= begin)


def attend_kernel(joined_ref, table_ref, begin_ref, qkv_ref, ctx_ref, lse_ref):
    length = joined_ref.shape[0]
    chunk = length // 2
    table = table_ref[...]
    qkv_ref[:, :PAIR] = turned(joined_ref[:, :PAIR], table, 1).astype(BF16)
    qkv_ref[:, PAIR : 2 * PAIR] = turned(joined_ref[:, PAIR : 2 * PAIR], table, 1).astype(BF16)
    qkv_ref[:, 2 * PAIR :] = joined_ref[:, 2 * PAIR :].astype(BF16)
    for i in range(2):
        rows, keys = pl.ds(i * chunk, chunk), (i + 1) * chunk
        allowed = kept(begin_ref[rows, :], i * chunk, chunk, keys)
        ctx, lse = [], []
        for h in range(2):
            q = qkv_ref[rows, h * HEAD_DIM : (h + 1) * HEAD_DIM] * jnp.asarray(SCALE, BF16)
            k = qkv_ref[:keys, PAIR + h * HEAD_DIM : PAIR + (h + 1) * HEAD_DIM]
            v = qkv_ref[:keys, 2 * PAIR + h * HEAD_DIM : 2 * PAIR + (h + 1) * HEAD_DIM]
            score = jnp.where(allowed, dot_nt(q, k), -1e30)
            peak = jnp.max(score, axis=1, keepdims=True)
            e = jnp.exp(score - peak)
            total = jnp.sum(e, axis=1, keepdims=True)
            prob = (e * (1.0 / total)).astype(BF16)
            ctx.append(jnp.dot(prob, v, preferred_element_type=F32))
            lse.append(jnp.broadcast_to(peak + jnp.log(total), (chunk, HEAD_DIM)))
        ctx_ref[rows, :] = jnp.concatenate(ctx, axis=1).astype(BF16)
        lse_ref[rows, :] = jnp.concatenate(lse, axis=1)


def attend_back_kernel(qkv_ref, lse_ref, dctx_ref, table_ref, begin_ref, out_ref):
    length = qkv_ref.shape[0]
    chunk = length // 2
    dqs, dks, dvs = [], [], []
    for h in range(2):
        head = slice(h * HEAD_DIM, (h + 1) * HEAD_DIM)
        k_at = slice(PAIR + h * HEAD_DIM, PAIR + (h + 1) * HEAD_DIM)
        v_at = slice(2 * PAIR + h * HEAD_DIM, 2 * PAIR + (h + 1) * HEAD_DIM)
        dq, dk, dv = [], None, None
        for i in (1, 0):
            rows, keys = pl.ds(i * chunk, chunk), (i + 1) * chunk
            allowed = kept(begin_ref[rows, :], i * chunk, chunk, keys)
            q = qkv_ref[rows, head] * jnp.asarray(SCALE, BF16)
            k, v = qkv_ref[:keys, k_at], qkv_ref[:keys, v_at]
            do = dctx_ref[rows, head]
            lse = lse_ref[rows, h * HEAD_DIM : h * HEAD_DIM + 1]
            p = jnp.exp(jnp.where(allowed, dot_nt(q, k) - lse, -1e30))
            part_v = dot_tn(p.astype(BF16), do)
            dp = dot_nt(do, v)
            inner = jnp.sum(p * dp, axis=1, keepdims=True)
            ds = (p * (dp - inner)).astype(BF16)
            dq.append(jnp.dot(ds, k, preferred_element_type=F32) * SCALE)
            part_k = dot_tn(ds, q)
            if dk is None:
                dk, dv = part_k, part_v
            else:
                dk = jnp.concatenate([dk[:chunk] + part_k, dk[chunk:]])
                dv = jnp.concatenate([dv[:chunk] + part_v, dv[chunk:]])
        dqs.append(jnp.concatenate([dq[1], dq[0]]))
        dks.append(dk)
        dvs.append(dv)
    table = table_ref[...]
    out_ref[:, :PAIR] = turned(jnp.concatenate(dqs, axis=1), table, -1).astype(BF16)
    out_ref[:, PAIR : 2 * PAIR] = turned(jnp.concatenate(dks, axis=1), table, -1).astype(BF16)
    out_ref[:, 2 * PAIR :] = jnp.concatenate(dvs, axis=1).astype(BF16)


def kernel_params():
    return pltpu.CompilerParams(vmem_limit_bytes=40 * 1024 * 1024)


def per_pair(length, width):
    return pl.BlockSpec((length, width), lambda s, p: (s, p))


def per_row(length, width):
    return pl.BlockSpec((length, width), lambda s, p: (s, 0))


def attend(joined, table, begin):
    tokens = joined.shape[0]
    length = tokens // 2
    return pl.pallas_call(
        attend_kernel,
        grid=(2, PAIRS),
        in_specs=[per_pair(length, 3 * PAIR), per_row(length, 2 * PAIR), per_row(length, 1)],
        out_specs=[per_pair(length, 3 * PAIR), per_pair(length, PAIR), per_pair(length, PAIR)],
        out_shape=[
            jax.ShapeDtypeStruct((tokens, QKVH), BF16),
            jax.ShapeDtypeStruct((tokens, HALF), BF16),
            jax.ShapeDtypeStruct((tokens, HALF), F32),
        ],
        compiler_params=kernel_params(),
        cost_estimate=pl.CostEstimate(flops=20_000_000_000, bytes_accessed=12_000_000, transcendentals=3_000_000),
    )(joined, table, begin)


def attend_back(qkv, lse, dctx, table, begin):
    tokens = qkv.shape[0]
    length = tokens // 2
    return pl.pallas_call(
        attend_back_kernel,
        grid=(2, PAIRS),
        in_specs=[
            per_pair(length, 3 * PAIR),
            per_pair(length, PAIR),
            per_pair(length, PAIR),
            per_row(length, 2 * PAIR),
            per_row(length, 1),
        ],
        out_specs=per_pair(length, 3 * PAIR),
        out_shape=jax.ShapeDtypeStruct((tokens, QKVH), BF16),
        compiler_params=kernel_params(),
        cost_estimate=pl.CostEstimate(flops=30_000_000_000, bytes_accessed=12_000_000, transcendentals=3_000_000),
    )(qkv, lse, dctx, table, begin)


def normalized(rows):
    center = rows - jnp.mean(rows, axis=-1, keepdims=True)
    spread = jnp.mean(center * center, axis=-1, keepdims=True)
    scale = lax.rsqrt(spread + 1e-05)
    return center * scale, scale


def matmul(a, b):
    return jnp.dot(a, b, preferred_element_type=F32)


def forward_attend(source, weights, table, begin, track):
    normed, scale = normalized(source.astype(F32))
    one = (normed * weights["g1"] + weights["b1"]).astype(BF16)
    two = (normed * weights["g2"] + weights["b2"]).astype(BF16)
    joined = matmul(one, weights["qkv"]) + weights["bqkv"]
    one, two, joined = track.step((one, two, joined))
    qkv, ctx, lse = track.step(attend(joined, table, begin))
    return source, one, two, qkv, ctx, lse


def forward_hidden(saved, weights, track):
    two, ctx = saved[2], saved[4]
    up = matmul(two, weights["up"]) + weights["bup"]
    phi = 0.5 * (1.0 + lax.erf(up * np.float32(0.5**0.5)))
    middle = (up * phi).astype(BF16)
    slope = (phi + up * jnp.exp(-0.5 * up * up) * np.float32((2 * np.pi) ** -0.5)).astype(BF16)
    middle, slope = track.step((middle, slope))
    part = matmul(ctx, weights["out"]) + matmul(middle, weights["down"])
    (part,) = track.step((part,))
    return part, (*saved, middle, slope)


def backward(saved, grad, weights, table, begin, track, send_hidden):
    source, one, two, qkv, ctx, lse, middle, slope = saved
    d_up = (dot_nt(grad, weights["down"]) * slope.astype(F32)).astype(BF16)
    (d_up,) = track.step((d_up,))
    down_grad = dot_tn(middle, grad).astype(BF16)
    up_grad = dot_tn(two, d_up).astype(BF16)
    send_hidden(up_grad, down_grad)
    d_ctx = dot_nt(grad, weights["out"]).astype(BF16)
    (d_ctx, d_up) = track.step((d_ctx, d_up))
    d_fused = attend_back(qkv, lse, d_ctx, table, begin)
    (d_fused, d_up) = track.step((d_fused, d_up))
    d_two = dot_nt(d_up, weights["up"])
    out_grad = dot_tn(ctx, grad).astype(BF16)
    qkv_grad = dot_tn(one, d_fused).astype(BF16)
    d_one = dot_nt(d_fused, weights["qkv"])
    d_one, d_two = track.step((d_one, d_two))
    normed, scale = normalized(source.astype(F32))
    mixed = d_one * weights["g1"] + d_two * weights["g2"]
    part = scale * (
        mixed
        - jnp.mean(mixed, axis=-1, keepdims=True)
        - normed * jnp.mean(mixed * normed, axis=-1, keepdims=True)
    )
    small = (
        jnp.sum(d_one * normed, axis=0),
        jnp.sum(d_one, axis=0),
        jnp.sum(d_two * normed, axis=0),
        jnp.sum(d_two, axis=0),
        jnp.sum(d_fused.astype(F32), axis=0),
        None,
        jnp.sum(d_up.astype(F32), axis=0),
        None,
    )
    return part, qkv_grad, out_grad, small


def body(
    tokens,
    segments,
    cotangent,
    ln1_gain,
    ln1_bias,
    ln2_gain,
    ln2_bias,
    qkv_weight,
    qkv_bias,
    out_weight,
    out_bias,
    up_weight,
    up_bias,
    down_weight,
    down_bias,
):
    n = lax.axis_size("dp")
    chips = n // 2
    r = D // n
    u = 2 * r
    f = FF // n
    section = lax.axis_index("section")
    dp = lax.axis_index("dp")
    core = lax.rem(dp, 2)
    low_core, low_section = core == 0, section == 0
    ring = Ring(n) if chips == 8 else None

    track = Track()

    def columns_for(t):
        wq, wo = qkv_weight[0], out_weight[0]
        columns = [
            wq[:, D * i + HALF * t + PAIR * p : D * i + HALF * t + PAIR * (p + 1)]
            for p in range(PAIRS)
            for i in range(3)
        ] + [wo[:, HALF * t : HALF * (t + 1)]]
        return jnp.concatenate(columns, axis=1)

    def hidden_for(t):
        return up_weight[0].reshape(r, chips, 2, f)[:, :, t].reshape(r, FFH)

    vectors = (ln1_gain, ln1_bias, ln2_gain, ln2_bias, qkv_bias, out_bias, up_bias, down_bias)
    own_small = jnp.concatenate([jnp.pad(v, ((0, 0), (0, LANES - v.shape[1]))) for v in vectors])

    def shared(for_core, rest):
        zero, one_ = for_core(0), for_core(1)
        mine, sent = pick(low_core, zero, one_), pick(low_core, one_, zero)
        if rest is not None:
            mine, sent = jnp.concatenate([mine, rest]), jnp.concatenate([sent, rest])
        theirs = swap_core(sent)
        return pick(low_core, mine, theirs), pick(low_core, theirs, mine)

    a, b = shared(columns_for, own_small)
    attn_block = jnp.concatenate([a[:r], b[:r], a[r:], b[r:]])
    other = swap_section(attn_block)
    attn_blocks = (pick(low_section, attn_block, other), pick(low_section, other, attn_block))
    a, b = shared(hidden_for, None)
    down = down_weight[0]
    mlp_block = jnp.concatenate([a, b, jnp.concatenate([down[:u], down[u:]], axis=1)])
    other = swap_section(mlp_block)
    mlp_blocks = (pick(low_section, mlp_block, other), pick(low_section, other, mlp_block))

    for layer in (0, 1):
        for kind, blocks in (("attn", attn_blocks), ("mlp", mlp_blocks)):
            if ring is not None:
                track.push((kind, layer), ring.gather(blocks[layer]))

    def gathered(kind, layer, sizes):
        if ring is None:
            own = (attn_blocks if kind == "attn" else mlp_blocks)[layer]
            every = lax.all_gather(own, "dp", axis=0, axis_index_groups=same_core(n))
            return every[:, : sizes[0]], every[:, sizes[0] :]
        parts = [jnp.zeros((chips, k, LANES), BF16) for k in sizes]
        for chip, piece in track.finish((kind, layer)):
            cuts = (piece[: sizes[0]], piece[sizes[0] :])
            parts = [lax.dynamic_update_index_in_dim(p, c, chip, 0) for p, c in zip(parts, cuts)]
        return parts

    def attn_weights(layer):
        qo, small = gathered("attn", layer, (u, PAD))
        qo = qo.reshape(D, LANES)
        columns = qo[:, QKVH:]
        halves = (columns[:HALF], columns[HALF:])
        kept_rows = pick(low_core, *halves)
        got = swap_core(pick(low_core, *halves[::-1]))
        small = small.reshape(n, len(SMALL), LANES).astype(F32)
        vectors = [small[:, i, : size * r].reshape(size * D) for i, size in enumerate(SMALL)]
        bq = vectors[4].reshape(3, 2, PAIRS, PAIR)
        bu = vectors[6].reshape(chips, 2, f)
        return {
            "g1": vectors[0],
            "b1": vectors[1],
            "g2": vectors[2],
            "b2": vectors[3],
            "qkv": qo[:, :QKVH],
            "bqkv": pick(low_core, bq[:, 0], bq[:, 1]).transpose(1, 0, 2).reshape(QKVH),
            "out": jnp.concatenate(
                [pick(low_core, kept_rows, got), pick(low_core, got, kept_rows)], axis=1
            ),
            "bout": vectors[5] + vectors[7],
            "bup": pick(low_core, bu[:, 0], bu[:, 1]).reshape(FFH),
        }

    def mlp_weights(layer):
        up, folded = gathered("mlp", layer, (u, u))
        return {
            "up": up.reshape(D, FFH),
            "down": jnp.stack([folded[:, :, :D], folded[:, :, D:]], axis=1).reshape(FFH, D),
        }

    length = tokens.shape[1]

    def paired(own):
        got = swap_core(own)
        return jnp.concatenate([pick(low_core, own, got), pick(low_core, got, own)])

    def own_half(rows):
        return pick(low_core, rows[:length], rows[length:])

    def other_half(rows):
        return pick(low_core, rows[length:], rows[:length])

    def summed(part):
        return own_half(part) + swap_core(other_half(part).astype(BF16)).astype(F32)

    own_tokens = pick(low_section, tokens[0], tokens[1])
    own_seg = pick(low_section, segments[0], segments[1])
    own_cot = pick(low_section, cotangent[0], cotangent[1])
    cot_low = own_cot.astype(BF16)
    (both, own_seg) = track.step((own_tokens, own_seg))
    table, begin = rotary_tables(paired(own_seg[None]))
    both = paired(both)

    weights_0 = attn_weights(0)
    saved_0 = forward_attend(both, weights_0, table, begin, track)
    weights_0.update(mlp_weights(0))
    part, saved_0 = forward_hidden(saved_0, weights_0, track)
    mid = (own_tokens.astype(F32) + summed(part) + weights_0["bout"]).astype(BF16)
    (mid,) = track.step((mid,))
    both = paired(mid)
    weights_1 = attn_weights(1)
    saved_1 = forward_attend(both, weights_1, table, begin, track)
    weights_1.update(mlp_weights(1))
    part, saved_1 = forward_hidden(saved_1, weights_1, track)
    last = (mid.astype(F32) + summed(part) + weights_1["bout"]).astype(BF16)
    kept_rows, got = pick(low_section, mid, last), swap_section(pick(low_section, last, mid))
    outputs = jnp.stack([pick(low_section, kept_rows, got), pick(low_section, got, kept_rows)])

    def reduce_group(name, group):
        if ring is None:
            block = jnp.concatenate(group, axis=1)
            summed_block = lax.psum_scatter(block, "dp", scatter_dimension=0, axis_index_groups=same_core(n))
            track.done[name] = summed_block.astype(F32)
            return

        def block_of(chip):
            cuts = [lax.dynamic_index_in_dim(g, chip, 0, keepdims=False) for g in group]
            return jnp.concatenate(cuts)

        track.push(name, ring.scatter(block_of, sum(g.shape[1] for g in group)))

    def send_mlp(layer, up_grad, down_grad):
        down_rows = down_grad.reshape(chips, 2, u, D)
        down_rows = jnp.concatenate([down_rows[:, 0], down_rows[:, 1]], axis=2)
        reduce_group(("d_mlp", layer), (up_grad.reshape(chips, u, LANES), down_rows))

    def send_attn(layer, qkv_grad, out_grad, small, own_grad):
        halves = (out_grad[:, :HALF], out_grad[:, HALF:])
        kept_columns = pick(low_core, *halves)
        got = swap_core(pick(low_core, *halves[::-1]))
        out_rows = jnp.concatenate([pick(low_core, kept_columns, got), pick(low_core, got, kept_columns)])
        bias = jnp.sum(own_grad.astype(F32), axis=0)
        bq = small[4].reshape(PAIRS, 3, PAIR).transpose(1, 0, 2)
        bu = small[6].reshape(chips, f)
        none_q, none_u = jnp.zeros_like(bq), jnp.zeros_like(bu)
        bq = jnp.stack([pick(low_core, bq, none_q), pick(low_core, none_q, bq)], axis=1)
        bu = jnp.stack([pick(low_core, bu, none_u), pick(low_core, none_u, bu)], axis=1)
        vectors = [v.reshape(n, 1, -1) for v in (*small[:4], bq, bias, bu, bias)]
        rows = [jnp.pad(v, ((0, 0), (0, 0), (0, LANES - v.shape[2]))) for v in vectors]
        flat = jnp.concatenate(rows, axis=1).astype(BF16).reshape(chips, PAD, LANES)
        qo = jnp.concatenate([qkv_grad, out_rows], axis=1).reshape(chips, u, LANES)
        reduce_group(("d_attn", layer), (qo, flat))

    both_grad = paired(cot_low)
    part, qkv_grad, out_grad, small = backward(
        saved_1, both_grad, weights_1, table, begin, track, lambda *g: send_mlp(1, *g)
    )
    send_attn(1, qkv_grad, out_grad, small, cot_low)
    grad_1 = own_cot + summed(part)
    low_1 = grad_1.astype(BF16)
    (low_1, grad_1) = track.step((low_1, grad_1))
    both_grad = paired(low_1)
    part, qkv_grad, out_grad, small = backward(
        saved_0, both_grad, weights_0, table, begin, track, lambda *g: send_mlp(0, *g)
    )
    send_attn(0, qkv_grad, out_grad, small, low_1)
    grad_0 = low_1.astype(F32) + summed(part)
    (grad_0,) = track.step((grad_0,))
    sent = swap_section(pick(low_section, grad_1, grad_0).astype(BF16)).astype(F32)
    kept_rows = pick(low_section, grad_0, grad_1)
    in_grads = jnp.stack([pick(low_section, kept_rows, sent), pick(low_section, sent, kept_rows)])

    def of_section(kind):
        zero, one_ = track.finish((kind, 0)), track.finish((kind, 1))
        got = swap_section(pick(low_section, one_, zero).astype(BF16))
        return pick(low_section, zero, one_) + got.astype(F32)

    def of_core(block, half):
        keep = pick(low_core, block[:half], block[half:])
        got = swap_core(pick(low_core, block[half:], block[:half]).astype(BF16)).astype(F32)
        return pick(low_core, keep, got), pick(low_core, got, keep), keep + got

    mlp = of_section("d_mlp")
    m0, m1, _ = of_core(mlp[:u], r)
    up_out = jnp.stack([m0.reshape(r, chips, f), m1.reshape(r, chips, f)], axis=2).reshape(r, FF)
    down_out = jnp.concatenate([mlp[u:, :D], mlp[u:, D:]])
    attn = of_section("d_attn")
    rows = len(SMALL)
    a0, a1, both_sum = of_core(
        jnp.concatenate([attn[:r], attn[u : u + rows], attn[r:u], attn[u + rows :]]), r + rows
    )
    qkv_out = jnp.concatenate(
        [
            half[:r, (3 * p + i) * PAIR : (3 * p + i + 1) * PAIR]
            for i in range(3)
            for half in (a0, a1)
            for p in range(PAIRS)
        ],
        axis=1,
    )
    out_out = jnp.concatenate([a0[:r, QKVH:], a1[:r, QKVH:]], axis=1)
    g1, b1, g2, b2, bq, bo, bu, bd = [both_sum[r + i : r + i + 1, : size * r] for i, size in enumerate(SMALL)]
    return (
        outputs[None],
        in_grads[None],
        g1,
        b1,
        g2,
        b2,
        qkv_out[None],
        bq,
        out_out[None],
        bo,
        up_out[None],
        bu,
        down_out[None],
        bd,
    )


def solution(mesh):
    row, matrix = P("section", "dp"), P("section", "dp", None)
    params = (row, row, row, row, matrix, row, matrix, row, matrix, row, matrix, row)
    return jax.shard_map(
        body,
        mesh=mesh,
        in_specs=(P(None, "dp", None), P(None, "dp"), P(None, "dp", None)) + params,
        out_specs=(P("section", None, "dp", None), P("section", None, "dp", None)) + params,
        check_vma=False,
    )
```

time: 1610 us -> 637 us (0.40)
  waiting for transfers between devices: 930 us -> 146 us
  matrix products: 208 us -> 73 us
  Pallas kernels: 0 us -> 70.5 us
  other arithmetic: 162 us -> 92.2 us
  blocking collectives: 58.3 us -> 0 us
  starting transfers between devices: 80.7 us -> 110 us
  local copies, waits for them, and re-layouts: 135 us -> 111 us
    reduce_scatter x4 -> x0, waiting for transfers between devices: 392 us -> none  [the longest x1 116 us: scatter_final(): lax.psum_scatter(g_eleven[None], 'dp', scatter_dimension=1, tiled=True)]
    unnamed x22 -> x0, waiting for transfers between devices: 329 us -> none
    dot_general x38 -> x24, matrix products: 208 us -> 73 us  [the longest x8 27.6 us: dot_nt(): lax.dot_general(a, b, (((1,), (1,)), ((), ())), preferred_element_type=F32)]
    all_gather x4 -> x0, waiting for transfers between devices: 120 us -> none  [the longest x1 54.7 us: gather_forward(): lax.all_gather(w_up, 'dp', axis=1, tiled=True)]
    pallas_call x0 -> x4, Pallas kernels: none -> 70.5 us  [the longest x2 35.3 us: attend_back(): pl.pallas_call(attend_back_kernel, grid=(2, PAIRS), in_specs=[per_pair(le...]
    squeeze x1 -> x0, blocking collectives: 58.3 us -> none  [gather_forward(): return tuple((member[0] for member in gathered))]
    ppermute x4 -> x87, waiting for transfers between devices: 88 us -> 146 us  [the longest x16 52.2 us: scatter(): back = lax.ppermute(back, 'dp', self.left)]
    dynamic_update_slice x27 -> x2, other arithmetic: 37.3 us -> 0.78 us  [gathered(): lax.dynamic_update_index_in_dim(p, c, chip, 0)]
  transfers between devices with their start and end apart: 19 -> 87, of which waited for: 15 -> 40; matrix products, arithmetic and copies ran while one was open for 10% -> 30% of each run, Pallas kernels for 0% -> 8%
where the time goes in v1:
time: 637 us; the launch traced here: 627 us
  waiting for transfers between devices  146 us (23%)
  local copies, waits for them, and re-layouts  111 us (17%)
  starting transfers between devices  110 us (17%)
  other arithmetic  92.2 us (14%)
  matrix products  73 us (11%)
  Pallas kernels  70.5 us (11%)
  between operations  25 us (4%)
    ppermute x17, starting transfers between devices, swap_core(): return lax.ppermute(block, 'dp', [(i, i ^ 1) for i in range(n)])  54.3 us
    ppermute x16, waiting for transfers between devices, scatter(): back = lax.ppermute(back, 'dp', self.left)  52.2 us
    ppermute x12, waiting for transfers between devices, gather(): ahead = lax.ppermute(ahead, 'dp', self.right)  39.2 us
    pallas_call x2, Pallas kernels, attend_back(): pl.pallas_call(attend_back_kernel, grid=(2, PAIRS), in_specs=[per_pair(le...  35.3 us
    pallas_call x2, Pallas kernels, attend(): pl.pallas_call(attend_kernel, grid=(2, PAIRS), in_specs=[per_pair(length,...  35.1 us
    unnamed x369, local copies, waits for them, and re-layouts  31.8 us
    dot_general x8, matrix products, dot_nt(): lax.dot_general(a, b, (((1,), (1,)), ((), ())), preferred_element_type=F32)  27.6 us
    dot_general x8, matrix products, matmul(): return jnp.dot(a, b, preferred_element_type=F32)  23.5 us
  transfers between devices with their start and end apart: 87, of which 40 were waited for; matrix products, arithmetic and copies ran while one was open for 30% of the time, Pallas kernels for 8%

profile of v1, /device:TPU:1, one launch (start us, length us, event | category | flops | bytes accessed | tf_op | source)
XLA Modules:
  0.0 627.0 jit_solution(5739603828158177437)
XLA Ops:
  53.2 6.5 %collective-permute-done.1 = bf16[112,1536]{1,0:T(8,128)(2,1)S(1)} collective-permute-done((bf16[112,1536]{1,0:T(8,128)(2,1)S(1)}, bf16[112,1536]{1,0:T(8,128)(2,1)S(1)}, u32[]{:S(2)}, u32[]{:S(2)}) %collective-permute-start.1) | collective-permute-done | bytes 344096 | tf_op jit(solution)/shard_map/ppermute | solution.py:38
  111.7 5.4 collective-permute-start.26
  127.8 17.6 %shard_map.281 = (bf16[1024,1152]{1,0:T(8,128)(2,1)S(1)}, bf16[1024,384]{1,0:T(8,128)(2,1)S(1)}, f32[1024,384]{1,0:T(8,128)S(1)}) custom-call(f32[1024,1152]{1,0:T(8,128)S(1)} %convolution_add_fusion.1.joined_ref, f32[1024,256]{1,0:T(8,128)S(1)} %pad_maximum_fusion.6.table_ref, s32[1024,1]{1,0:T(8,128)S(1)} %bitcast.443), custom_call_target="tpu_custom_call" | custom-call | flops 20000000000 | bytes 12000000 | tf_op jit(solution)/shard_map/pallas_call | solution.py:264
  149.9 12.7 %collective-permute-done.18 = bf16[192,1536]{1,0:T(8,128)(2,1)S(1)} collective-permute-done((bf16[192,1536]{1,0:T(8,128)(2,1)S(1)}, bf16[192,1536]{1,0:T(8,128)(2,1)S(1)}, u32[]{:S(2)}, u32[]{:S(2)}) %collective-permute-start.18) | collective-permute-done | bytes 589856 | tf_op jit(solution)/shard_map/ppermute | solution.py:76
  165.1 5.1 collective-permute-done.21
  173.2 6.8 %fusion.4 = (bf16[1024,1536]{1,0:T(8,128)(2,1)}, bf16[1024,1536]{1,0:T(8,128)(2,1)S(1)}) fusion(f32[1536]{0:T(1024)S(1)} %select_n.778, bf16[1024,768]{1,0:T(8,128)(2,1)S(1)} %get-tuple-element.155, bf16[768,1536]{1,0:T(8,128)(2,1)S(1)} %bitcast.459), kind=kOutput, calls=%fused_computation.6 | convolution fusion | flops 2434793472 | bytes 10229760 | tf_op jit(solution)/shard_map/dot_general | solution.py:307
  189.7 6.4 %collective-permute-start.29 = (bf16[512,768]{1,0:T(8,128)(2,1)S(1)}, bf16[512,768]{1,0:T(8,128)(2,1)S(1)}, u32[]{:S(2)}, u32[]{:S(2)}) collective-permute-start(bf16[512,768]{1,0:T(8,128)(2,1)S(1)} %select_convert_fusion.4), channel_id=1, source_target_pairs={{0,1},{1,0},{2,3},{3,2},{4,5},{5,4},{6,7},{7,6},{8,9},{9,8},{10,11... | collective-permute-start | bytes 2359304 | tf_op jit(solution)/shard_map/ppermute | solution.py:34
  234.4 17.6 %shard_map.282 = (bf16[1024,1152]{1,0:T(8,128)(2,1)S(1)}, bf16[1024,384]{1,0:T(8,128)(2,1)S(1)}, f32[1024,384]{1,0:T(8,128)S(1)}) custom-call(f32[1024,1152]{1,0:T(8,128)S(1)} %convolution_add_fusion.joined_ref, f32[1024,256]{1,0:T(8,128)S(1)} %pad_maximum_fusion.6.table_ref, s32[1024,1]{1,0:T(8,128)S(1)} %bitcast.444), custom_call_target="tpu_custom_call" | custom-call | flops 20000000000 | bytes 12000000 | tf_op jit(solution)/shard_map/pallas_call | solution.py:264
  257.3 10.1 %collective-permute-done.35 = bf16[192,1536]{1,0:T(8,128)(2,1)S(1)} collective-permute-done((bf16[192,1536]{1,0:T(8,128)(2,1)}, bf16[192,1536]{1,0:T(8,128)(2,1)S(1)}, u32[]{:S(2)}, u32[]{:S(2)}) %collective-permute-start.35) | collective-permute-done | bytes 589856 | tf_op jit(solution)/shard_map/ppermute | solution.py:76
  273.4 11.0 %collective-permute-done.38 = bf16[192,1536]{1,0:T(8,128)(2,1)S(1)} collective-permute-done((bf16[192,1536]{1,0:T(8,128)(2,1)S(1)}, bf16[192,1536]{1,0:T(8,128)(2,1)S(1)}, u32[]{:S(2)}, u32[]{:S(2)}) %collective-permute-start.38) | collective-permute-done | bytes 589856 | tf_op jit(solution)/shard_map/ppermute | solution.py:76
  305.8 4.9 multiply_convert_fusion.1
  324.6 17.7 %shard_map.283 = bf16[1024,1152]{1,0:T(8,128)(2,1)S(1)} custom-call(bf16[1024,1152]{1,0:T(8,128)(2,1)S(1)} %get-tuple-element.186.qkv_ref, f32[1024,384]{1,0:T(8,128)S(1)} %get-tuple-element.187.lse_ref, bf16[1024,384]{1,0:T(8,128)(2,1)S(1)} %convolution_convert_fusion.7.dctx_ref, f32[1024,256]{1,0:T(8,128)S(1)} %pad_maximum_fusion.6.table_ref, ...), custom_call_target="tpu_custom_call" | custom-call | flops 30000001024 | bytes 12000000 | tf_op jit(solution)/shard_map/pallas_call | solution.py:282
  372.9 6.4 %fusion.114 = (bf16[768]{0:T(1024)(128)(2,1)}, bf16[768]{0:T(1024)(128)(2,1)}, f32[1024]{0:T(1024)}, f32[1024]{0:T(1024)}, f32[1024,768]{1,0:T(8,128)}, /*index=5*/bf16[768]{0:T(1024)(128)(2,1)}, bf16[768]{0:T(1024)(128)(2,1)}) fusion(f32[1024,768]{1,0:T(8,128)S(1)} %copy-done.35, f32[1024]{0:T(1024)S(1)} %copy-done.129, f32[1024]{0:T(1024)S(1)} %copy-done.124, ...), kind=kLoop, calls=%fused_computation.541 | loop fusion | flops 14150656 | bytes 11038720 | tf_op jit(solution)/shard_map/reduce_sum | solution.py:359
  408.8 5.7 collective-permute-done.51
  446.4 17.7 %shard_map.284 = bf16[1024,1152]{1,0:T(8,128)(2,1)S(1)} custom-call(bf16[1024,1152]{1,0:T(8,128)(2,1)S(1)} %copy-done.6, f32[1024,384]{1,0:T(8,128)S(1)} %copy-done.8, bf16[1024,384]{1,0:T(8,128)(2,1)S(1)} %convolution_convert_fusion.6.dctx_ref, f32[1024,256]{1,0:T(8,128)S(1)} %pad_maximum_fusion.6.table_ref, s32[1024,1]{1,0:T(8,128)S(1)} %bitcast.446), custom_call_target="tpu_custom_call" | custom-call | flops 30000001024 | bytes 12000000 | tf_op jit(solution)/shard_map/pallas_call | solution.py:282
  470.6 5.4 fusion.51
  525.8 9.3 %collective-permute-done.70 = bf16[192,1536]{1,0:T(8,128)(2,1)S(1)} collective-permute-done((bf16[192,1536]{1,0:T(8,128)(2,1)S(1)}, bf16[192,1536]{1,0:T(8,128)(2,1)S(1)}, u32[]{:S(2)}, u32[]{:S(2)}) %collective-permute-start.70) | collective-permute-done | bytes 589856 | tf_op jit(solution)/shard_map/ppermute | solution.py:101
  541.9 6.6 %collective-permute-done.72 = bf16[192,1536]{1,0:T(8,128)(2,1)} collective-permute-done((bf16[192,1536]{1,0:T(8,128)(2,1)}, bf16[192,1536]{1,0:T(8,128)(2,1)}, u32[]{:S(2)}, u32[]{:S(2)}) %collective-permute-start.72) | collective-permute-done | bytes 589856 | tf_op jit(solution)/shard_map/ppermute | solution.py:101
  555.0 6.9 %collective-permute-done.74 = bf16[192,1536]{1,0:T(8,128)(2,1)S(1)} collective-permute-done((bf16[192,1536]{1,0:T(8,128)(2,1)S(1)}, bf16[192,1536]{1,0:T(8,128)(2,1)S(1)}, u32[]{:S(2)}, u32[]{:S(2)}) %collective-permute-start.74) | collective-permute-done | bytes 589856 | tf_op jit(solution)/shard_map/ppermute | solution.py:101
  573.7 5.8 collective-permute-done.78
  582.7 6.6 %collective-permute-done.80 = bf16[112,1536]{1,0:T(8,128)(2,1)S(1)} collective-permute-done((bf16[112,1536]{1,0:T(8,128)(2,1)S(1)}, bf16[112,1536]{1,0:T(8,128)(2,1)S(1)}, u32[]{:S(2)}, u32[]{:S(2)}) %collective-permute-start.80) | collective-permute-done | bytes 344096 | tf_op jit(solution)/shard_map/ppermute | solution.py:101
  591.7 12.2 %collective-permute-start.86 = (bf16[48,1536]{1,0:T(8,128)(2,1)S(1)}, bf16[48,1536]{1,0:T(8,128)(2,1)S(1)}, u32[]{:S(2)}, u32[]{:S(2)}) collective-permute-start(bf16[48,1536]{1,0:T(8,128)(2,1)S(1)} %select_convert_fusion.8), channel_id=1, source_target_pairs={{0,1},{1,0},{2,3},{3,2},{4,5},{5,4},{6,7},{7,6},{8,9},{9,8},{10,11... | collective-permute-start | bytes 442376 | tf_op jit(solution)/shard_map/ppermute | solution.py:34
  606.5 5.0 collective-permute-done.83
  612.9 8.1 %collective-permute-start.84 = (bf16[56,1536]{1,0:T(8,128)(2,1)S(1)}, bf16[56,1536]{1,0:T(8,128)(2,1)S(1)}, u32[]{:S(2)}, u32[]{:S(2)}) collective-permute-start(bf16[56,1536]{1,0:T(8,128)(2,1)S(1)} %select_convert_fusion.7), channel_id=1, source_target_pairs={{0,1},{1,0},{2,3},{3,2},{4,5},{5,4},{6,7},{7,6},{8,9},{9,8},{10,11... | collective-permute-start | bytes 516104 | tf_op jit(solution)/shard_map/ppermute | solution.py:34
  (853 shorter events, 384.8 us)
Async XLA Ops:
  15.5 32.1 %collective-permute-start = (bf16[56,1536]{1,0:T(8,128)(2,1)}, bf16[56,1536]{1,0:T(8,128)(2,1)}, u32[]{:S(2)}, u32[]{:S(2)}) collective-permute-start(bf16[56,1536]{1,0:T(8,128)(2,1)} %concatenate.204), channel_id=1, source_target_pairs={{0,1},{1,0},{2,3},{3,2},{4,5},{5,4},{6,7},{7,6},{8,9},{9,8},{10,11... | collective-permute-start | bytes 516104 | tf_op jit(solution)/shard_map/ppermute | solution.py:34
  18.6 32.8 %collective-permute-start.2 = (bf16[48,1536]{1,0:T(8,128)(2,1)}, bf16[48,1536]{1,0:T(8,128)(2,1)}, u32[]{:S(2)}, u32[]{:S(2)}) collective-permute-start(bf16[48,1536]{1,0:T(8,128)(2,1)} %select_n.737), channel_id=1, source_target_pairs={{0,1},{1,0},{2,3},{3,2},{4,5},{5,4},{6,7},{7,6},{8,9},{9,8},{10,11... | collective-permute-start | bytes 442376 | tf_op jit(solution)/shard_map/ppermute | solution.py:34
  20.8 53.9 %collective-permute-start.44 = (bf16[512,768]{1,0:T(8,128)(2,1)}, bf16[512,768]{1,0:T(8,128)(2,1)}, u32[]{:S(2)}, u32[]{:S(2)}) collective-permute-start(bf16[512,768]{1,0:T(8,128)(2,1)} %get-tuple-element.270), channel_id=1, source_target_pairs={{0,1},{1,0},{2,3},{3,2},{4,5},{5,4},{6,7},{7,6},{8,9},{9,8},{10,11... | collective-permute-start | bytes 2359304 | tf_op jit(solution)/shard_map/ppermute | solution.py:34
  53.2 19.2 %collective-permute-start.3 = (bf16[192,1536]{1,0:T(8,128)(2,1)}, bf16[192,1536]{1,0:T(8,128)(2,1)}, u32[]{:S(2)}, u32[]{:S(2)}) collective-permute-start(bf16[192,1536]{1,0:T(8,128)(2,1)} %maximum_maximum_fusion.2), channel_id=1, source_target_pairs={{0,16},{16,0},{1,17},{17,1},{2,18},{18,2},{3,19},{19,3},{4,20},{20... | collective-permute-start | bytes 1769480 | tf_op jit(solution)/shard_map/ppermute | solution.py:38
  60.5 16.9 %collective-permute-start.5 = (bf16[112,1536]{1,0:T(8,128)(2,1)S(1)}, bf16[112,1536]{1,0:T(8,128)(2,1)}, u32[]{:S(2)}, u32[]{:S(2)}) collective-permute-start(bf16[112,1536]{1,0:T(8,128)(2,1)S(1)} %get-tuple-element.130), channel_id=1, source_target_pairs={{0,2},{1,3},{4,0},{5,1},{8,4},{9,5},{12,8},{13,9},{14,12},{15,13},... | collective-permute-start | bytes 1032200 | tf_op jit(solution)/shard_map/ppermute | solution.py:77
  66.1 24.1 %collective-permute-start.14 = (bf16[512,768]{1,0:T(8,128)(2,1)S(1)}, bf16[512,768]{1,0:T(8,128)(2,1)}, u32[]{:S(2)}, u32[]{:S(2)}) collective-permute-start(bf16[512,768]{1,0:T(8,128)(2,1)S(1)} %select_bitcast_fusion.2), channel_id=1, source_target_pairs={{0,1},{1,0},{2,3},{3,2},{4,5},{5,4},{6,7},{7,6},{8,9},{9,8},{10,11... | collective-permute-start | bytes 2359304 | tf_op jit(solution)/shard_map/ppermute | solution.py:34
  103.2 23.0 %collective-permute-start.13 = (bf16[192,1536]{1,0:T(8,128)(2,1)}, bf16[192,1536]{1,0:T(8,128)(2,1)}, u32[]{:S(2)}, u32[]{:S(2)}) collective-permute-start(bf16[192,1536]{1,0:T(8,128)(2,1)} %get-tuple-element.139), channel_id=1, source_target_pairs={{0,2},{1,3},{4,0},{5,1},{8,4},{9,5},{12,8},{13,9},{14,12},{15,13},... | collective-permute-start | bytes 1769480 | tf_op jit(solution)/shard_map/ppermute | solution.py:77
  103.4 22.8 %collective-permute-start.12 = (bf16[192,1536]{1,0:T(8,128)(2,1)}, bf16[192,1536]{1,0:T(8,128)(2,1)}, u32[]{:S(2)}, u32[]{:S(2)}) collective-permute-start(bf16[192,1536]{1,0:T(8,128)(2,1)} %get-tuple-element.139), channel_id=1, source_target_pairs={{0,4},{1,5},{4,8},{5,9},{8,12},{9,13},{12,14},{13,15},{14,10},{15,... | collective-permute-start | bytes 1769480 | tf_op jit(solution)/shard_map/ppermute | solution.py:76
  126.2 22.0 %collective-permute-start.15 = (bf16[192,1536]{1,0:T(8,128)(2,1)}, bf16[192,1536]{1,0:T(8,128)(2,1)S(1)}, u32[]{:S(2)}, u32[]{:S(2)}) collective-permute-start(bf16[192,1536]{1,0:T(8,128)(2,1)} %collective-permute-done.12), channel_id=1, source_target_pairs={{0,4},{1,5},{4,8},{5,9},{8,12},{9,13},{12,14},{13,15},{14,10},{15,... | collective-permute-start | bytes 1769480 | tf_op jit(solution)/shard_map/ppermute | solution.py:76
  127.5 20.7 %collective-permute-start.16 = (bf16[192,1536]{1,0:T(8,128)(2,1)}, bf16[192,1536]{1,0:T(8,128)(2,1)S(1)}, u32[]{:S(2)}, u32[]{:S(2)}) collective-permute-start(bf16[192,1536]{1,0:T(8,128)(2,1)} %collective-permute-done.13), channel_id=1, source_target_pairs={{0,2},{1,3},{4,0},{5,1},{8,4},{9,5},{12,8},{13,9},{14,12},{15,13},... | collective-permute-start | bytes 1769480 | tf_op jit(solution)/shard_map/ppermute | solution.py:77
  200.2 27.8 %collective-permute-start.34 = (bf16[512,768]{1,0:T(8,128)(2,1)S(1)}, bf16[512,768]{1,0:T(8,128)(2,1)}, u32[]{:S(2)}, u32[]{:S(2)}) collective-permute-start(bf16[512,768]{1,0:T(8,128)(2,1)S(1)} %add_convert_fusion.1), channel_id=1, source_target_pairs={{0,1},{1,0},{2,3},{3,2},{4,5},{5,4},{6,7},{7,6},{8,9},{9,8},{10,11... | collective-permute-start | bytes 2359304 | tf_op jit(solution)/shard_map/ppermute | solution.py:34
  205.3 29.0 %collective-permute-start.33 = (bf16[192,1536]{1,0:T(8,128)(2,1)S(1)}, bf16[192,1536]{1,0:T(8,128)(2,1)}, u32[]{:S(2)}, u32[]{:S(2)}) collective-permute-start(bf16[192,1536]{1,0:T(8,128)(2,1)S(1)} %copy-done.53), channel_id=1, source_target_pairs={{0,2},{1,3},{4,0},{5,1},{8,4},{9,5},{12,8},{13,9},{14,12},{15,13},... | collective-permute-start | bytes 1769480 | tf_op jit(solution)/shard_map/ppermute | solution.py:77
  206.6 27.8 %collective-permute-start.32 = (bf16[192,1536]{1,0:T(8,128)(2,1)S(1)}, bf16[192,1536]{1,0:T(8,128)(2,1)}, u32[]{:S(2)}, u32[]{:S(2)}) collective-permute-start(bf16[192,1536]{1,0:T(8,128)(2,1)S(1)} %copy-done.53), channel_id=1, source_target_pairs={{0,4},{1,5},{4,8},{5,9},{8,12},{9,13},{12,14},{13,15},{14,10},{15,... | collective-permute-start | bytes 1769480 | tf_op jit(solution)/shard_map/ppermute | solution.py:76
  318.1 49.5 %collective-permute-start.42 = (bf16[512,768]{1,0:T(8,128)(2,1)}, bf16[512,768]{1,0:T(8,128)(2,1)}, u32[]{:S(2)}, u32[]{:S(2)}) collective-permute-start(bf16[512,768]{1,0:T(8,128)(2,1)} %select_convert_fusion.3), channel_id=1, source_target_pairs={{0,1},{1,0},{2,3},{3,2},{4,5},{5,4},{6,7},{7,6},{8,9},{9,8},{10,11... | collective-permute-start | bytes 2359304 | tf_op jit(solution)/shard_map/ppermute | solution.py:34
  322.7 20.2 %collective-permute-start.45 = (bf16[96,1536]{1,0:T(8,128)(2,1)S(1)}, bf16[96,1536]{1,0:T(8,128)(2,1)S(1)}, u32[]{:S(2)}, u32[]{:S(2)}) collective-permute-start(bf16[96,1536]{1,0:T(8,128)(2,1)S(1)} %get-tuple-element.184), channel_id=1, source_target_pairs={{0,4},{1,5},{4,8},{5,9},{8,12},{9,13},{12,14},{13,15},{14,10},{15,... | collective-permute-start | bytes 884744 | tf_op jit(solution)/shard_map/ppermute | solution.py:92
  322.8 20.1 %collective-permute-start.46 = (bf16[96,1536]{1,0:T(8,128)(2,1)S(1)}, bf16[96,1536]{1,0:T(8,128)(2,1)S(1)}, u32[]{:S(2)}, u32[]{:S(2)}) collective-permute-start(bf16[96,1536]{1,0:T(8,128)(2,1)S(1)} %get-tuple-element.185), channel_id=1, source_target_pairs={{0,2},{1,3},{4,0},{5,1},{8,4},{9,5},{12,8},{13,9},{14,12},{15,13},... | collective-permute-start | bytes 884744 | tf_op jit(solution)/shard_map/ppermute | solution.py:93
  354.6 18.3 %collective-permute-start.49 = (bf16[192,1536]{1,0:T(8,128)(2,1)}, bf16[192,1536]{1,0:T(8,128)(2,1)}, u32[]{:S(2)}, u32[]{:S(2)}) collective-permute-start(bf16[192,1536]{1,0:T(8,128)(2,1)} %pad_maximum_fusion.11), channel_id=1, source_target_pairs={{0,2},{1,3},{4,0},{5,1},{8,4},{9,5},{12,8},{13,9},{14,12},{15,13},... | collective-permute-start | bytes 1769480 | tf_op jit(solution)/shard_map/ppermute | solution.py:101
  356.9 16.0 %collective-permute-start.48 = (bf16[192,1536]{1,0:T(8,128)(2,1)}, bf16[192,1536]{1,0:T(8,128)(2,1)}, u32[]{:S(2)}, u32[]{:S(2)}) collective-permute-start(bf16[192,1536]{1,0:T(8,128)(2,1)} %pad_maximum_fusion.10), channel_id=1, source_target_pairs={{0,4},{1,5},{4,8},{5,9},{8,12},{9,13},{12,14},{13,15},{14,10},{15,... | collective-permute-start | bytes 1769480 | tf_op jit(solution)/shard_map/ppermute | solution.py:100
  371.7 30.3 %collective-permute-start.43 = (bf16[512,768]{1,0:T(8,128)(2,1)}, bf16[512,768]{1,0:T(8,128)(2,1)}, u32[]{:S(2)}, u32[]{:S(2)}) collective-permute-start(bf16[512,768]{1,0:T(8,128)(2,1)} %get-tuple-element.274), channel_id=1, source_target_pairs={{0,16},{16,0},{1,17},{17,1},{2,18},{18,2},{3,19},{19,3},{4,20},{20... | collective-permute-start | bytes 2359304 | tf_op jit(solution)/shard_map/ppermute | solution.py:38
  440.6 23.5 %collective-permute-start.66 = (bf16[384,384]{1,0:T(8,128)(2,1)S(1)}, bf16[384,384]{1,0:T(8,128)(2,1)S(1)}, u32[]{:S(2)}, u32[]{:S(2)}) collective-permute-start(bf16[384,384]{1,0:T(8,128)(2,1)S(1)} %broadcast_select_fusion.17), channel_id=1, source_target_pairs={{0,1},{1,0},{2,3},{3,2},{4,5},{5,4},{6,7},{7,6},{8,9},{9,8},{10,11... | collective-permute-start | bytes 884744 | tf_op jit(solution)/shard_map/ppermute | solution.py:34
  444.5 19.6 %collective-permute-start.59 = (bf16[112,1536]{1,0:T(8,128)(2,1)S(1)}, bf16[112,1536]{1,0:T(8,128)(2,1)S(1)}, u32[]{:S(2)}, u32[]{:S(2)}) collective-permute-start(bf16[112,1536]{1,0:T(8,128)(2,1)S(1)} %pad_maximum_fusion.21), channel_id=1, source_target_pairs={{0,2},{1,3},{4,0},{5,1},{8,4},{9,5},{12,8},{13,9},{14,12},{15,13},... | collective-permute-start | bytes 1032200 | tf_op jit(solution)/shard_map/ppermute | solution.py:101
  446.0 18.2 %collective-permute-start.58 = (bf16[112,1536]{1,0:T(8,128)(2,1)S(1)}, bf16[112,1536]{1,0:T(8,128)(2,1)S(1)}, u32[]{:S(2)}, u32[]{:S(2)}) collective-permute-start(bf16[112,1536]{1,0:T(8,128)(2,1)S(1)} %fusion.61), channel_id=1, source_target_pairs={{0,4},{1,5},{4,8},{5,9},{8,12},{9,13},{12,14},{13,15},{14,10},{15,... | collective-permute-start | bytes 1032200 | tf_op jit(solution)/shard_map/ppermute | solution.py:100
  540.4 23.3 %collective-permute-start.65 = (bf16[512,768]{1,0:T(8,128)(2,1)}, bf16[512,768]{1,0:T(8,128)(2,1)S(1)}, u32[]{:S(2)}, u32[]{:S(2)}) collective-permute-start(bf16[512,768]{1,0:T(8,128)(2,1)} %select_convert_fusion), channel_id=1, source_target_pairs={{0,16},{16,0},{1,17},{17,1},{2,18},{18,2},{3,19},{19,3},{4,20},{20... | collective-permute-start | bytes 2359304 | tf_op jit(solution)/shard_map/ppermute | solution.py:38
  591.7 29.3 %collective-permute-start.86 = (bf16[48,1536]{1,0:T(8,128)(2,1)S(1)}, bf16[48,1536]{1,0:T(8,128)(2,1)S(1)}, u32[]{:S(2)}, u32[]{:S(2)}) collective-permute-start(bf16[48,1536]{1,0:T(8,128)(2,1)S(1)} %select_convert_fusion.8), channel_id=1, source_target_pairs={{0,1},{1,0},{2,3},{3,2},{4,5},{5,4},{6,7},{7,6},{8,9},{9,8},{10,11... | collective-permute-start | bytes 442376 | tf_op jit(solution)/shard_map/ppermute | solution.py:34
  (226 other events, 2332.2 us)

commit v2 on v1

--- a/solution.py
+++ b/solution.py
@@ -69,20 +69,24 @@
 
     def gather(self, own):
         (own,) = yield [own]
-        found = [(self.chip_at(0), own)]
+        found = [own]
         reach = self.chips // 2
         ahead = back = own
         for k in range(1, reach):
             ahead = lax.ppermute(ahead, "dp", self.right)
             back = lax.ppermute(back, "dp", self.left)
             ahead, back = yield [ahead, back]
-            found += [(self.chip_at(-k), ahead), (self.chip_at(k), back)]
+            found += [ahead, back]
         cut = own.shape[0] // 32 * 16
         ahead = lax.ppermute(ahead[:cut], "dp", self.right)
         back = lax.ppermute(back[cut:], "dp", self.left)
         ahead, back = yield [ahead, back]
-        found.append((self.chip_at(reach), jnp.concatenate([ahead, back])))
-        return found
+        return found + [ahead, back]
+
+    def found_at(self):
+        reach = self.chips // 2
+        offsets = [0] + [o for k in range(1, reach) for o in (-k, k)] + [reach]
+        return jnp.stack([self.chip_at(o) for o in offsets])
 
     def scatter(self, block_of, rows):
         reach = self.chips // 2
@@ -246,6 +250,130 @@
     out_ref[:, 2 * PAIR :] = jnp.concatenate(dvs, axis=1).astype(BF16)
 
 
+def smem():
+    return pl.BlockSpec(memory_space=pltpu.SMEM)
+
+
+def vmem():
+    return pl.BlockSpec(memory_space=pltpu.VMEM)
+
+
+def pack_kernel(core_ref, wq_ref, wo_ref, wu_ref, wd_ref, *refs):
+    small_refs, (attn_keep, attn_send, mlp_keep, mlp_send, fold_ref, rows_ref) = refs[:-6], refs[-6:]
+    r, chips, f = wq_ref.shape[1], D // wq_ref.shape[1] // 2, wd_ref.shape[1]
+    rows_ref[...] = jnp.zeros_like(rows_ref)
+    for i, ref in enumerate(small_refs):
+        rows_ref[i : i + 1, : ref.shape[1]] = ref[...].astype(F32)
+    rows = rows_ref[...].astype(BF16)
+    attn_keep[r:, :] = rows
+    attn_send[r:, :] = rows
+    fold_ref[:, :D] = wd_ref[0, : f // 2]
+    fold_ref[:, D:] = wd_ref[0, f // 2 :]
+    for core, targets in ((0, (attn_keep, attn_send)), (1, (attn_send, attn_keep))):
+
+        @pl.when(core_ref[0] == core)
+        def _(targets=targets):
+            for t, ref in enumerate(targets):
+                for p in range(PAIRS):
+                    for i in range(3):
+                        at, to = D * i + HALF * t + PAIR * p, (3 * p + i) * PAIR
+                        ref[:r, to : to + PAIR] = wq_ref[0, :, at : at + PAIR]
+                ref[:r, QKVH:] = wo_ref[0, :, HALF * t : HALF * (t + 1)]
+
+    for core, targets in ((0, (mlp_keep, mlp_send)), (1, (mlp_send, mlp_keep))):
+
+        @pl.when(core_ref[0] == core)
+        def _(targets=targets):
+            for t, ref in enumerate(targets):
+                for j in range(chips):
+                    at = (2 * j + t) * f
+                    ref[:, j * f : (j + 1) * f] = wu_ref[0, :, at : at + f]
+
+
+def assemble_attn_kernel(place_ref, *refs):
+    blocks, (qkv_ref, keep_ref, send_ref, vec_ref, col_ref, row_ref, all_ref, bq_ref, bu_ref) = refs[:-9], refs[-9:]
+    chips = len(blocks) - 1
+    core = place_ref[chips]
+    u = blocks[0].shape[0] - PAD
+    n = 2 * chips
+    r, f = u // 2, 2 * u
+    for k in range(chips):
+        chip = place_ref[k]
+        if k < chips - 1:
+            parts = [(0, u, blocks[k], 0)]
+            small = blocks[k][u:, :]
+        else:
+            cut = blocks[k].shape[0]
+            parts = [(0, cut, blocks[k], 0), (cut, u - cut, blocks[k + 1], 0)]
+            small = blocks[k + 1][u - cut :, :]
+        for start, count, ref, at in parts:
+            rows = pl.ds(pl.multiple_of(chip * u + start, 16), count)
+            qkv_ref[rows, :] = ref[at : at + count, :QKVH]
+            col_ref[rows, :] = ref[at : at + count, QKVH:]
+        row_ref[chip] = small[:, : row_ref.shape[2]].astype(F32)
+    keep_ref[...] = col_ref[pl.ds(pl.multiple_of(core * HALF, HALF), HALF), :]
+    send_ref[...] = col_ref[pl.ds(pl.multiple_of((1 - core) * HALF, HALF), HALF), :]
+    for i in range(n):
+        piece = row_ref[i // 2, 8 * (i % 2) : 8 * (i % 2) + 8, :]
+        all_ref[:, r * i : r * (i + 1)] = piece[:, :r]
+        bq_ref[:, 3 * r * i : 3 * r * (i + 1)] = piece[4:5, : 3 * r]
+        bu_ref[i % 2, :, f * (i // 2) : f * (i // 2 + 1)] = piece[6:7, :f]
+    vec_ref[...] = jnp.zeros_like(vec_ref)
+    vec_ref[:, :D] = all_ref[...]
+    vec_ref[5:6, :D] = all_ref[5:6, :] + all_ref[7:8, :]
+    for c in range(2):
+
+        @pl.when(core == c)
+        def _(c=c):
+            for p in range(PAIRS):
+                for i in range(3):
+                    at, to = D * i + HALF * c + PAIR * p, (3 * p + i) * PAIR
+                    vec_ref[4:5, to : to + PAIR] = bq_ref[:, at : at + PAIR]
+            vec_ref[6:7, :] = bu_ref[c]
+
+
+def assemble_mlp_kernel(place_ref, *refs):
+    blocks, (up_ref, down_ref) = refs[:-2], refs[-2:]
+    chips = len(blocks) - 1
+    u = blocks[0].shape[0] // 2
+    for k in range(chips):
+        chip = place_ref[k]
+        if k < chips - 1:
+            up, down = blocks[k].at[:u], blocks[k].at[u:]
+        else:
+            up, down = blocks[k], blocks[k + 1]
+        up_ref[pl.ds(pl.multiple_of(chip * u, 16), u), :] = up[...]
+        down_ref[pl.ds(pl.multiple_of(chip * 2 * u, 16), u), :] = down[:, :D]
+        down_ref[pl.ds(pl.multiple_of(chip * 2 * u + u, 16), u), :] = down[:, D:]
+
+
+def grads_mlp_kernel(two_ref, d_up_ref, middle_ref, grad_ref, out_ref):
+    count, u = out_ref.shape[0], out_ref.shape[1] // 2
+    up = dot_tn(two_ref[...], d_up_ref[...]).astype(BF16)
+    for i in range(count):
+        out_ref[i, :u, :] = up[u * i : u * (i + 1)]
+    down = dot_tn(middle_ref[...], grad_ref[...]).astype(BF16)
+    for i in range(count):
+        out_ref[i, u:, :D] = down[2 * u * i : 2 * u * i + u]
+        out_ref[i, u:, D:] = down[2 * u * i + u : 2 * u * (i + 1)]
+
+
+def grads_attn_kernel(one_ref, fused_ref, out_rows_ref, all_ref, bq_ref, bu_ref, out_ref, row_ref):
+    count, u = out_ref.shape[0], out_ref.shape[1] - PAD
+    r = u // 2
+    qkv = dot_tn(one_ref[...], fused_ref[...]).astype(BF16)
+    for i in range(count):
+        out_ref[i, :u, :QKVH] = qkv[u * i : u * (i + 1)]
+        out_ref[i, :u, QKVH:] = out_rows_ref[u * i : u * (i + 1), :]
+        row_ref[...] = jnp.zeros_like(row_ref)
+        for c in range(2):
+            d = 2 * i + c
+            row_ref[8 * c : 8 * c + 8, :r] = all_ref[:, r * d : r * (d + 1)]
+            row_ref[8 * c + 4 : 8 * c + 5, : 3 * r] = bq_ref[:, 3 * r * d : 3 * r * (d + 1)]
+            row_ref[8 * c + 6 : 8 * c + 7, : 4 * r] = bu_ref[:, 4 * r * d : 4 * r * (d + 1)]
+        out_ref[i, u:, :] = row_ref[...].astype(BF16)
+
+
 def kernel_params():
     return pltpu.CompilerParams(vmem_limit_bytes=40 * 1024 * 1024)
 
@@ -333,16 +461,12 @@
     source, one, two, qkv, ctx, lse, middle, slope = saved
     d_up = (dot_nt(grad, weights["down"]) * slope.astype(F32)).astype(BF16)
     (d_up,) = track.step((d_up,))
-    down_grad = dot_tn(middle, grad).astype(BF16)
-    up_grad = dot_tn(two, d_up).astype(BF16)
-    send_hidden(up_grad, down_grad)
+    send_hidden(two, d_up, middle, grad)
     d_ctx = dot_nt(grad, weights["out"]).astype(BF16)
     (d_ctx, d_up) = track.step((d_ctx, d_up))
     d_fused = attend_back(qkv, lse, d_ctx, table, begin)
     (d_fused, d_up) = track.step((d_fused, d_up))
     d_two = dot_nt(d_up, weights["up"])
-    out_grad = dot_tn(ctx, grad).astype(BF16)
-    qkv_grad = dot_tn(one, d_fused).astype(BF16)
     d_one = dot_nt(d_fused, weights["qkv"])
     d_one, d_two = track.step((d_one, d_two))
     normed, scale = normalized(source.astype(F32))
@@ -362,7 +486,7 @@
         jnp.sum(d_up.astype(F32), axis=0),
         None,
     )
-    return part, qkv_grad, out_grad, small
+    return part, d_fused, small
 
 
 def body(
@@ -395,36 +519,45 @@
 
     track = Track()
 
-    def columns_for(t):
-        wq, wo = qkv_weight[0], out_weight[0]
-        columns = [
-            wq[:, D * i + HALF * t + PAIR * p : D * i + HALF * t + PAIR * (p + 1)]
-            for p in range(PAIRS)
-            for i in range(3)
-        ] + [wo[:, HALF * t : HALF * (t + 1)]]
-        return jnp.concatenate(columns, axis=1)
-
-    def hidden_for(t):
-        return up_weight[0].reshape(r, chips, 2, f)[:, :, t].reshape(r, FFH)
-
     vectors = (ln1_gain, ln1_bias, ln2_gain, ln2_bias, qkv_bias, out_bias, up_bias, down_bias)
-    own_small = jnp.concatenate([jnp.pad(v, ((0, 0), (0, LANES - v.shape[1]))) for v in vectors])
-
-    def shared(for_core, rest):
-        zero, one_ = for_core(0), for_core(1)
-        mine, sent = pick(low_core, zero, one_), pick(low_core, one_, zero)
-        if rest is not None:
-            mine, sent = jnp.concatenate([mine, rest]), jnp.concatenate([sent, rest])
+    core_scalar = core[None].astype(jnp.int32)
+
+    def packed():
+        if ring is not None:
+            shapes = [(r + 8, LANES)] * 2 + [(r, LANES)] * 2 + [(u, LANES)]
+            return pl.pallas_call(
+                pack_kernel,
+                in_specs=[smem()] + [vmem()] * (4 + len(vectors)),
+                out_specs=[vmem()] * 5,
+                out_shape=[jax.ShapeDtypeStruct(shape, BF16) for shape in shapes],
+                scratch_shapes=[pltpu.VMEM((8, LANES), F32)],
+                compiler_params=kernel_params(),
+            )(core_scalar, qkv_weight, out_weight, up_weight, down_weight, *vectors)
+        rows = jnp.concatenate([jnp.pad(v, ((0, 0), (0, LANES - v.shape[1]))) for v in vectors])
+        attn, hidden = [], []
+        for t in (0, 1):
+            columns = [
+                qkv_weight[0, :, D * i + HALF * t + PAIR * p : D * i + HALF * t + PAIR * (p + 1)]
+                for p in range(PAIRS)
+                for i in range(3)
+            ] + [out_weight[0, :, HALF * t : HALF * (t + 1)]]
+            attn.append(jnp.concatenate([jnp.concatenate(columns, axis=1), rows]))
+            hidden.append(up_weight[0].reshape(r, chips, 2, f)[:, :, t].reshape(r, FFH))
+        halves = [pick(low_core, *x) for x in (attn, attn[::-1], hidden, hidden[::-1])]
+        down = down_weight[0]
+        return halves + [jnp.concatenate([down[:u], down[u:]], axis=1)]
+
+    def shared(mine, sent):
         theirs = swap_core(sent)
         return pick(low_core, mine, theirs), pick(low_core, theirs, mine)
 
-    a, b = shared(columns_for, own_small)
+    attn_keep, attn_send, mlp_keep, mlp_send, folded = packed()
+    a, b = shared(attn_keep, attn_send)
     attn_block = jnp.concatenate([a[:r], b[:r], a[r:], b[r:]])
     other = swap_section(attn_block)
     attn_blocks = (pick(low_section, attn_block, other), pick(low_section, other, attn_block))
-    a, b = shared(hidden_for, None)
-    down = down_weight[0]
-    mlp_block = jnp.concatenate([a, b, jnp.concatenate([down[:u], down[u:]], axis=1)])
+    a, b = shared(mlp_keep, mlp_send)
+    mlp_block = jnp.concatenate([a, b, folded])
     other = swap_section(mlp_block)
     mlp_blocks = (pick(low_section, mlp_block, other), pick(low_section, other, mlp_block))
 
@@ -433,48 +566,61 @@
             if ring is not None:
                 track.push((kind, layer), ring.gather(blocks[layer]))
 
-    def gathered(kind, layer, sizes):
+    place = None if ring is None else jnp.concatenate([ring.found_at().astype(jnp.int32), core_scalar])
+
+    def gathered(own):
+        return lax.all_gather(own, "dp", axis=0, axis_index_groups=same_core(n))
+
+    def attn_weights(layer):
         if ring is None:
-            own = (attn_blocks if kind == "attn" else mlp_blocks)[layer]
-            every = lax.all_gather(own, "dp", axis=0, axis_index_groups=same_core(n))
-            return every[:, : sizes[0]], every[:, sizes[0] :]
-        parts = [jnp.zeros((chips, k, LANES), BF16) for k in sizes]
-        for chip, piece in track.finish((kind, layer)):
-            cuts = (piece[: sizes[0]], piece[sizes[0] :])
-            parts = [lax.dynamic_update_index_in_dim(p, c, chip, 0) for p, c in zip(parts, cuts)]
-        return parts
-
-    def attn_weights(layer):
-        qo, small = gathered("attn", layer, (u, PAD))
-        qo = qo.reshape(D, LANES)
-        columns = qo[:, QKVH:]
-        halves = (columns[:HALF], columns[HALF:])
-        kept_rows = pick(low_core, *halves)
-        got = swap_core(pick(low_core, *halves[::-1]))
-        small = small.reshape(n, len(SMALL), LANES).astype(F32)
-        vectors = [small[:, i, : size * r].reshape(size * D) for i, size in enumerate(SMALL)]
-        bq = vectors[4].reshape(3, 2, PAIRS, PAIR)
-        bu = vectors[6].reshape(chips, 2, f)
-        return {
-            "g1": vectors[0],
-            "b1": vectors[1],
-            "g2": vectors[2],
-            "b2": vectors[3],
-            "qkv": qo[:, :QKVH],
-            "bqkv": pick(low_core, bq[:, 0], bq[:, 1]).transpose(1, 0, 2).reshape(QKVH),
-            "out": jnp.concatenate(
-                [pick(low_core, kept_rows, got), pick(low_core, got, kept_rows)], axis=1
-            ),
-            "bout": vectors[5] + vectors[7],
-            "bup": pick(low_core, bu[:, 0], bu[:, 1]).reshape(FFH),
-        }
+            every = gathered(attn_blocks[layer])
+            qo = every[:, :u].reshape(D, LANES)
+            columns = qo[:, QKVH:]
+            halves = (columns[:HALF], columns[HALF:])
+            qkv, kept_rows, sent = qo[:, :QKVH], pick(low_core, *halves), pick(low_core, *halves[::-1])
+            small = every[:, u:].reshape(n, len(SMALL), LANES).astype(F32)
+            found = [small[:, i, : size * r].reshape(size * D) for i, size in enumerate(SMALL)]
+            bq, bu = found[4].reshape(3, 2, PAIRS, PAIR), found[6].reshape(chips, 2, f)
+            found[4] = pick(low_core, bq[:, 0], bq[:, 1]).transpose(1, 0, 2).reshape(QKVH)
+            found[5] = found[5] + found[7]
+            found[6] = pick(low_core, bu[:, 0], bu[:, 1]).reshape(FFH)
+        else:
+            shapes = [((D, QKVH), BF16), ((HALF, HALF), BF16), ((HALF, HALF), BF16), ((8, LANES), F32)]
+            qkv, kept_rows, sent, vec = pl.pallas_call(
+                assemble_attn_kernel,
+                in_specs=[smem()] + [vmem()] * (chips + 1),
+                out_specs=[vmem()] * 4,
+                out_shape=[jax.ShapeDtypeStruct(*shape) for shape in shapes],
+                scratch_shapes=[
+                    pltpu.VMEM((D, HALF), BF16),
+                    pltpu.VMEM((chips, PAD, 256), F32),
+                    pltpu.VMEM((8, D), F32),
+                    pltpu.VMEM((1, 3 * D), F32),
+                    pltpu.VMEM((2, 1, FFH), F32),
+                ],
+                compiler_params=kernel_params(),
+            )(place, *track.finish(("attn", layer)))
+            widths = (D, D, D, D, QKVH, D, FFH)
+            found = [vec[i, :w] for i, w in enumerate(widths)]
+        got = swap_core(sent)
+        out = jnp.concatenate([pick(low_core, kept_rows, got), pick(low_core, got, kept_rows)], axis=1)
+        names = ("g1", "b1", "g2", "b2", "bqkv", "bout", "bup")
+        return {"qkv": qkv, "out": out, **dict(zip(names, found))}
 
     def mlp_weights(layer):
-        up, folded = gathered("mlp", layer, (u, u))
-        return {
-            "up": up.reshape(D, FFH),
-            "down": jnp.stack([folded[:, :, :D], folded[:, :, D:]], axis=1).reshape(FFH, D),
-        }
+        if ring is None:
+            every = gathered(mlp_blocks[layer])
+            up, folded = every[:, :u].reshape(D, FFH), every[:, u:]
+            down = jnp.stack([folded[:, :, :D], folded[:, :, D:]], axis=1).reshape(FFH, D)
+        else:
+            up, down = pl.pallas_call(
+                assemble_mlp_kernel,
+                in_specs=[smem()] + [vmem()] * (chips + 1),
+                out_specs=[vmem()] * 2,
+                out_shape=[jax.ShapeDtypeStruct((D, FFH), BF16), jax.ShapeDtypeStruct((FFH, D), BF16)],
+                compiler_params=kernel_params(),
+            )(place, *track.finish(("mlp", layer)))
+        return {"up": up, "down": down}
 
     length = tokens.shape[1]
 
@@ -516,52 +662,88 @@
 
     def reduce_group(name, group):
         if ring is None:
-            block = jnp.concatenate(group, axis=1)
-            summed_block = lax.psum_scatter(block, "dp", scatter_dimension=0, axis_index_groups=same_core(n))
-            track.done[name] = summed_block.astype(F32)
+            total = lax.psum_scatter(group, "dp", scatter_dimension=0, axis_index_groups=same_core(n))
+            track.done[name] = total.astype(F32)
             return
-
-        def block_of(chip):
-            cuts = [lax.dynamic_index_in_dim(g, chip, 0, keepdims=False) for g in group]
-            return jnp.concatenate(cuts)
-
-        track.push(name, ring.scatter(block_of, sum(g.shape[1] for g in group)))
-
-    def send_mlp(layer, up_grad, down_grad):
-        down_rows = down_grad.reshape(chips, 2, u, D)
-        down_rows = jnp.concatenate([down_rows[:, 0], down_rows[:, 1]], axis=2)
-        reduce_group(("d_mlp", layer), (up_grad.reshape(chips, u, LANES), down_rows))
-
-    def send_attn(layer, qkv_grad, out_grad, small, own_grad):
+        block_of = lambda chip: lax.dynamic_index_in_dim(group, chip, 0, keepdims=False)
+        track.push(name, ring.scatter(block_of, group.shape[1]))
+
+    def send_mlp(layer, two, d_up, middle, grad):
+        if ring is None:
+            up_grad, down_rows = dot_tn(two, d_up), dot_tn(middle, grad).reshape(chips, 2, u, D)
+            down_rows = jnp.concatenate([down_rows[:, 0], down_rows[:, 1]], axis=2)
+            group = jnp.concatenate([up_grad.reshape(chips, u, LANES), down_rows], axis=1).astype(BF16)
+        else:
+            rows = two.shape[0]
+            group = pl.pallas_call(
+                grads_mlp_kernel,
+                grid=(2,),
+                in_specs=[
+                    pl.BlockSpec((rows, HALF), lambda g: (0, g)),
+                    pl.BlockSpec((rows, FFH), lambda g: (0, 0)),
+                    pl.BlockSpec((rows, FFH // 2), lambda g: (0, g)),
+                    pl.BlockSpec((rows, D), lambda g: (0, 0)),
+                ],
+                out_specs=pl.BlockSpec((chips // 2, 2 * u, LANES), lambda g: (g, 0, 0)),
+                out_shape=jax.ShapeDtypeStruct((chips, 2 * u, LANES), BF16),
+                compiler_params=kernel_params(),
+            )(two, d_up, middle, grad)
+        reduce_group(("d_mlp", layer), group)
+
+    def send_attn(layer, one, d_fused, out_rows, small, bias):
+        bq = small[4].reshape(PAIRS, 3, PAIR).transpose(1, 0, 2)
+        bu = small[6].reshape(chips, f)
+        none_q, none_u = jnp.zeros_like(bq), jnp.zeros_like(bu)
+        bq = jnp.stack([pick(low_core, bq, none_q), pick(low_core, none_q, bq)], axis=1).reshape(1, 3 * D)
+        bu = jnp.stack([pick(low_core, bu, none_u), pick(low_core, none_u, bu)], axis=1).reshape(1, FF)
+        if ring is None:
+            vectors = [v.reshape(n, 1, -1) for v in (*small[:4], bq, bias, bu, bias)]
+            rows = [jnp.pad(v, ((0, 0), (0, 0), (0, LANES - v.shape[2]))) for v in vectors]
+            flat = jnp.concatenate(rows, axis=1).astype(BF16).reshape(chips, PAD, LANES)
+            qo = jnp.concatenate([dot_tn(one, d_fused).astype(BF16), out_rows], axis=1)
+            group = jnp.concatenate([qo.reshape(chips, u, LANES), flat], axis=1)
+        else:
+            unit = jnp.stack([*small[:4], bias, bias, bias, bias])
+            rows = one.shape[0]
+            group = pl.pallas_call(
+                grads_attn_kernel,
+                grid=(2,),
+                in_specs=[
+                    pl.BlockSpec((rows, HALF), lambda g: (0, g)),
+                    pl.BlockSpec((rows, QKVH), lambda g: (0, 0)),
+                    pl.BlockSpec((HALF, HALF), lambda g: (g, 0)),
+                    pl.BlockSpec((8, HALF), lambda g: (0, g)),
+                    pl.BlockSpec((1, 3 * HALF), lambda g: (0, g)),
+                    pl.BlockSpec((1, FFH), lambda g: (0, g)),
+                ],
+                out_specs=pl.BlockSpec((chips // 2, u + PAD, LANES), lambda g: (g, 0, 0)),
+                out_shape=jax.ShapeDtypeStruct((chips, u + PAD, LANES), BF16),
+                scratch_shapes=[pltpu.VMEM((PAD, LANES), F32)],
+                compiler_params=kernel_params(),
+            )(one, d_fused, out_rows, unit, bq, bu)
+        reduce_group(("d_attn", layer), group)
+
+    def out_rows_of(ctx, grad):
+        out_grad = dot_tn(ctx, grad).astype(BF16)
         halves = (out_grad[:, :HALF], out_grad[:, HALF:])
         kept_columns = pick(low_core, *halves)
         got = swap_core(pick(low_core, *halves[::-1]))
-        out_rows = jnp.concatenate([pick(low_core, kept_columns, got), pick(low_core, got, kept_columns)])
-        bias = jnp.sum(own_grad.astype(F32), axis=0)
-        bq = small[4].reshape(PAIRS, 3, PAIR).transpose(1, 0, 2)
-        bu = small[6].reshape(chips, f)
-        none_q, none_u = jnp.zeros_like(bq), jnp.zeros_like(bu)
-        bq = jnp.stack([pick(low_core, bq, none_q), pick(low_core, none_q, bq)], axis=1)
-        bu = jnp.stack([pick(low_core, bu, none_u), pick(low_core, none_u, bu)], axis=1)
-        vectors = [v.reshape(n, 1, -1) for v in (*small[:4], bq, bias, bu, bias)]
-        rows = [jnp.pad(v, ((0, 0), (0, 0), (0, LANES - v.shape[2]))) for v in vectors]
-        flat = jnp.concatenate(rows, axis=1).astype(BF16).reshape(chips, PAD, LANES)
-        qo = jnp.concatenate([qkv_grad, out_rows], axis=1).reshape(chips, u, LANES)
-        reduce_group(("d_attn", layer), (qo, flat))
-
-    both_grad = paired(cot_low)
-    part, qkv_grad, out_grad, small = backward(
-        saved_1, both_grad, weights_1, table, begin, track, lambda *g: send_mlp(1, *g)
-    )
-    send_attn(1, qkv_grad, out_grad, small, cot_low)
+        return jnp.concatenate([pick(low_core, kept_columns, got), pick(low_core, got, kept_columns)])
+
+    def back(layer, saved, weights, low_grad):
+        grad = paired(low_grad)
+        part, d_fused, small = backward(
+            saved, grad, weights, table, begin, track, lambda *parts: send_mlp(layer, *parts)
+        )
+        out_rows = out_rows_of(saved[4], grad)
+        send_attn(layer, saved[1], d_fused, out_rows, small, jnp.sum(low_grad.astype(F32), axis=0))
+        return part
+
+    part = back(1, saved_1, weights_1, cot_low)
     grad_1 = own_cot + summed(part)
     low_1 = grad_1.astype(BF16)
     (low_1, grad_1) = track.step((low_1, grad_1))
-    both_grad = paired(low_1)
-    part, qkv_grad, out_grad, small = backward(
-        saved_0, both_grad, weights_0, table, begin, track, lambda *g: send_mlp(0, *g)
-    )
-    send_attn(0, qkv_grad, out_grad, small, low_1)
+    part = back(0, saved_0, weights_0, low_1)
     grad_0 = low_1.astype(F32) + summed(part)
     (grad_0,) = track.step((grad_0,))
     sent = swap_section(pick(low_section, grad_1, grad_0).astype(BF16)).astype(F32)

time: 637 us -> 530 us (0.83)
  local copies, waits for them, and re-layouts: 111 us -> 31.4 us
  matrix products: 73 us -> 49.7 us
  Pallas kernels: 70.5 us -> 92 us
  waiting for transfers between devices: 146 us -> 132 us
  other arithmetic: 92.2 us -> 79.8 us
    ppermute x16, waiting for transfers between devices: 52.2 us -> 11.8 us  [scatter(): back = lax.ppermute(back, 'dp', self.left)]
    ppermute x16, waiting for transfers between devices: 18.3 us -> 46.9 us  [scatter(): ahead = lax.ppermute(ahead, 'dp', self.right)]
    dynamic_update_slice x50 -> x0, local copies, waits for them, and re-layouts: 22.3 us -> none  [gathered(): lax.dynamic_update_index_in_dim(p, c, chip, 0)]
    pallas_call x0 -> x9, Pallas kernels: none -> 21.5 us  [the longest x2 11.4 us: send_mlp(): pl.pallas_call(grads_mlp_kernel, grid=(2,), in_specs=[pl.BlockSpec((rows,...]
    dot_general x8 -> x2, matrix products: 21.8 us -> 1.63 us  [dot_tn(): lax.dot_general(a, b, (((0,), (0,)), ((), ())), preferred_element_type=F32)]
    ppermute x4, waiting for transfers between devices: 1.92 us -> 18.9 us  [gather(): ahead = lax.ppermute(ahead[:cut], 'dp', self.right)]
    unnamed x369 -> x246, local copies, waits for them, and re-layouts: 31.8 us -> 18.5 us
    ppermute x12, waiting for transfers between devices: 39.2 us -> 27.9 us  [gather(): ahead = lax.ppermute(ahead, 'dp', self.right)]
  transfers between devices with their start and end apart: 87 -> 87, of which waited for: 40 -> 47; matrix products, arithmetic and copies ran while one was open for 30% -> 23% of each run, Pallas kernels for 8% -> 17%
where the time goes in v2:
time: 530 us; the launch traced here: 521 us
  waiting for transfers between devices  132 us (25%)
  starting transfers between devices  112 us (21%)
  Pallas kernels  92 us (17%)
  other arithmetic  79.8 us (15%)
  matrix products  49.7 us (9%)
  local copies, waits for them, and re-layouts  31.4 us (6%)
  between operations  24.2 us (5%)
    ppermute x17, starting transfers between devices, swap_core(): return lax.ppermute(block, 'dp', [(i, i ^ 1) for i in range(n)])  58.1 us
    ppermute x16, waiting for transfers between devices, scatter(): ahead = lax.ppermute(ahead, 'dp', self.right)  46.9 us
    pallas_call x2, Pallas kernels, attend_back(): pl.pallas_call(attend_back_kernel, grid=(2, PAIRS), in_specs=[per_pair(le...  35.4 us
    pallas_call x2, Pallas kernels, attend(): pl.pallas_call(attend_kernel, grid=(2, PAIRS), in_specs=[per_pair(length,...  35.2 us
    ppermute x12, waiting for transfers between devices, gather(): ahead = lax.ppermute(ahead, 'dp', self.right)  27.9 us
    dot_general x8, matrix products, dot_nt(): lax.dot_general(a, b, (((1,), (1,)), ((), ())), preferred_element_type=F32)  24.3 us
    dot_general x8, matrix products, matmul(): return jnp.dot(a, b, preferred_element_type=F32)  23.7 us
    ppermute x4, waiting for transfers between devices, gather(): ahead = lax.ppermute(ahead[:cut], 'dp', self.right)  18.9 us
  transfers between devices with their start and end apart: 87, of which 47 were waited for; matrix products, arithmetic and copies ran while one was open for 23% of the time, Pallas kernels for 17%

profile of v2, /device:TPU:1, one launch (start us, length us, event | category | flops | bytes accessed | tf_op | source)
XLA Modules:
  0.0 521.3 jit_solution(18044605017691083604)
XLA Ops:
  20.2 5.3 %concatenate.85.place_ref = s32[9]{0:T(128)S(1)} concatenate(s32[1]{0:T(128)} %get-tuple-element.427, s32[1]{0:T(128)} %get-tuple-element.426, s32[1]{0:T(128)} %get-tuple-element.425, s32[1]{0:T(128)} %get-tuple-element.424, s32[1]{0:T(128)} %get-tuple-element.423, s32[1]{0:T(128)} %get-tuple-element.422, s32[1]{0:T(128)} %get-tuple-element.428, s32[1]{0:T(128)} %get-tuple-element.421, ...), dimensions={0} | concatenate | bytes 72 | tf_op jit(solution)/shard_map/concatenate | solution.py:569
  28.0 8.0 %collective-permute-done.1 = bf16[112,1536]{1,0:T(8,128)(2,1)S(1)} collective-permute-done((bf16[112,1536]{1,0:T(8,128)(2,1)S(1)}, bf16[112,1536]{1,0:T(8,128)(2,1)S(1)}, u32[]{:S(2)}, u32[]{:S(2)}) %collective-permute-start.1) | collective-permute-done | bytes 344096 | tf_op jit(solution)/shard_map/ppermute | solution.py:38
  86.0 17.6 %shard_map.283 = (bf16[1024,1152]{1,0:T(8,128)(2,1)S(1)}, bf16[1024,384]{1,0:T(8,128)(2,1)S(1)}, f32[1024,384]{1,0:T(8,128)S(1)}) custom-call(f32[1024,1152]{1,0:T(8,128)S(1)} %convolution_add_fusion.1.joined_ref, f32[1024,256]{1,0:T(8,128)S(1)} %pad_maximum_fusion.4.table_ref, s32[1024,1]{1,0:T(8,128)S(1)} %bitcast.226), custom_call_target="tpu_custom_call" | custom-call | flops 20000000000 | bytes 12000000 | tf_op jit(solution)/shard_map/pallas_call | solution.py:392
  106.3 10.1 %collective-permute-start.26 = (bf16[384,384]{1,0:T(8,128)(2,1)S(1)}, bf16[384,384]{1,0:T(8,128)(2,1)S(1)}, u32[]{:S(2)}, u32[]{:S(2)}) collective-permute-start(bf16[384,384]{1,0:T(8,128)(2,1)S(1)} %get-tuple-element.185), channel_id=1, source_target_pairs={{0,1},{1,0},{2,3},{3,2},{4,5},{5,4},{6,7},{7,6},{8,9},{9,8},{10,11... | collective-permute-start | bytes 884744 | tf_op jit(solution)/shard_map/ppermute | solution.py:34
  118.1 7.4 %collective-permute-done.20.refs_7_ = bf16[96,1536]{1,0:T(8,128)(2,1)S(1)} collective-permute-done((bf16[96,1536]{1,0:T(8,128)(2,1)S(1)}, bf16[96,1536]{1,0:T(8,128)(2,1)S(1)}, u32[]{:S(2)}, u32[]{:S(2)}) %collective-permute-start.20) | collective-permute-done | bytes 294944 | tf_op jit(solution)/shard_map/ppermute | solution.py:81
  128.9 6.9 %fusion.4 = (bf16[1024,1536]{1,0:T(8,128)(2,1)}, bf16[1024,1536]{1,0:T(8,128)(2,1)S(1)}) fusion(f32[1536]{0:T(1024)S(1)} %slice_reduce_fusion.1, bf16[1024,768]{1,0:T(8,128)(2,1)S(1)} %get-tuple-element.179.two_ref, bf16[768,1536]{1,0:T(8,128)(2,1)S(1)} %get-tuple-element.180), kind=kOutput, calls=%fused_computation.6 | convolution fusion | flops 2434793472 | bytes 10229760 | tf_op jit(solution)/shard_map/dot_general | solution.py:435
  145.8 9.3 %collective-permute-start.29 = (bf16[512,768]{1,0:T(8,128)(2,1)}, bf16[512,768]{1,0:T(8,128)(2,1)}, u32[]{:S(2)}, u32[]{:S(2)}) collective-permute-start(bf16[512,768]{1,0:T(8,128)(2,1)} %select_convert_fusion.4), channel_id=1, source_target_pairs={{0,1},{1,0},{2,3},{3,2},{4,5},{5,4},{6,7},{7,6},{8,9},{9,8},{10,11... | collective-permute-start | bytes 2359304 | tf_op jit(solution)/shard_map/ppermute | solution.py:34
  180.8 5.3 %collective-permute-done.30.refs_7_ = bf16[48,1536]{1,0:T(8,128)(2,1)S(1)} collective-permute-done((bf16[48,1536]{1,0:T(8,128)(2,1)S(1)}, bf16[48,1536]{1,0:T(8,128)(2,1)S(1)}, u32[]{:S(2)}, u32[]{:S(2)}) %collective-permute-start.30) | collective-permute-done | bytes 147488 | tf_op jit(solution)/shard_map/ppermute | solution.py:81
  196.1 5.7 %collective-permute-done.32.refs_1_ = bf16[192,1536]{1,0:T(8,128)(2,1)S(1)} collective-permute-done((bf16[192,1536]{1,0:T(8,128)(2,1)S(1)}, bf16[192,1536]{1,0:T(8,128)(2,1)S(1)}, u32[]{:S(2)}, u32[]{:S(2)}) %collective-permute-start.32) | collective-permute-done | bytes 589856 | tf_op jit(solution)/shard_map/ppermute | solution.py:76
  203.3 17.6 %shard_map.286 = (bf16[1024,1152]{1,0:T(8,128)(2,1)S(1)}, bf16[1024,384]{1,0:T(8,128)(2,1)S(1)}, f32[1024,384]{1,0:T(8,128)S(1)}) custom-call(f32[1024,1152]{1,0:T(8,128)S(1)} %convolution_add_fusion.joined_ref, f32[1024,256]{1,0:T(8,128)S(1)} %pad_maximum_fusion.4.table_ref, s32[1024,1]{1,0:T(8,128)S(1)} %bitcast.227), custom_call_target="tpu_custom_call" | custom-call | flops 20000000000 | bytes 12000000 | tf_op jit(solution)/shard_map/pallas_call | solution.py:392
  227.5 5.8 %collective-permute-done.38.refs_5_ = bf16[192,1536]{1,0:T(8,128)(2,1)S(1)} collective-permute-done((bf16[192,1536]{1,0:T(8,128)(2,1)S(1)}, bf16[192,1536]{1,0:T(8,128)(2,1)S(1)}, u32[]{:S(2)}, u32[]{:S(2)}) %collective-permute-start.38) | collective-permute-done | bytes 589856 | tf_op jit(solution)/shard_map/ppermute | solution.py:76
  253.3 4.8 collective-permute-start.42
  258.1 4.9 multiply_convert_fusion.1.d_up_ref
  263.0 5.7 %shard_map.288 = bf16[8,192,1536]{2,1,0:T(8,128)(2,1)S(1)} custom-call(bf16[1024,768]{1,0:T(8,128)(2,1)S(1)} %get-tuple-element.208.two_ref, bf16[1024,1536]{1,0:T(8,128)(2,1)S(1)} %multiply_convert_fusion.1.d_up_ref, bf16[1024,1536]{1,0:T(8,128)(2,1)S(1)} %get-tuple-element.429.middle_ref, bf16[1024,768]{1,0:T(8,128)(2,1)S(1)} %pad_maximum_fusion.2.grad_ref), custom_call_target="tpu_custom_call" | custom-call | tf_op jit(solution)/shard_map/pallas_call | solution.py:678
  270.3 17.7 %shard_map.289.fused_ref = bf16[1024,1152]{1,0:T(8,128)(2,1)S(1)} custom-call(bf16[1024,1152]{1,0:T(8,128)(2,1)S(1)} %get-tuple-element.220.qkv_ref, f32[1024,384]{1,0:T(8,128)S(1)} %get-tuple-element.221.lse_ref, bf16[1024,384]{1,0:T(8,128)(2,1)S(1)} %convolution_convert_fusion.1.dctx_ref, f32[1024,256]{1,0:T(8,128)S(1)} %copy-done.15, s32[1024,1]{1,0:T(8,128)S(1)} %bitcast.228), custom_call_target="tpu_custom_call" | custom-call | flops 30000001024 | bytes 12000000 | tf_op jit(solution)/shard_map/pallas_call | solution.py:410
  296.8 5.4 %fusion.95 = f32[1024,768]{1,0:T(8,128)} fusion(bf16[1024,1152]{1,0:T(8,128)(2,1)S(1)} %shard_map.289.fused_ref, bf16[768,1152]{1,0:T(8,128)(2,1)} %copy-done.46), kind=kOutput, calls=%fused_computation.323 | convolution fusion | flops 1811939328 | bytes 7274496 | tf_op jit(solution)/shard_map/dot_general | solution.py:177
  351.3 8.3 %collective-permute-done.53 = bf16[192,1536]{1,0:T(8,128)(2,1)S(1)} collective-permute-done((bf16[192,1536]{1,0:T(8,128)(2,1)S(1)}, bf16[192,1536]{1,0:T(8,128)(2,1)S(1)}, u32[]{:S(2)}, u32[]{:S(2)}) %collective-permute-start.53) | collective-permute-done | bytes 589856 | tf_op jit(solution)/shard_map/ppermute | solution.py:104
  368.0 17.7 %shard_map.291.fused_ref = bf16[1024,1152]{1,0:T(8,128)(2,1)S(1)} custom-call(bf16[1024,1152]{1,0:T(8,128)(2,1)S(1)} %copy-done.48, f32[1024,384]{1,0:T(8,128)S(1)} %copy-done.50, bf16[1024,384]{1,0:T(8,128)(2,1)S(1)} %convolution_convert_fusion.dctx_ref, f32[1024,256]{1,0:T(8,128)S(1)} %copy-done.16, s32[1024,1]{1,0:T(8,128)S(1)} %bitcast.229), custom_call_target="tpu_custom_call" | custom-call | flops 30000001024 | bytes 12000000 | tf_op jit(solution)/shard_map/pallas_call | solution.py:410
  403.1 5.7 %shard_map.293 = bf16[8,192,1536]{2,1,0:T(8,128)(2,1)S(1)} custom-call(bf16[1024,768]{1,0:T(8,128)(2,1)S(1)} %copy-done.7, bf16[1024,1536]{1,0:T(8,128)(2,1)S(1)} %multiply_convert_fusion.d_up_ref, bf16[1024,1536]{1,0:T(8,128)(2,1)S(1)} %copy-done.13, bf16[1024,768]{1,0:T(8,128)(2,1)S(1)} %pad_maximum_fusion.3.grad_ref), custom_call_target="tpu_custom_call" | custom-call | tf_op jit(solution)/shard_map/pallas_call | solution.py:678
  426.7 8.5 %collective-permute-done.69 = bf16[192,1536]{1,0:T(8,128)(2,1)S(1)} collective-permute-done((bf16[192,1536]{1,0:T(8,128)(2,1)S(1)}, bf16[192,1536]{1,0:T(8,128)(2,1)S(1)}, u32[]{:S(2)}, u32[]{:S(2)}) %collective-permute-start.69) | collective-permute-done | bytes 589856 | tf_op jit(solution)/shard_map/ppermute | solution.py:104
  441.0 6.6 %collective-permute-done.71 = bf16[192,1536]{1,0:T(8,128)(2,1)} collective-permute-done((bf16[192,1536]{1,0:T(8,128)(2,1)}, bf16[192,1536]{1,0:T(8,128)(2,1)}, u32[]{:S(2)}, u32[]{:S(2)}) %collective-permute-start.71) | collective-permute-done | bytes 589856 | tf_op jit(solution)/shard_map/ppermute | solution.py:104
  489.8 11.4 %collective-permute-start.86 = (bf16[48,1536]{1,0:T(8,128)(2,1)S(1)}, bf16[48,1536]{1,0:T(8,128)(2,1)S(1)}, u32[]{:S(2)}, u32[]{:S(2)}) collective-permute-start(bf16[48,1536]{1,0:T(8,128)(2,1)S(1)} %select_convert_fusion.8), channel_id=1, source_target_pairs={{0,1},{1,0},{2,3},{3,2},{4,5},{5,4},{6,7},{7,6},{8,9},{9,8},{10,11... | collective-permute-start | bytes 442376 | tf_op jit(solution)/shard_map/ppermute | solution.py:34
  502.5 5.2 collective-permute-done.83
  508.1 7.3 %collective-permute-start.84 = (bf16[56,1536]{1,0:T(8,128)(2,1)S(1)}, bf16[56,1536]{1,0:T(8,128)(2,1)S(1)}, u32[]{:S(2)}, u32[]{:S(2)}) collective-permute-start(bf16[56,1536]{1,0:T(8,128)(2,1)S(1)} %select_convert_fusion.7), channel_id=1, source_target_pairs={{0,1},{1,0},{2,3},{3,2},{4,5},{5,4},{6,7},{7,6},{8,9},{9,8},{10,11... | collective-permute-start | bytes 516104 | tf_op jit(solution)/shard_map/ppermute | solution.py:34
  (602 shorter events, 289.0 us)
Async XLA Ops:
  9.9 15.5 %collective-permute-start = (bf16[56,1536]{1,0:T(8,128)(2,1)S(1)}, bf16[56,1536]{1,0:T(8,128)(2,1)S(1)}, u32[]{:S(2)}, u32[]{:S(2)}) collective-permute-start(bf16[56,1536]{1,0:T(8,128)(2,1)S(1)} %get-tuple-element.148), channel_id=1, source_target_pairs={{0,1},{1,0},{2,3},{3,2},{4,5},{5,4},{6,7},{7,6},{8,9},{9,8},{10,11... | collective-permute-start | bytes 516104 | tf_op jit(solution)/shard_map/ppermute | solution.py:34
  10.1 17.9 %collective-permute-start.2 = (bf16[48,1536]{1,0:T(8,128)(2,1)S(1)}, bf16[48,1536]{1,0:T(8,128)(2,1)S(1)}, u32[]{:S(2)}, u32[]{:S(2)}) collective-permute-start(bf16[48,1536]{1,0:T(8,128)(2,1)S(1)} %get-tuple-element.150), channel_id=1, source_target_pairs={{0,1},{1,0},{2,3},{3,2},{4,5},{5,4},{6,7},{7,6},{8,9},{9,8},{10,11... | collective-permute-start | bytes 442376 | tf_op jit(solution)/shard_map/ppermute | solution.py:34
  38.0 15.3 %collective-permute-start.3 = (bf16[192,1536]{1,0:T(8,128)(2,1)}, bf16[192,1536]{1,0:T(8,128)(2,1)}, u32[]{:S(2)}, u32[]{:S(2)}) collective-permute-start(bf16[192,1536]{1,0:T(8,128)(2,1)} %pad_maximum_fusion.6), channel_id=1, source_target_pairs={{0,16},{16,0},{1,17},{17,1},{2,18},{18,2},{3,19},{19,3},{4,20},{20... | collective-permute-start | bytes 1769480 | tf_op jit(solution)/shard_map/ppermute | solution.py:38
  40.9 19.8 %collective-permute-start.14 = (bf16[512,768]{1,0:T(8,128)(2,1)}, bf16[512,768]{1,0:T(8,128)(2,1)}, u32[]{:S(2)}, u32[]{:S(2)}) collective-permute-start(bf16[512,768]{1,0:T(8,128)(2,1)} %select_bitcast_fusion.2), channel_id=1, source_target_pairs={{0,1},{1,0},{2,3},{3,2},{4,5},{5,4},{6,7},{7,6},{8,9},{9,8},{10,11... | collective-permute-start | bytes 2359304 | tf_op jit(solution)/shard_map/ppermute | solution.py:34
  84.4 20.4 %collective-permute-start.15 = (bf16[192,1536]{1,0:T(8,128)(2,1)S(1)}, bf16[192,1536]{1,0:T(8,128)(2,1)S(1)}, u32[]{:S(2)}, u32[]{:S(2)}) collective-permute-start(bf16[192,1536]{1,0:T(8,128)(2,1)S(1)} %collective-permute-done.12.refs_1_), channel_id=1, source_target_pairs={{0,4},{1,5},{4,8},{5,9},{8,12},{9,13},{12,14},{13,15},{14,10},{15,... | collective-permute-start | bytes 1769480 | tf_op jit(solution)/shard_map/ppermute | solution.py:76
  85.3 19.4 %collective-permute-start.16 = (bf16[192,1536]{1,0:T(8,128)(2,1)S(1)}, bf16[192,1536]{1,0:T(8,128)(2,1)S(1)}, u32[]{:S(2)}, u32[]{:S(2)}) collective-permute-start(bf16[192,1536]{1,0:T(8,128)(2,1)S(1)} %collective-permute-done.13.refs_2_), channel_id=1, source_target_pairs={{0,2},{1,3},{4,0},{5,1},{8,4},{9,5},{12,8},{13,9},{14,12},{15,13},... | collective-permute-start | bytes 1769480 | tf_op jit(solution)/shard_map/ppermute | solution.py:77
  145.8 27.4 %collective-permute-start.29 = (bf16[512,768]{1,0:T(8,128)(2,1)}, bf16[512,768]{1,0:T(8,128)(2,1)}, u32[]{:S(2)}, u32[]{:S(2)}) collective-permute-start(bf16[512,768]{1,0:T(8,128)(2,1)} %select_convert_fusion.4), channel_id=1, source_target_pairs={{0,1},{1,0},{2,3},{3,2},{4,5},{5,4},{6,7},{7,6},{8,9},{9,8},{10,11... | collective-permute-start | bytes 2359304 | tf_op jit(solution)/shard_map/ppermute | solution.py:34
  156.2 23.0 %collective-permute-start.44 = (bf16[512,768]{1,0:T(8,128)(2,1)}, bf16[512,768]{1,0:T(8,128)(2,1)}, u32[]{:S(2)}, u32[]{:S(2)}) collective-permute-start(bf16[512,768]{1,0:T(8,128)(2,1)} %get-tuple-element.304), channel_id=1, source_target_pairs={{0,1},{1,0},{2,3},{3,2},{4,5},{5,4},{6,7},{7,6},{8,9},{9,8},{10,11... | collective-permute-start | bytes 2359304 | tf_op jit(solution)/shard_map/ppermute | solution.py:34
  156.2 20.1 %collective-permute-start.27 = (bf16[112,1536]{1,0:T(8,128)(2,1)}, bf16[112,1536]{1,0:T(8,128)(2,1)S(1)}, u32[]{:S(2)}, u32[]{:S(2)}) collective-permute-start(bf16[112,1536]{1,0:T(8,128)(2,1)} %collective-permute-done.24.refs_3_), channel_id=1, source_target_pairs={{0,4},{1,5},{4,8},{5,9},{8,12},{9,13},{12,14},{13,15},{14,10},{15,... | collective-permute-start | bytes 1032200 | tf_op jit(solution)/shard_map/ppermute | solution.py:76
  156.2 20.0 %collective-permute-start.28 = (bf16[112,1536]{1,0:T(8,128)(2,1)}, bf16[112,1536]{1,0:T(8,128)(2,1)S(1)}, u32[]{:S(2)}, u32[]{:S(2)}) collective-permute-start(bf16[112,1536]{1,0:T(8,128)(2,1)} %collective-permute-done.25.refs_4_), channel_id=1, source_target_pairs={{0,2},{1,3},{4,0},{5,1},{8,4},{9,5},{12,8},{13,9},{14,12},{15,13},... | collective-permute-start | bytes 1032200 | tf_op jit(solution)/shard_map/ppermute | solution.py:77
  189.5 37.0 %collective-permute-start.37 = (bf16[384,384]{1,0:T(8,128)(2,1)S(1)}, bf16[384,384]{1,0:T(8,128)(2,1)S(1)}, u32[]{:S(2)}, u32[]{:S(2)}) collective-permute-start(bf16[384,384]{1,0:T(8,128)(2,1)S(1)} %get-tuple-element.207), channel_id=1, source_target_pairs={{0,1},{1,0},{2,3},{3,2},{4,5},{5,4},{6,7},{7,6},{8,9},{9,8},{10,11... | collective-permute-start | bytes 884744 | tf_op jit(solution)/shard_map/ppermute | solution.py:34
  201.8 19.1 %collective-permute-start.35 = (bf16[192,1536]{1,0:T(8,128)(2,1)S(1)}, bf16[192,1536]{1,0:T(8,128)(2,1)S(1)}, u32[]{:S(2)}, u32[]{:S(2)}) collective-permute-start(bf16[192,1536]{1,0:T(8,128)(2,1)S(1)} %collective-permute-done.32.refs_1_), channel_id=1, source_target_pairs={{0,4},{1,5},{4,8},{5,9},{8,12},{9,13},{12,14},{13,15},{14,10},{15,... | collective-permute-start | bytes 1769480 | tf_op jit(solution)/shard_map/ppermute | solution.py:76
  201.9 19.1 %collective-permute-start.36 = (bf16[192,1536]{1,0:T(8,128)(2,1)S(1)}, bf16[192,1536]{1,0:T(8,128)(2,1)S(1)}, u32[]{:S(2)}, u32[]{:S(2)}) collective-permute-start(bf16[192,1536]{1,0:T(8,128)(2,1)S(1)} %collective-permute-done.33.refs_2_), channel_id=1, source_target_pairs={{0,2},{1,3},{4,0},{5,1},{8,4},{9,5},{12,8},{13,9},{14,12},{15,13},... | collective-permute-start | bytes 1769480 | tf_op jit(solution)/shard_map/ppermute | solution.py:77
  253.3 49.3 %collective-permute-start.42 = (bf16[512,768]{1,0:T(8,128)(2,1)}, bf16[512,768]{1,0:T(8,128)(2,1)}, u32[]{:S(2)}, u32[]{:S(2)}) collective-permute-start(bf16[512,768]{1,0:T(8,128)(2,1)} %select_convert_fusion.3), channel_id=1, source_target_pairs={{0,1},{1,0},{2,3},{3,2},{4,5},{5,4},{6,7},{7,6},{8,9},{9,8},{10,11... | collective-permute-start | bytes 2359304 | tf_op jit(solution)/shard_map/ppermute | solution.py:34
  268.8 19.2 %collective-permute-start.45 = (bf16[96,1536]{1,0:T(8,128)(2,1)S(1)}, bf16[96,1536]{1,0:T(8,128)(2,1)S(1)}, u32[]{:S(2)}, u32[]{:S(2)}) collective-permute-start(bf16[96,1536]{1,0:T(8,128)(2,1)S(1)} %get-tuple-element.218), channel_id=1, source_target_pairs={{0,4},{1,5},{4,8},{5,9},{8,12},{9,13},{12,14},{13,15},{14,10},{15,... | collective-permute-start | bytes 884744 | tf_op jit(solution)/shard_map/ppermute | solution.py:96
  270.3 17.7 %collective-permute-start.46 = (bf16[96,1536]{1,0:T(8,128)(2,1)S(1)}, bf16[96,1536]{1,0:T(8,128)(2,1)S(1)}, u32[]{:S(2)}, u32[]{:S(2)}) collective-permute-start(bf16[96,1536]{1,0:T(8,128)(2,1)S(1)} %get-tuple-element.219), channel_id=1, source_target_pairs={{0,2},{1,3},{4,0},{5,1},{8,4},{9,5},{12,8},{13,9},{14,12},{15,13},... | collective-permute-start | bytes 884744 | tf_op jit(solution)/shard_map/ppermute | solution.py:97
  307.0 33.5 %collective-permute-start.43 = (bf16[512,768]{1,0:T(8,128)(2,1)}, bf16[512,768]{1,0:T(8,128)(2,1)}, u32[]{:S(2)}, u32[]{:S(2)}) collective-permute-start(bf16[512,768]{1,0:T(8,128)(2,1)} %get-tuple-element.308), channel_id=1, source_target_pairs={{0,16},{16,0},{1,17},{17,1},{2,18},{18,2},{3,19},{19,3},{4,20},{20... | collective-permute-start | bytes 2359304 | tf_op jit(solution)/shard_map/ppermute | solution.py:38
  322.9 15.1 %collective-permute-start.50 = (bf16[192,1536]{1,0:T(8,128)(2,1)}, bf16[192,1536]{1,0:T(8,128)(2,1)}, u32[]{:S(2)}, u32[]{:S(2)}) collective-permute-start(bf16[192,1536]{1,0:T(8,128)(2,1)} %get-tuple-element.335), channel_id=1, source_target_pairs={{0,4},{1,5},{4,8},{5,9},{8,12},{9,13},{12,14},{13,15},{14,10},{15,... | collective-permute-start | bytes 1769480 | tf_op jit(solution)/shard_map/ppermute | solution.py:104
  344.6 15.0 %collective-permute-start.53 = (bf16[192,1536]{1,0:T(8,128)(2,1)S(1)}, bf16[192,1536]{1,0:T(8,128)(2,1)S(1)}, u32[]{:S(2)}, u32[]{:S(2)}) collective-permute-start(bf16[192,1536]{1,0:T(8,128)(2,1)S(1)} %get-tuple-element.333), channel_id=1, source_target_pairs={{0,4},{1,5},{4,8},{5,9},{8,12},{9,13},{12,14},{13,15},{14,10},{15,... | collective-permute-start | bytes 1769480 | tf_op jit(solution)/shard_map/ppermute | solution.py:104
  366.1 19.6 %collective-permute-start.58 = (bf16[112,1536]{1,0:T(8,128)(2,1)S(1)}, bf16[112,1536]{1,0:T(8,128)(2,1)S(1)}, u32[]{:S(2)}, u32[]{:S(2)}) collective-permute-start(bf16[112,1536]{1,0:T(8,128)(2,1)S(1)} %pad_maximum_fusion.20), channel_id=1, source_target_pairs={{0,4},{1,5},{4,8},{5,9},{8,12},{9,13},{12,14},{13,15},{14,10},{15,... | collective-permute-start | bytes 1032200 | tf_op jit(solution)/shard_map/ppermute | solution.py:104
  366.8 19.0 %collective-permute-start.59 = (bf16[112,1536]{1,0:T(8,128)(2,1)S(1)}, bf16[112,1536]{1,0:T(8,128)(2,1)S(1)}, u32[]{:S(2)}, u32[]{:S(2)}) collective-permute-start(bf16[112,1536]{1,0:T(8,128)(2,1)S(1)} %pad_maximum_fusion.21), channel_id=1, source_target_pairs={{0,2},{1,3},{4,0},{5,1},{8,4},{9,5},{12,8},{13,9},{14,12},{15,13},... | collective-permute-start | bytes 1032200 | tf_op jit(solution)/shard_map/ppermute | solution.py:105
  403.0 17.1 %collective-permute-start.66 = (bf16[384,384]{1,0:T(8,128)(2,1)}, bf16[384,384]{1,0:T(8,128)(2,1)}, u32[]{:S(2)}, u32[]{:S(2)}) collective-permute-start(bf16[384,384]{1,0:T(8,128)(2,1)} %broadcast_select_fusion.17), channel_id=1, source_target_pairs={{0,1},{1,0},{2,3},{3,2},{4,5},{5,4},{6,7},{7,6},{8,9},{9,8},{10,11... | collective-permute-start | bytes 884744 | tf_op jit(solution)/shard_map/ppermute | solution.py:34
  441.0 21.9 %collective-permute-start.65 = (bf16[512,768]{1,0:T(8,128)(2,1)}, bf16[512,768]{1,0:T(8,128)(2,1)}, u32[]{:S(2)}, u32[]{:S(2)}) collective-permute-start(bf16[512,768]{1,0:T(8,128)(2,1)} %select_convert_fusion), channel_id=1, source_target_pairs={{0,16},{16,0},{1,17},{17,1},{2,18},{18,2},{3,19},{19,3},{4,20},{20... | collective-permute-start | bytes 2359304 | tf_op jit(solution)/shard_map/ppermute | solution.py:38
  489.8 25.6 %collective-permute-start.86 = (bf16[48,1536]{1,0:T(8,128)(2,1)S(1)}, bf16[48,1536]{1,0:T(8,128)(2,1)S(1)}, u32[]{:S(2)}, u32[]{:S(2)}) collective-permute-start(bf16[48,1536]{1,0:T(8,128)(2,1)S(1)} %select_convert_fusion.8), channel_id=1, source_target_pairs={{0,1},{1,0},{2,3},{3,2},{4,5},{5,4},{6,7},{7,6},{8,9},{9,8},{10,11... | collective-permute-start | bytes 442376 | tf_op jit(solution)/shard_map/ppermute | solution.py:34
  (176 other events, 1904.7 us)

commit v3 on v2

--- a/solution.py
+++ b/solution.py
@@ -47,12 +47,9 @@
     def __init__(self, n):
         self.chips = n // 2
         self.order = ring_order(self.chips)
-        place = [0] * self.chips
-        for position, chip in enumerate(self.order):
-            place[chip] = position
         chip = lax.axis_index("dp") // 2
-        self.position = jnp.asarray(place, jnp.int32)[chip]
-        self.table = jnp.asarray(self.order, jnp.int32)
+        row = chip // 2
+        self.position = jnp.where(chip % 2 == 0, row, self.chips - 1 - row)
         self.right = self.route(1)
         self.left = self.route(-1)
 
@@ -65,7 +62,9 @@
         return pairs
 
     def chip_at(self, offset):
-        return self.table[lax.rem(self.position + offset + self.chips, self.chips)]
+        at = (self.position + offset + self.chips) % self.chips
+        turn = at >= self.chips // 2
+        return 2 * jnp.where(turn, self.chips - 1 - at, at) + turn.astype(jnp.int32)
 
     def gather(self, own):
         (own,) = yield [own]
@@ -86,7 +85,7 @@
     def found_at(self):
         reach = self.chips // 2
         offsets = [0] + [o for k in range(1, reach) for o in (-k, k)] + [reach]
-        return jnp.stack([self.chip_at(o) for o in offsets])
+        return self.chip_at(jnp.asarray(np.array(offsets, np.int32)))
 
     def scatter(self, block_of, rows):
         reach = self.chips // 2
@@ -138,10 +137,23 @@
                 self.active = self.waiting.pop(0)
                 self.held, last = lax.optimization_barrier((next(self.active[1]), last))
 
+
+class Tracks:
+    def __init__(self):
+        self.rows = (Track(), Track())
+
+    def push(self, row, name, steps):
+        self.rows[row].push(name, steps)
+
+    def step(self, values=()):
+        for row in self.rows:
+            values = row.step(values)
+        return values
+
     def finish(self, name):
-        while name not in self.done:
+        while all(name not in row.done for row in self.rows):
             self.step()
-        return self.done[name]
+        return {**self.rows[0].done, **self.rows[1].done}[name]
 
 
 def add_low(one, two):
@@ -167,7 +179,7 @@
 
 
 def turned(x, table, sign):
-    lane = lax.rem(lax.broadcasted_iota(jnp.int32, x.shape, 1), HEAD_DIM)
+    lane = lax.broadcasted_iota(jnp.int32, x.shape, 1) & (HEAD_DIM - 1)
     partner = jnp.where(lane < ROT // 2, pltpu.roll(x, PAIR - ROT // 2, 1), pltpu.roll(x, ROT // 2, 1))
     moved = partner * table[:, PAIR:]
     return x * table[:, :PAIR] + moved if sign > 0 else x * table[:, :PAIR] - moved
@@ -189,69 +201,64 @@
 
 def attend_kernel(joined_ref, table_ref, begin_ref, qkv_ref, ctx_ref, lse_ref):
     length = joined_ref.shape[0]
+    table = table_ref[...]
+    query = turned(joined_ref[:, :PAIR], table, 1).astype(BF16)
+    key = turned(joined_ref[:, PAIR : 2 * PAIR], table, 1).astype(BF16)
+    value = joined_ref[:, 2 * PAIR :].astype(BF16)
+    qkv_ref[:, :PAIR] = query
+    qkv_ref[:, PAIR : 2 * PAIR] = key
+    qkv_ref[:, 2 * PAIR :] = value
+    allowed = kept(begin_ref[...], 0, length, length)
+    first = lax.broadcasted_iota(jnp.int32, (length, PAIR), 1) < HEAD_DIM
+    scaled = query.astype(F32) * SCALE
+    heads = [jnp.where(first == (h == 0), scaled, 0.0).astype(BF16) for h in range(2)]
+    scores = [jnp.where(allowed, dot_nt(q, key), -1e30) for q in heads]
+    peaks = [jnp.max(s, axis=1, keepdims=True) for s in scores]
+    exps = [jnp.exp(s - p) for s, p in zip(scores, peaks)]
+    totals = [jnp.sum(e, axis=1, keepdims=True) for e in exps]
+    ctx = [
+        jnp.dot(e.astype(BF16), value, preferred_element_type=F32) * (1.0 / t) for e, t in zip(exps, totals)
+    ]
+    lses = [p + jnp.log(t) for p, t in zip(peaks, totals)]
+    ctx_ref[...] = jnp.where(first, ctx[0], ctx[1]).astype(BF16)
+    lse_ref[...] = jnp.where(first, lses[0], lses[1])
+
+
+def attend_back_kernel(qkv_ref, lse_ref, dctx_ref, table_ref, begin_ref, out_ref):
+    length = qkv_ref.shape[0]
     chunk = length // 2
-    table = table_ref[...]
-    qkv_ref[:, :PAIR] = turned(joined_ref[:, :PAIR], table, 1).astype(BF16)
-    qkv_ref[:, PAIR : 2 * PAIR] = turned(joined_ref[:, PAIR : 2 * PAIR], table, 1).astype(BF16)
-    qkv_ref[:, 2 * PAIR :] = joined_ref[:, 2 * PAIR :].astype(BF16)
+    first = lax.broadcasted_iota(jnp.int32, (chunk, PAIR), 1) < HEAD_DIM
+    parts = []
     for i in range(2):
         rows, keys = pl.ds(i * chunk, chunk), (i + 1) * chunk
         allowed = kept(begin_ref[rows, :], i * chunk, chunk, keys)
-        ctx, lse = [], []
-        for h in range(2):
-            q = qkv_ref[rows, h * HEAD_DIM : (h + 1) * HEAD_DIM] * jnp.asarray(SCALE, BF16)
-            k = qkv_ref[:keys, PAIR + h * HEAD_DIM : PAIR + (h + 1) * HEAD_DIM]
-            v = qkv_ref[:keys, 2 * PAIR + h * HEAD_DIM : 2 * PAIR + (h + 1) * HEAD_DIM]
-            score = jnp.where(allowed, dot_nt(q, k), -1e30)
-            peak = jnp.max(score, axis=1, keepdims=True)
-            e = jnp.exp(score - peak)
-            total = jnp.sum(e, axis=1, keepdims=True)
-            prob = (e * (1.0 / total)).astype(BF16)
-            ctx.append(jnp.dot(prob, v, preferred_element_type=F32))
-            lse.append(jnp.broadcast_to(peak + jnp.log(total), (chunk, HEAD_DIM)))
-        ctx_ref[rows, :] = jnp.concatenate(ctx, axis=1).astype(BF16)
-        lse_ref[rows, :] = jnp.concatenate(lse, axis=1)
-
-
-def attend_back_kernel(qkv_ref, lse_ref, dctx_ref, table_ref, begin_ref, out_ref):
-    length = qkv_ref.shape[0]
-    chunk = length // 2
-    dqs, dks, dvs = [], [], []
-    for h in range(2):
-        head = slice(h * HEAD_DIM, (h + 1) * HEAD_DIM)
-        k_at = slice(PAIR + h * HEAD_DIM, PAIR + (h + 1) * HEAD_DIM)
-        v_at = slice(2 * PAIR + h * HEAD_DIM, 2 * PAIR + (h + 1) * HEAD_DIM)
-        dq, dk, dv = [], None, None
-        for i in (1, 0):
-            rows, keys = pl.ds(i * chunk, chunk), (i + 1) * chunk
-            allowed = kept(begin_ref[rows, :], i * chunk, chunk, keys)
-            q = qkv_ref[rows, head] * jnp.asarray(SCALE, BF16)
-            k, v = qkv_ref[:keys, k_at], qkv_ref[:keys, v_at]
-            do = dctx_ref[rows, head]
-            lse = lse_ref[rows, h * HEAD_DIM : h * HEAD_DIM + 1]
-            p = jnp.exp(jnp.where(allowed, dot_nt(q, k) - lse, -1e30))
-            part_v = dot_tn(p.astype(BF16), do)
-            dp = dot_nt(do, v)
-            inner = jnp.sum(p * dp, axis=1, keepdims=True)
-            ds = (p * (dp - inner)).astype(BF16)
-            dq.append(jnp.dot(ds, k, preferred_element_type=F32) * SCALE)
-            part_k = dot_tn(ds, q)
-            if dk is None:
-                dk, dv = part_k, part_v
-            else:
-                dk = jnp.concatenate([dk[:chunk] + part_k, dk[chunk:]])
-                dv = jnp.concatenate([dv[:chunk] + part_v, dv[chunk:]])
-        dqs.append(jnp.concatenate([dq[1], dq[0]]))
-        dks.append(dk)
-        dvs.append(dv)
+        key, value = qkv_ref[:keys, PAIR : 2 * PAIR], qkv_ref[:keys, 2 * PAIR :]
+        scaled, grad = qkv_ref[rows, :PAIR].astype(F32) * SCALE, dctx_ref[rows, :].astype(F32)
+        qs = [jnp.where(first == (h == 0), scaled, 0.0).astype(BF16) for h in range(2)]
+        dos = [jnp.where(first == (h == 0), grad, 0.0).astype(BF16) for h in range(2)]
+        lses = [lse_ref[rows, h * HEAD_DIM : h * HEAD_DIM + 1] for h in range(2)]
+        ps = [jnp.exp(jnp.where(allowed, dot_nt(q, key) - lse, -1e30)) for q, lse in zip(qs, lses)]
+        dps = [dot_nt(do, value) for do in dos]
+        inner = [jnp.sum(p * dp, axis=1, keepdims=True) for p, dp in zip(ps, dps)]
+        dss = [(p * (dp - m)).astype(BF16) for p, dp, m in zip(ps, dps, inner)]
+        dqs = [jnp.dot(ds, key, preferred_element_type=F32) for ds in dss]
+        dv = dot_tn(ps[0].astype(BF16), dos[0]) + dot_tn(ps[1].astype(BF16), dos[1])
+        dk = dot_tn(dss[0], qs[0]) + dot_tn(dss[1], qs[1])
+        parts.append((jnp.where(first, dqs[0], dqs[1]) * SCALE, dk, dv))
+    (dq0, dk0, dv0), (dq1, dk1, dv1) = parts
     table = table_ref[...]
-    out_ref[:, :PAIR] = turned(jnp.concatenate(dqs, axis=1), table, -1).astype(BF16)
-    out_ref[:, PAIR : 2 * PAIR] = turned(jnp.concatenate(dks, axis=1), table, -1).astype(BF16)
-    out_ref[:, 2 * PAIR :] = jnp.concatenate(dvs, axis=1).astype(BF16)
+    out_ref[:, :PAIR] = turned(jnp.concatenate([dq0, dq1]), table, -1).astype(BF16)
+    dk = jnp.concatenate([dk0 + dk1[:chunk], dk1[chunk:]])
+    out_ref[:, PAIR : 2 * PAIR] = turned(dk, table, -1).astype(BF16)
+    out_ref[:, 2 * PAIR :] = jnp.concatenate([dv0 + dv1[:chunk], dv1[chunk:]]).astype(BF16)
 
 
 def smem():
     return pl.BlockSpec(memory_space=pltpu.SMEM)
+
+
+def whole(shape):
+    return pl.BlockSpec(shape, lambda i: (0,) * len(shape))
 
 
 def vmem():
@@ -347,6 +354,14 @@
         down_ref[pl.ds(pl.multiple_of(chip * 2 * u + u, 16), u), :] = down[:, D:]
 
 
+def assemble_whole_kernel(every_ref, up_ref, down_ref):
+    u = every_ref.shape[1] // 2
+    for chip in range(every_ref.shape[0]):
+        up_ref[u * chip : u * (chip + 1), :] = every_ref[chip, :u, :]
+        down_ref[2 * u * chip : 2 * u * chip + u, :] = every_ref[chip, u:, :D]
+        down_ref[2 * u * chip + u : 2 * u * (chip + 1), :] = every_ref[chip, u:, D:]
+
+
 def grads_mlp_kernel(two_ref, d_up_ref, middle_ref, grad_ref, out_ref):
     count, u = out_ref.shape[0], out_ref.shape[1] // 2
     up = dot_tn(two_ref[...], d_up_ref[...]).astype(BF16)
@@ -463,10 +478,10 @@
     (d_up,) = track.step((d_up,))
     send_hidden(two, d_up, middle, grad)
     d_ctx = dot_nt(grad, weights["out"]).astype(BF16)
-    (d_ctx, d_up) = track.step((d_ctx, d_up))
+    d_two = dot_nt(d_up, weights["up"])
+    (d_ctx, d_two) = track.step((d_ctx, d_two))
     d_fused = attend_back(qkv, lse, d_ctx, table, begin)
-    (d_fused, d_up) = track.step((d_fused, d_up))
-    d_two = dot_nt(d_up, weights["up"])
+    (d_fused,) = track.step((d_fused,))
     d_one = dot_nt(d_fused, weights["qkv"])
     d_one, d_two = track.step((d_one, d_two))
     normed, scale = normalized(source.astype(F32))
@@ -517,22 +532,24 @@
     low_core, low_section = core == 0, section == 0
     ring = Ring(n) if chips == 8 else None
 
-    track = Track()
+    track = Tracks()
 
     vectors = (ln1_gain, ln1_bias, ln2_gain, ln2_bias, qkv_bias, out_bias, up_bias, down_bias)
     core_scalar = core[None].astype(jnp.int32)
+    weights_in = (qkv_weight, out_weight, up_weight, down_weight)
 
     def packed():
         if ring is not None:
             shapes = [(r + 8, LANES)] * 2 + [(r, LANES)] * 2 + [(u, LANES)]
             return pl.pallas_call(
                 pack_kernel,
-                in_specs=[smem()] + [vmem()] * (4 + len(vectors)),
+                grid=(1,),
+                in_specs=[smem()] + [whole(v.shape) for v in weights_in + vectors],
                 out_specs=[vmem()] * 5,
                 out_shape=[jax.ShapeDtypeStruct(shape, BF16) for shape in shapes],
                 scratch_shapes=[pltpu.VMEM((8, LANES), F32)],
                 compiler_params=kernel_params(),
-            )(core_scalar, qkv_weight, out_weight, up_weight, down_weight, *vectors)
+            )(core_scalar, *weights_in, *vectors)
         rows = jnp.concatenate([jnp.pad(v, ((0, 0), (0, LANES - v.shape[1]))) for v in vectors])
         attn, hidden = [], []
         for t in (0, 1):
@@ -561,12 +578,10 @@
     other = swap_section(mlp_block)
     mlp_blocks = (pick(low_section, mlp_block, other), pick(low_section, other, mlp_block))
 
-    for layer in (0, 1):
-        for kind, blocks in (("attn", attn_blocks), ("mlp", mlp_blocks)):
-            if ring is not None:
-                track.push((kind, layer), ring.gather(blocks[layer]))
-
-    place = None if ring is None else jnp.concatenate([ring.found_at().astype(jnp.int32), core_scalar])
+    if ring is not None:
+        track.push(0, ("attn", 0), ring.gather(attn_blocks[0]))
+
+    place = None if ring is None else jnp.append(ring.found_at(), core)
 
     def gathered(own):
         return lax.all_gather(own, "dp", axis=0, axis_index_groups=same_core(n))
@@ -608,7 +623,15 @@
         return {"qkv": qkv, "out": out, **dict(zip(names, found))}
 
     def mlp_weights(layer):
-        if ring is None:
+        if layer == 1 and ring is not None:
+            up, down = pl.pallas_call(
+                assemble_whole_kernel,
+                in_specs=[vmem()],
+                out_specs=[vmem()] * 2,
+                out_shape=[jax.ShapeDtypeStruct((D, FFH), BF16), jax.ShapeDtypeStruct((FFH, D), BF16)],
+                compiler_params=kernel_params(),
+            )(every_mlp_1)
+        elif ring is None:
             every = gathered(mlp_blocks[layer])
             up, folded = every[:, :u].reshape(D, FFH), every[:, u:]
             down = jnp.stack([folded[:, :, :D], folded[:, :, D:]], axis=1).reshape(FFH, D)
@@ -645,7 +668,11 @@
     table, begin = rotary_tables(paired(own_seg[None]))
     both = paired(both)
 
+    every_mlp_1 = None if ring is None else gathered(mlp_blocks[1])
     weights_0 = attn_weights(0)
+    if ring is not None:
+        track.push(0, ("attn", 1), ring.gather(attn_blocks[1]))
+        track.push(1, ("mlp", 0), ring.gather(mlp_blocks[0]))
     saved_0 = forward_attend(both, weights_0, table, begin, track)
     weights_0.update(mlp_weights(0))
     part, saved_0 = forward_hidden(saved_0, weights_0, track)
@@ -661,12 +688,12 @@
     outputs = jnp.stack([pick(low_section, kept_rows, got), pick(low_section, got, kept_rows)])
 
     def reduce_group(name, group):
-        if ring is None:
+        if ring is None or name == ("d_mlp", 1):
             total = lax.psum_scatter(group, "dp", scatter_dimension=0, axis_index_groups=same_core(n))
-            track.done[name] = total.astype(F32)
+            track.rows[0].done[name] = total.astype(F32)
             return
         block_of = lambda chip: lax.dynamic_index_in_dim(group, chip, 0, keepdims=False)
-        track.push(name, ring.scatter(block_of, group.shape[1]))
+        track.push(int(name[0] == "d_mlp"), name, ring.scatter(block_of, group.shape[1]))
 
     def send_mlp(layer, two, d_up, middle, grad):
         if ring is None:

time: 530 us -> 536 us (1.011)
  waiting for transfers between devices: 132 us -> 181 us
  Pallas kernels: 92 us -> 64.8 us
  other arithmetic: 79.8 us -> 61.6 us
  matrix products: 49.7 us -> 58.6 us
  between operations: 24.2 us -> 16.8 us
  starting transfers between devices: 112 us -> 105 us
  local copies, waits for them, and re-layouts: 31.4 us -> 37.7 us
    pallas_call x2, Pallas kernels: 35.2 us -> 18.6 us  [attend(): pl.pallas_call(attend_kernel, grid=(2, PAIRS), in_specs=[per_pair(length,...]
    ppermute x16 -> x12, waiting for transfers between devices: 11.8 us -> 26.4 us  [scatter(): back = lax.ppermute(back, 'dp', self.left)]
    unnamed x246 -> x284, local copies, waits for them, and re-layouts: 18.5 us -> 30 us
    all_gather x0 -> x1, waiting for transfers between devices: none -> 10.5 us  [gathered(): return lax.all_gather(own, 'dp', axis=0, axis_index_groups=same_core(n))]
    ppermute x6, waiting for transfers between devices: 16.5 us -> 26.9 us  [swap_section(): return lax.ppermute(block, 'section', [(0, 1), (1, 0)])]
    pallas_call x2, Pallas kernels: 35.4 us -> 25.4 us  [attend_back(): pl.pallas_call(attend_back_kernel, grid=(2, PAIRS), in_specs=[per_pair(le...]
    ppermute x16 -> x12, waiting for transfers between devices: 46.9 us -> 55.9 us  [scatter(): ahead = lax.ppermute(ahead, 'dp', self.right)]
    ppermute x12 -> x9, starting transfers between devices: 11.4 us -> 2.64 us  [gather(): back = lax.ppermute(back, 'dp', self.left)]
  transfers between devices with their start and end apart: 87 -> 73, of which waited for: 47 -> 40; matrix products, arithmetic and copies ran while one was open for 23% -> 19% of each run, Pallas kernels for 17% -> 12%
where the time goes in v3:
time: 536 us; the launch traced here: 526 us
  waiting for transfers between devices  181 us (34%)
  starting transfers between devices  105 us (20%)
  Pallas kernels  64.8 us (12%)
  other arithmetic  61.6 us (11%)
  matrix products  58.6 us (11%)
  local copies, waits for them, and re-layouts  37.7 us (7%)
  between operations  16.8 us (3%)
    ppermute x12, waiting for transfers between devices, scatter(): ahead = lax.ppermute(ahead, 'dp', self.right)  55.9 us
    ppermute x17, starting transfers between devices, swap_core(): return lax.ppermute(block, 'dp', [(i, i ^ 1) for i in range(n)])  49.8 us
    ppermute x9, waiting for transfers between devices, gather(): ahead = lax.ppermute(ahead, 'dp', self.right)  34.5 us
    unnamed x284, local copies, waits for them, and re-layouts  30 us
    dot_general x8, matrix products, dot_nt(): lax.dot_general(a, b, (((1,), (1,)), ((), ())), preferred_element_type=F32)  28.8 us
    ppermute x6, waiting for transfers between devices, swap_section(): return lax.ppermute(block, 'section', [(0, 1), (1, 0)])  26.9 us
    ppermute x12, waiting for transfers between devices, scatter(): back = lax.ppermute(back, 'dp', self.left)  26.4 us
    dot_general x8, matrix products, matmul(): return jnp.dot(a, b, preferred_element_type=F32)  25.6 us
  transfers between devices with their start and end apart: 73, of which 40 were waited for; matrix products, arithmetic and copies ran while one was open for 19% of the time, Pallas kernels for 12%

profile of v3, /device:TPU:1, one launch (start us, length us, event | category | flops | bytes accessed | tf_op | source)
XLA Modules:
  0.0 525.8 jit_solution(9119068127608334847)
XLA Ops:
  22.9 8.0 %collective-permute-done.3 = bf16[112,1536]{1,0:T(8,128)(2,1)S(1)} collective-permute-done((bf16[112,1536]{1,0:T(8,128)(2,1)S(1)}, bf16[112,1536]{1,0:T(8,128)(2,1)S(1)}, u32[]{:S(2)}, u32[]{:S(2)}) %collective-permute-start.3) | collective-permute-done | bytes 344096 | tf_op jit(solution)/shard_map/ppermute | solution.py:38
  74.7 9.3 %shard_map.274 = (bf16[1024,1152]{1,0:T(8,128)(2,1)S(1)}, bf16[1024,384]{1,0:T(8,128)(2,1)S(1)}, f32[1024,384]{1,0:T(8,128)S(1)}) custom-call(f32[1024,1152]{1,0:T(8,128)S(1)} %convolution_add_fusion.1.joined_ref, f32[1024,256]{1,0:T(8,128)S(1)} %pad_maximum_fusion.4.table_ref, s32[1024,1]{1,0:T(8,128)S(1)} %bitcast.184), custom_call_target="tpu_custom_call" | custom-call | flops 20000000000 | bytes 12000000 | tf_op jit(solution)/shard_map/pallas_call | solution.py:407
  91.8 8.8 %collective-permute-done.19.refs_3_ = bf16[192,1536]{1,0:T(8,128)(2,1)S(1)} collective-permute-done((bf16[192,1536]{1,0:T(8,128)(2,1)S(1)}, bf16[192,1536]{1,0:T(8,128)(2,1)S(1)}, u32[]{:S(2)}, u32[]{:S(2)}) %collective-permute-start.19) | collective-permute-done | bytes 589856 | tf_op jit(solution)/shard_map/ppermute | solution.py:75
  103.8 11.5 %collective-permute-start.18 = (bf16[384,384]{1,0:T(8,128)(2,1)S(1)}, bf16[384,384]{1,0:T(8,128)(2,1)S(1)}, u32[]{:S(2)}, u32[]{:S(2)}) collective-permute-start(bf16[384,384]{1,0:T(8,128)(2,1)S(1)} %get-tuple-element.155), channel_id=1, source_target_pairs={{0,1},{1,0},{2,3},{3,2},{4,5},{5,4},{6,7},{7,6},{8,9},{9,8},{10,11... | collective-permute-start | bytes 884744 | tf_op jit(solution)/shard_map/ppermute | solution.py:34
  118.5 7.2 %collective-permute-done.23.refs_7_ = bf16[96,1536]{1,0:T(8,128)(2,1)S(1)} collective-permute-done((bf16[96,1536]{1,0:T(8,128)(2,1)S(1)}, bf16[96,1536]{1,0:T(8,128)(2,1)S(1)}, u32[]{:S(2)}, u32[]{:S(2)}) %collective-permute-start.23) | collective-permute-done | bytes 294944 | tf_op jit(solution)/shard_map/ppermute | solution.py:80
  138.5 8.6 %collective-permute-start.25 = (bf16[512,768]{1,0:T(8,128)(2,1)}, bf16[512,768]{1,0:T(8,128)(2,1)}, u32[]{:S(2)}, u32[]{:S(2)}) collective-permute-start(bf16[512,768]{1,0:T(8,128)(2,1)} %select_convert_fusion.4), channel_id=1, source_target_pairs={{0,1},{1,0},{2,3},{3,2},{4,5},{5,4},{6,7},{7,6},{8,9},{9,8},{10,11... | collective-permute-start | bytes 2359304 | tf_op jit(solution)/shard_map/ppermute | solution.py:34
  148.7 8.2 %collective-permute-done.27.refs_3_ = bf16[112,1536]{1,0:T(8,128)(2,1)S(1)} collective-permute-done((bf16[112,1536]{1,0:T(8,128)(2,1)S(1)}, bf16[112,1536]{1,0:T(8,128)(2,1)S(1)}, u32[]{:S(2)}, u32[]{:S(2)}) %collective-permute-start.27) | collective-permute-done | bytes 344096 | tf_op jit(solution)/shard_map/ppermute | solution.py:75
  198.1 9.3 %shard_map.277 = (bf16[1024,1152]{1,0:T(8,128)(2,1)S(1)}, bf16[1024,384]{1,0:T(8,128)(2,1)S(1)}, f32[1024,384]{1,0:T(8,128)S(1)}) custom-call(f32[1024,1152]{1,0:T(8,128)S(1)} %convolution_add_fusion.joined_ref, f32[1024,256]{1,0:T(8,128)S(1)} %pad_maximum_fusion.4.table_ref, s32[1024,1]{1,0:T(8,128)S(1)} %bitcast.185), custom_call_target="tpu_custom_call" | custom-call | flops 20000000000 | bytes 12000000 | tf_op jit(solution)/shard_map/pallas_call | solution.py:407
  208.7 12.7 %shard_map.279.fused_ref = bf16[1024,1152]{1,0:T(8,128)(2,1)S(1)} custom-call(bf16[1024,1152]{1,0:T(8,128)(2,1)S(1)} %get-tuple-element.182.qkv_ref, f32[1024,384]{1,0:T(8,128)S(1)} %get-tuple-element.183.lse_ref, bf16[1024,384]{1,0:T(8,128)(2,1)S(1)} %convolution_convert_fusion.1.dctx_ref, f32[1024,256]{1,0:T(8,128)S(1)} %pad_maximum_fusion.4.table_ref, ...), custom_call_target="tpu_custom_call" | custom-call | flops 30000001024 | bytes 12000000 | tf_op jit(solution)/shard_map/pallas_call | solution.py:425
  229.0 10.5 %all-gather.3.cloned.1.call-done = bf16[1536,1536]{1,0:T(8,128)(2,1)} async-done(((bf16[192,1536]{1,0:T(8,128)(2,1)}), bf16[1536,1536]{1,0:T(8,128)(2,1)}) %all-gather.3.cloned.1.call-update) | async-done | bytes 4718608 | tf_op jit(solution)/shard_map/all_gather | solution.py:587
  276.4 5.7 %shard_map.284 = bf16[8,192,1536]{2,1,0:T(8,128)(2,1)S(1)} custom-call(bf16[1024,768]{1,0:T(8,128)(2,1)S(1)} %copy-done.10, bf16[1024,1536]{1,0:T(8,128)(2,1)S(1)} %copy-done.21, bf16[1024,1536]{1,0:T(8,128)(2,1)S(1)} %copy-done.19, bf16[1024,768]{1,0:T(8,128)(2,1)S(1)} %copy-done.8), custom_call_target="tpu_custom_call" | custom-call | tf_op jit(solution)/shard_map/pallas_call | solution.py:705
  291.6 7.1 %multiply_convert_fusion.d_up_ref = bf16[1024,1536]{1,0:T(8,128)(2,1)S(1)} fusion(bf16[1536,768]{1,0:T(8,128)(2,1)S(1)} %copy-done.53, f32[1024,1536]{1,0:T(8,128)} %get-tuple-element.360, f32[1536]{0:T(1024)S(1)} %slice_reduce_fusion.1, bf16[512,768]{1,0:T(8,128)(2,1)S(1)} %get-tuple-element.305, bf16[512,768]{1,0:T(8,128)(2,1)S(1)} %get-tuple-element.304), kind=kOutput, calls=%fused_computation.13 | convolution fusion | flops 2439512064 | bytes 13375488 | tf_op jit(solution)/shard_map/dot_general | solution.py:189
  299.0 6.2 %collective-permute-done.40 = bf16[64,1536]{1,0:T(8,128)(2,1)S(1)} collective-permute-done((bf16[64,1536]{1,0:T(8,128)(2,1)}, bf16[64,1536]{1,0:T(8,128)(2,1)S(1)}, u32[]{:S(2)}, u32[]{:S(2)}) %collective-permute-start.40) | collective-permute-done | bytes 196640 | tf_op jit(solution)/shard_map/ppermute | solution.py:96
  320.5 5.7 %shard_map.281 = bf16[8,192,1536]{2,1,0:T(8,128)(2,1)S(1)} custom-call(bf16[1024,768]{1,0:T(8,128)(2,1)S(1)} %copy-done.7, bf16[1024,1536]{1,0:T(8,128)(2,1)S(1)} %multiply_convert_fusion.d_up_ref, bf16[1024,1536]{1,0:T(8,128)(2,1)S(1)} %copy-done.18, bf16[1024,768]{1,0:T(8,128)(2,1)S(1)} %copy-done.11), custom_call_target="tpu_custom_call" | custom-call | tf_op jit(solution)/shard_map/pallas_call | solution.py:705
  328.2 7.1 %collective-permute-done.43 = bf16[112,1536]{1,0:T(8,128)(2,1)S(1)} collective-permute-done((bf16[112,1536]{1,0:T(8,128)(2,1)S(1)}, bf16[112,1536]{1,0:T(8,128)(2,1)S(1)}, u32[]{:S(2)}, u32[]{:S(2)}) %collective-permute-start.43) | collective-permute-done | bytes 344096 | tf_op jit(solution)/shard_map/ppermute | solution.py:104
  340.3 12.7 %shard_map.282.fused_ref = bf16[1024,1152]{1,0:T(8,128)(2,1)S(1)} custom-call(bf16[1024,1152]{1,0:T(8,128)(2,1)S(1)} %copy-done.61, f32[1024,384]{1,0:T(8,128)S(1)} %copy-done.63, bf16[1024,384]{1,0:T(8,128)(2,1)S(1)} %convolution_convert_fusion.dctx_ref, f32[1024,256]{1,0:T(8,128)S(1)} %copy-done.24, s32[1024,1]{1,0:T(8,128)S(1)} %bitcast.187), custom_call_target="tpu_custom_call" | custom-call | flops 30000001024 | bytes 12000000 | tf_op jit(solution)/shard_map/pallas_call | solution.py:425
  353.1 7.4 %collective-permute-done.44 = bf16[96,1536]{1,0:T(8,128)(2,1)S(1)} collective-permute-done((bf16[96,1536]{1,0:T(8,128)(2,1)S(1)}, bf16[96,1536]{1,0:T(8,128)(2,1)S(1)}, u32[]{:S(2)}, u32[]{:S(2)}) %collective-permute-start.44) | collective-permute-done | bytes 294944 | tf_op jit(solution)/shard_map/ppermute | solution.py:95
  369.0 23.1 %collective-permute-done.50 = bf16[112,1536]{1,0:T(8,128)(2,1)S(1)} collective-permute-done((bf16[112,1536]{1,0:T(8,128)(2,1)S(1)}, bf16[112,1536]{1,0:T(8,128)(2,1)S(1)}, u32[]{:S(2)}, u32[]{:S(2)}) %collective-permute-start.50) | collective-permute-done | bytes 344096 | tf_op jit(solution)/shard_map/ppermute | solution.py:103
  392.1 5.8 %collective-permute-start.54 = (bf16[384,384]{1,0:T(8,128)(2,1)}, bf16[384,384]{1,0:T(8,128)(2,1)S(1)}, u32[]{:S(2)}, u32[]{:S(2)}) collective-permute-start(bf16[384,384]{1,0:T(8,128)(2,1)} %broadcast_select_fusion.17), channel_id=1, source_target_pairs={{0,1},{1,0},{2,3},{3,2},{4,5},{5,4},{6,7},{7,6},{8,9},{9,8},{10,11... | collective-permute-start | bytes 884744 | tf_op jit(solution)/shard_map/ppermute | solution.py:34
  437.3 5.8 %collective-permute-done.52 = bf16[192,1536]{1,0:T(8,128)(2,1)S(1)} collective-permute-done((bf16[192,1536]{1,0:T(8,128)(2,1)S(1)}, bf16[192,1536]{1,0:T(8,128)(2,1)S(1)}, u32[]{:S(2)}, u32[]{:S(2)}) %collective-permute-start.52) | collective-permute-done | bytes 589856 | tf_op jit(solution)/shard_map/ppermute | solution.py:103
  445.9 7.4 %collective-permute-done.60 = bf16[112,1536]{1,0:T(8,128)(2,1)S(1)} collective-permute-done((bf16[112,1536]{1,0:T(8,128)(2,1)S(1)}, bf16[112,1536]{1,0:T(8,128)(2,1)S(1)}, u32[]{:S(2)}, u32[]{:S(2)}) %collective-permute-start.60) | collective-permute-done | bytes 344096 | tf_op jit(solution)/shard_map/ppermute | solution.py:104
  466.6 7.7 %collective-permute-done.67 = bf16[192,1536]{1,0:T(8,128)(2,1)S(1)} collective-permute-done((bf16[192,1536]{1,0:T(8,128)(2,1)S(1)}, bf16[192,1536]{1,0:T(8,128)(2,1)S(1)}, u32[]{:S(2)}, u32[]{:S(2)}) %collective-permute-start.67) | collective-permute-done | bytes 589856 | tf_op jit(solution)/shard_map/ppermute | solution.py:103
  474.9 6.8 %collective-permute-done.63 = bf16[112,1536]{1,0:T(8,128)(2,1)S(1)} collective-permute-done((bf16[112,1536]{1,0:T(8,128)(2,1)S(1)}, bf16[112,1536]{1,0:T(8,128)(2,1)S(1)}, u32[]{:S(2)}, u32[]{:S(2)}) %collective-permute-start.63) | collective-permute-done | bytes 344096 | tf_op jit(solution)/shard_map/ppermute | solution.py:103
  500.9 11.5 %collective-permute-done.69 = bf16[192,1536]{1,0:T(8,128)(2,1)S(1)} collective-permute-done((bf16[192,1536]{1,0:T(8,128)(2,1)S(1)}, bf16[192,1536]{1,0:T(8,128)(2,1)S(1)}, u32[]{:S(2)}, u32[]{:S(2)}) %collective-permute-start.69) | collective-permute-done | bytes 589856 | tf_op jit(solution)/shard_map/ppermute | solution.py:38
  (604 shorter events, 294.9 us)
Async XLA Ops:
  7.2 232.3 %all-gather.3.cloned.1.call-start = ((), (), s32[]{:S(2)}) async-start(), calls=%async_computation.2 | async-start | bytes 5308416 | tf_op jit(solution)/shard_map/all_gather | solution.py:587
  35.8 19.8 %collective-permute-start.4 = (bf16[512,768]{1,0:T(8,128)(2,1)}, bf16[512,768]{1,0:T(8,128)(2,1)}, u32[]{:S(2)}, u32[]{:S(2)}) collective-permute-start(bf16[512,768]{1,0:T(8,128)(2,1)} %select_bitcast_fusion.2), channel_id=1, source_target_pairs={{0,1},{1,0},{2,3},{3,2},{4,5},{5,4},{6,7},{7,6},{8,9},{9,8},{10,11... | collective-permute-start | bytes 2359304 | tf_op jit(solution)/shard_map/ppermute | solution.py:34
  116.5 43.3 %collective-permute-start.36 = (bf16[512,768]{1,0:T(8,128)(2,1)}, bf16[512,768]{1,0:T(8,128)(2,1)}, u32[]{:S(2)}, u32[]{:S(2)}) collective-permute-start(bf16[512,768]{1,0:T(8,128)(2,1)} %get-tuple-element.259), channel_id=1, source_target_pairs={{0,1},{1,0},{2,3},{3,2},{4,5},{5,4},{6,7},{7,6},{8,9},{9,8},{10,11... | collective-permute-start | bytes 2359304 | tf_op jit(solution)/shard_map/ppermute | solution.py:34
  138.5 30.3 %collective-permute-start.25 = (bf16[512,768]{1,0:T(8,128)(2,1)}, bf16[512,768]{1,0:T(8,128)(2,1)}, u32[]{:S(2)}, u32[]{:S(2)}) collective-permute-start(bf16[512,768]{1,0:T(8,128)(2,1)} %select_convert_fusion.4), channel_id=1, source_target_pairs={{0,1},{1,0},{2,3},{3,2},{4,5},{5,4},{6,7},{7,6},{8,9},{9,8},{10,11... | collective-permute-start | bytes 2359304 | tf_op jit(solution)/shard_map/ppermute | solution.py:34
  159.7 336.1 %reduce-scatter.2.cloned.1.call-start = ((), (), s32[]{:S(2)}) async-start(), calls=%async_computation.1 | async-start | bytes 5308416 | tf_op jit(solution)/shard_map/reduce_scatter | solution.py:692
  171.0 19.4 %collective-permute-start.26 = (bf16[512,768]{1,0:T(8,128)(2,1)S(1)}, bf16[512,768]{1,0:T(8,128)(2,1)S(1)}, u32[]{:S(2)}, u32[]{:S(2)}) collective-permute-start(bf16[512,768]{1,0:T(8,128)(2,1)S(1)} %add_convert_fusion.1), channel_id=1, source_target_pairs={{0,1},{1,0},{2,3},{3,2},{4,5},{5,4},{6,7},{7,6},{8,9},{9,8},{10,11... | collective-permute-start | bytes 2359304 | tf_op jit(solution)/shard_map/ppermute | solution.py:34
  272.0 19.4 %collective-permute-start.41 = (bf16[512,768]{1,0:T(8,128)(2,1)S(1)}, bf16[512,768]{1,0:T(8,128)(2,1)S(1)}, u32[]{:S(2)}, u32[]{:S(2)}) collective-permute-start(bf16[512,768]{1,0:T(8,128)(2,1)S(1)} %get-tuple-element.186), channel_id=1, source_target_pairs={{0,1},{1,0},{2,3},{3,2},{4,5},{5,4},{6,7},{7,6},{8,9},{9,8},{10,11... | collective-permute-start | bytes 2359304 | tf_op jit(solution)/shard_map/ppermute | solution.py:34
  289.5 145.1 %collective-permute-start.34 = (bf16[512,768]{1,0:T(8,128)(2,1)}, bf16[512,768]{1,0:T(8,128)(2,1)}, u32[]{:S(2)}, u32[]{:S(2)}) collective-permute-start(bf16[512,768]{1,0:T(8,128)(2,1)} %select_convert_fusion.3), channel_id=1, source_target_pairs={{0,1},{1,0},{2,3},{3,2},{4,5},{5,4},{6,7},{7,6},{8,9},{9,8},{10,11... | collective-permute-start | bytes 2359304 | tf_op jit(solution)/shard_map/ppermute | solution.py:34
  314.5 20.8 %collective-permute-start.43 = (bf16[112,1536]{1,0:T(8,128)(2,1)S(1)}, bf16[112,1536]{1,0:T(8,128)(2,1)S(1)}, u32[]{:S(2)}, u32[]{:S(2)}) collective-permute-start(bf16[112,1536]{1,0:T(8,128)(2,1)S(1)} %pad_maximum_fusion.19), channel_id=1, source_target_pairs={{0,2},{1,3},{4,0},{5,1},{8,4},{9,5},{12,8},{13,9},{14,12},{15,13},... | collective-permute-start | bytes 1032200 | tf_op jit(solution)/shard_map/ppermute | solution.py:104
  315.7 19.7 %collective-permute-start.42 = (bf16[112,1536]{1,0:T(8,128)(2,1)S(1)}, bf16[112,1536]{1,0:T(8,128)(2,1)S(1)}, u32[]{:S(2)}, u32[]{:S(2)}) collective-permute-start(bf16[112,1536]{1,0:T(8,128)(2,1)S(1)} %pad_maximum_fusion.18), channel_id=1, source_target_pairs={{0,4},{1,5},{4,8},{5,9},{8,12},{9,13},{12,14},{13,15},{14,10},{15,... | collective-permute-start | bytes 1032200 | tf_op jit(solution)/shard_map/ppermute | solution.py:103
  335.5 17.5 %collective-permute-start.46 = (bf16[112,1536]{1,0:T(8,128)(2,1)S(1)}, bf16[112,1536]{1,0:T(8,128)(2,1)S(1)}, u32[]{:S(2)}, u32[]{:S(2)}) collective-permute-start(bf16[112,1536]{1,0:T(8,128)(2,1)S(1)} %get-tuple-element.293), channel_id=1, source_target_pairs={{0,4},{1,5},{4,8},{5,9},{8,12},{9,13},{12,14},{13,15},{14,10},{15,... | collective-permute-start | bytes 1032200 | tf_op jit(solution)/shard_map/ppermute | solution.py:103
  338.8 21.6 %collective-permute-start.44 = (bf16[96,1536]{1,0:T(8,128)(2,1)S(1)}, bf16[96,1536]{1,0:T(8,128)(2,1)S(1)}, u32[]{:S(2)}, u32[]{:S(2)}) collective-permute-start(bf16[96,1536]{1,0:T(8,128)(2,1)S(1)} %get-tuple-element.192), channel_id=1, source_target_pairs={{0,4},{1,5},{4,8},{5,9},{8,12},{9,13},{12,14},{13,15},{14,10},{15,... | collective-permute-start | bytes 884744 | tf_op jit(solution)/shard_map/ppermute | solution.py:95
  338.8 23.4 %collective-permute-start.45 = (bf16[96,1536]{1,0:T(8,128)(2,1)S(1)}, bf16[96,1536]{1,0:T(8,128)(2,1)S(1)}, u32[]{:S(2)}, u32[]{:S(2)}) collective-permute-start(bf16[96,1536]{1,0:T(8,128)(2,1)S(1)} %get-tuple-element.193), channel_id=1, source_target_pairs={{0,2},{1,3},{4,0},{5,1},{8,4},{9,5},{12,8},{13,9},{14,12},{15,13},... | collective-permute-start | bytes 884744 | tf_op jit(solution)/shard_map/ppermute | solution.py:96
  362.5 35.4 %collective-permute-start.49 = (bf16[192,1536]{1,0:T(8,128)(2,1)S(1)}, bf16[192,1536]{1,0:T(8,128)(2,1)S(1)}, u32[]{:S(2)}, u32[]{:S(2)}) collective-permute-start(bf16[192,1536]{1,0:T(8,128)(2,1)S(1)} %pad_maximum_fusion.11), channel_id=1, source_target_pairs={{0,2},{1,3},{4,0},{5,1},{8,4},{9,5},{12,8},{13,9},{14,12},{15,13},... | collective-permute-start | bytes 1769480 | tf_op jit(solution)/shard_map/ppermute | solution.py:104
  364.9 33.9 %collective-permute-start.48 = (bf16[192,1536]{1,0:T(8,128)(2,1)S(1)}, bf16[192,1536]{1,0:T(8,128)(2,1)}, u32[]{:S(2)}, u32[]{:S(2)}) collective-permute-start(bf16[192,1536]{1,0:T(8,128)(2,1)S(1)} %pad_maximum_fusion.10), channel_id=1, source_target_pairs={{0,4},{1,5},{4,8},{5,9},{8,12},{9,13},{12,14},{13,15},{14,10},{15,... | collective-permute-start | bytes 1769480 | tf_op jit(solution)/shard_map/ppermute | solution.py:103
  365.1 26.9 %collective-permute-start.50 = (bf16[112,1536]{1,0:T(8,128)(2,1)S(1)}, bf16[112,1536]{1,0:T(8,128)(2,1)S(1)}, u32[]{:S(2)}, u32[]{:S(2)}) collective-permute-start(bf16[112,1536]{1,0:T(8,128)(2,1)S(1)} %get-tuple-element.291), channel_id=1, source_target_pairs={{0,4},{1,5},{4,8},{5,9},{8,12},{9,13},{12,14},{13,15},{14,10},{15,... | collective-permute-start | bytes 1032200 | tf_op jit(solution)/shard_map/ppermute | solution.py:103
  365.3 32.6 %collective-permute-start.51 = (bf16[112,1536]{1,0:T(8,128)(2,1)S(1)}, bf16[112,1536]{1,0:T(8,128)(2,1)S(1)}, u32[]{:S(2)}, u32[]{:S(2)}) collective-permute-start(bf16[112,1536]{1,0:T(8,128)(2,1)S(1)} %get-tuple-element.290), channel_id=1, source_target_pairs={{0,2},{1,3},{4,0},{5,1},{8,4},{9,5},{12,8},{13,9},{14,12},{15,13},... | collective-permute-start | bytes 1032200 | tf_op jit(solution)/shard_map/ppermute | solution.py:104
  430.8 22.5 %collective-permute-start.60 = (bf16[112,1536]{1,0:T(8,128)(2,1)S(1)}, bf16[112,1536]{1,0:T(8,128)(2,1)S(1)}, u32[]{:S(2)}, u32[]{:S(2)}) collective-permute-start(bf16[112,1536]{1,0:T(8,128)(2,1)S(1)} %pad_maximum_fusion.21), channel_id=1, source_target_pairs={{0,2},{1,3},{4,0},{5,1},{8,4},{9,5},{12,8},{13,9},{14,12},{15,13},... | collective-permute-start | bytes 1032200 | tf_op jit(solution)/shard_map/ppermute | solution.py:104
  432.0 21.2 %collective-permute-start.59 = (bf16[112,1536]{1,0:T(8,128)(2,1)S(1)}, bf16[112,1536]{1,0:T(8,128)(2,1)S(1)}, u32[]{:S(2)}, u32[]{:S(2)}) collective-permute-start(bf16[112,1536]{1,0:T(8,128)(2,1)S(1)} %pad_maximum_fusion.20), channel_id=1, source_target_pairs={{0,4},{1,5},{4,8},{5,9},{8,12},{9,13},{12,14},{13,15},{14,10},{15,... | collective-permute-start | bytes 1032200 | tf_op jit(solution)/shard_map/ppermute | solution.py:103
  436.2 28.7 %collective-permute-start.35 = (bf16[512,768]{1,0:T(8,128)(2,1)S(1)}, bf16[512,768]{1,0:T(8,128)(2,1)S(1)}, u32[]{:S(2)}, u32[]{:S(2)}) collective-permute-start(bf16[512,768]{1,0:T(8,128)(2,1)S(1)} %get-tuple-element.260), channel_id=1, source_target_pairs={{0,16},{16,0},{1,17},{17,1},{2,18},{18,2},{3,19},{19,3},{4,20},{20... | collective-permute-start | bytes 2359304 | tf_op jit(solution)/shard_map/ppermute | solution.py:38
  455.2 19.2 %collective-permute-start.67 = (bf16[192,1536]{1,0:T(8,128)(2,1)S(1)}, bf16[192,1536]{1,0:T(8,128)(2,1)S(1)}, u32[]{:S(2)}, u32[]{:S(2)}) collective-permute-start(bf16[192,1536]{1,0:T(8,128)(2,1)S(1)} %get-tuple-element.271), channel_id=1, source_target_pairs={{0,4},{1,5},{4,8},{5,9},{8,12},{9,13},{12,14},{13,15},{14,10},{15,... | collective-permute-start | bytes 1769480 | tf_op jit(solution)/shard_map/ppermute | solution.py:103
  456.4 18.5 %collective-permute-start.68 = (bf16[192,1536]{1,0:T(8,128)(2,1)S(1)}, bf16[192,1536]{1,0:T(8,128)(2,1)S(1)}, u32[]{:S(2)}, u32[]{:S(2)}) collective-permute-start(bf16[192,1536]{1,0:T(8,128)(2,1)S(1)} %get-tuple-element.270), channel_id=1, source_target_pairs={{0,2},{1,3},{4,0},{5,1},{8,4},{9,5},{12,8},{13,9},{14,12},{15,13},... | collective-permute-start | bytes 1769480 | tf_op jit(solution)/shard_map/ppermute | solution.py:104
  461.7 21.9 %collective-permute-start.56 = (bf16[512,768]{1,0:T(8,128)(2,1)S(1)}, bf16[512,768]{1,0:T(8,128)(2,1)S(1)}, u32[]{:S(2)}, u32[]{:S(2)}) collective-permute-start(bf16[512,768]{1,0:T(8,128)(2,1)S(1)} %select_convert_fusion), channel_id=1, source_target_pairs={{0,16},{16,0},{1,17},{17,1},{2,18},{18,2},{3,19},{19,3},{4,20},{20... | collective-permute-start | bytes 2359304 | tf_op jit(solution)/shard_map/ppermute | solution.py:38
  462.9 18.8 %collective-permute-start.63 = (bf16[112,1536]{1,0:T(8,128)(2,1)S(1)}, bf16[112,1536]{1,0:T(8,128)(2,1)S(1)}, u32[]{:S(2)}, u32[]{:S(2)}) collective-permute-start(bf16[112,1536]{1,0:T(8,128)(2,1)S(1)} %get-tuple-element.283), channel_id=1, source_target_pairs={{0,4},{1,5},{4,8},{5,9},{8,12},{9,13},{12,14},{13,15},{14,10},{15,... | collective-permute-start | bytes 1032200 | tf_op jit(solution)/shard_map/ppermute | solution.py:103
  (181 other events, 2345.4 us)
Sparse Core Ops, SparseCore 0:
  159.8 79.6 all-gather.2
  284.4 121.6 reduce-scatter.1

commit v4 on v3

--- a/solution.py
+++ b/solution.py
@@ -110,50 +110,38 @@
         return own.astype(F32) + ahead.astype(F32) + back.astype(F32)
 
 
-class Track:
-    def __init__(self):
-        self.waiting, self.active, self.held = [], None, []
-        self.done = {}
-
-    def push(self, name, steps):
-        self.waiting.append((name, steps))
-
-    def step(self, values=()):
-        if self.active is None:
-            if not self.waiting:
-                return values
-            self.active = self.waiting.pop(0)
-            self.held = next(self.active[1])
-        self.held, values = lax.optimization_barrier((self.held, values))
-        while True:
-            try:
-                self.held = self.active[1].send(self.held)
-                return values
-            except StopIteration as end:
-                self.done[self.active[0]] = end.value
-                last, self.active = self.held, None
-                if not self.waiting:
-                    return values
-                self.active = self.waiting.pop(0)
-                self.held, last = lax.optimization_barrier((next(self.active[1]), last))
-
-
 class Tracks:
     def __init__(self):
-        self.rows = (Track(), Track())
+        self.waiting, self.active, self.done = ([], []), [None, None], {}
 
     def push(self, row, name, steps):
-        self.rows[row].push(name, steps)
+        self.waiting[row].append((name, steps))
 
     def step(self, values=()):
-        for row in self.rows:
-            values = row.step(values)
+        for row in (0, 1):
+            if self.active[row] is None and self.waiting[row]:
+                name, steps = self.waiting[row].pop(0)
+                self.active[row] = (name, steps, next(steps))
+        held = [a[2] if a else [] for a in self.active]
+        held, values = lax.optimization_barrier((held, values))
+        for row in (0, 1):
+            if self.active[row]:
+                name, steps, _ = self.active[row]
+                try:
+                    self.active[row] = (name, steps, steps.send(held[row]))
+                except StopIteration as end:
+                    self.done[name] = end.value
+                    self.active[row] = None
+                    if self.waiting[row]:
+                        name, steps = self.waiting[row].pop(0)
+                        first, _ = lax.optimization_barrier((next(steps), held[row]))
+                        self.active[row] = (name, steps, steps.send(first))
         return values
 
     def finish(self, name):
-        while all(name not in row.done for row in self.rows):
+        while name not in self.done:
             self.step()
-        return {**self.rows[0].done, **self.rows[1].done}[name]
+        return self.done[name]
 
 
 def add_low(one, two):
@@ -354,14 +342,6 @@
         down_ref[pl.ds(pl.multiple_of(chip * 2 * u + u, 16), u), :] = down[:, D:]
 
 
-def assemble_whole_kernel(every_ref, up_ref, down_ref):
-    u = every_ref.shape[1] // 2
-    for chip in range(every_ref.shape[0]):
-        up_ref[u * chip : u * (chip + 1), :] = every_ref[chip, :u, :]
-        down_ref[2 * u * chip : 2 * u * chip + u, :] = every_ref[chip, u:, :D]
-        down_ref[2 * u * chip + u : 2 * u * (chip + 1), :] = every_ref[chip, u:, D:]
-
-
 def grads_mlp_kernel(two_ref, d_up_ref, middle_ref, grad_ref, out_ref):
     count, u = out_ref.shape[0], out_ref.shape[1] // 2
     up = dot_tn(two_ref[...], d_up_ref[...]).astype(BF16)
@@ -472,18 +452,22 @@
     return part, (*saved, middle, slope)
 
 
-def backward(saved, grad, weights, table, begin, track, send_hidden):
-    source, one, two, qkv, ctx, lse, middle, slope = saved
-    d_up = (dot_nt(grad, weights["down"]) * slope.astype(F32)).astype(BF16)
-    (d_up,) = track.step((d_up,))
-    send_hidden(two, d_up, middle, grad)
+def back_attend(saved, grad, weights, table, begin, track):
+    qkv, lse = saved[3], saved[5]
     d_ctx = dot_nt(grad, weights["out"]).astype(BF16)
-    d_two = dot_nt(d_up, weights["up"])
-    (d_ctx, d_two) = track.step((d_ctx, d_two))
     d_fused = attend_back(qkv, lse, d_ctx, table, begin)
     (d_fused,) = track.step((d_fused,))
     d_one = dot_nt(d_fused, weights["qkv"])
-    d_one, d_two = track.step((d_one, d_two))
+    return d_fused, d_one
+
+
+def back_hidden(slope, grad, weights, track):
+    d_up = (dot_nt(grad, weights["down"]) * slope.astype(F32)).astype(BF16)
+    (d_up,) = track.step((d_up,))
+    return d_up, dot_nt(d_up, weights["up"])
+
+
+def back_norms(source, d_one, d_two, weights):
     normed, scale = normalized(source.astype(F32))
     mixed = d_one * weights["g1"] + d_two * weights["g2"]
     part = scale * (
@@ -491,17 +475,13 @@
         - jnp.mean(mixed, axis=-1, keepdims=True)
         - normed * jnp.mean(mixed * normed, axis=-1, keepdims=True)
     )
-    small = (
+    sums = (
         jnp.sum(d_one * normed, axis=0),
         jnp.sum(d_one, axis=0),
         jnp.sum(d_two * normed, axis=0),
         jnp.sum(d_two, axis=0),
-        jnp.sum(d_fused.astype(F32), axis=0),
-        None,
-        jnp.sum(d_up.astype(F32), axis=0),
-        None,
     )
-    return part, d_fused, small
+    return part, sums
 
 
 def body(
@@ -623,15 +603,7 @@
         return {"qkv": qkv, "out": out, **dict(zip(names, found))}
 
     def mlp_weights(layer):
-        if layer == 1 and ring is not None:
-            up, down = pl.pallas_call(
-                assemble_whole_kernel,
-                in_specs=[vmem()],
-                out_specs=[vmem()] * 2,
-                out_shape=[jax.ShapeDtypeStruct((D, FFH), BF16), jax.ShapeDtypeStruct((FFH, D), BF16)],
-                compiler_params=kernel_params(),
-            )(every_mlp_1)
-        elif ring is None:
+        if ring is None:
             every = gathered(mlp_blocks[layer])
             up, folded = every[:, :u].reshape(D, FFH), every[:, u:]
             down = jnp.stack([folded[:, :, :D], folded[:, :, D:]], axis=1).reshape(FFH, D)
@@ -668,10 +640,10 @@
     table, begin = rotary_tables(paired(own_seg[None]))
     both = paired(both)
 
-    every_mlp_1 = None if ring is None else gathered(mlp_blocks[1])
     weights_0 = attn_weights(0)
     if ring is not None:
         track.push(0, ("attn", 1), ring.gather(attn_blocks[1]))
+        track.push(0, ("mlp", 1), ring.gather(mlp_blocks[1]))
         track.push(1, ("mlp", 0), ring.gather(mlp_blocks[0]))
     saved_0 = forward_attend(both, weights_0, table, begin, track)
     weights_0.update(mlp_weights(0))
@@ -680,17 +652,10 @@
     (mid,) = track.step((mid,))
     both = paired(mid)
     weights_1 = attn_weights(1)
-    saved_1 = forward_attend(both, weights_1, table, begin, track)
-    weights_1.update(mlp_weights(1))
-    part, saved_1 = forward_hidden(saved_1, weights_1, track)
-    last = (mid.astype(F32) + summed(part) + weights_1["bout"]).astype(BF16)
-    kept_rows, got = pick(low_section, mid, last), swap_section(pick(low_section, last, mid))
-    outputs = jnp.stack([pick(low_section, kept_rows, got), pick(low_section, got, kept_rows)])
-
     def reduce_group(name, group):
-        if ring is None or name == ("d_mlp", 1):
+        if ring is None:
             total = lax.psum_scatter(group, "dp", scatter_dimension=0, axis_index_groups=same_core(n))
-            track.rows[0].done[name] = total.astype(F32)
+            track.done[name] = total.astype(F32)
             return
         block_of = lambda chip: lax.dynamic_index_in_dim(group, chip, 0, keepdims=False)
         track.push(int(name[0] == "d_mlp"), name, ring.scatter(block_of, group.shape[1]))
@@ -757,20 +722,41 @@
         got = swap_core(pick(low_core, *halves[::-1]))
         return jnp.concatenate([pick(low_core, kept_columns, got), pick(low_core, got, kept_columns)])
 
-    def back(layer, saved, weights, low_grad):
-        grad = paired(low_grad)
-        part, d_fused, small = backward(
-            saved, grad, weights, table, begin, track, lambda *parts: send_mlp(layer, *parts)
-        )
-        out_rows = out_rows_of(saved[4], grad)
-        send_attn(layer, saved[1], d_fused, out_rows, small, jnp.sum(low_grad.astype(F32), axis=0))
-        return part
-
-    part = back(1, saved_1, weights_1, cot_low)
+    def sums_of(rows):
+        return jnp.sum(rows.astype(F32), axis=0)
+
+    grad = paired(cot_low)
+    saved_1 = forward_attend(both, weights_1, table, begin, track)
+    d_fused, d_one = back_attend(saved_1, grad, weights_1, table, begin, track)
+    out_rows = out_rows_of(saved_1[4], grad)
+    (d_one, out_rows) = track.step((d_one, out_rows))
+    weights_1.update(mlp_weights(1))
+    part, (source, one, two, _, _, _, middle, slope) = forward_hidden(saved_1, weights_1, track)
+    last = (mid.astype(F32) + summed(part) + weights_1["bout"]).astype(BF16)
+    kept_rows, got = pick(low_section, mid, last), swap_section(pick(low_section, last, mid))
+    outputs = jnp.stack([pick(low_section, kept_rows, got), pick(low_section, got, kept_rows)])
+    d_up, d_two = back_hidden(slope, grad, weights_1, track)
+    send_mlp(1, two, d_up, middle, grad)
+    (d_two,) = track.step((d_two,))
+    part, sums = back_norms(source, d_one, d_two, weights_1)
+    small = (*sums, sums_of(d_fused), None, sums_of(d_up))
+    (part,) = track.step((part,))
+    send_attn(1, one, d_fused, out_rows, small, sums_of(cot_low))
     grad_1 = own_cot + summed(part)
     low_1 = grad_1.astype(BF16)
     (low_1, grad_1) = track.step((low_1, grad_1))
-    part = back(0, saved_0, weights_0, low_1)
+
+    source, one, two, _, ctx, _, middle, slope = saved_0
+    grad = paired(low_1)
+    d_up, d_two = back_hidden(slope, grad, weights_0, track)
+    send_mlp(0, two, d_up, middle, grad)
+    (d_two,) = track.step((d_two,))
+    out_rows = out_rows_of(ctx, grad)
+    d_fused, d_one = back_attend(saved_0, grad, weights_0, table, begin, track)
+    (d_one,) = track.step((d_one,))
+    part, sums = back_norms(source, d_one, d_two, weights_0)
+    small = (*sums, sums_of(d_fused), None, sums_of(d_up))
+    send_attn(0, one, d_fused, out_rows, small, sums_of(low_1))
     grad_0 = low_1.astype(F32) + summed(part)
     (grad_0,) = track.step((grad_0,))
     sent = swap_section(pick(low_section, grad_1, grad_0).astype(BF16)).astype(F32)

time: 536 us -> 505 us (0.942)
  waiting for transfers between devices: 181 us -> 150 us
  other arithmetic: 61.6 us -> 80.9 us
  between operations: 16.8 us -> 3.37 us
  starting transfers between devices: 105 us -> 99.5 us
    ppermute x12 -> x16, waiting for transfers between devices: 55.9 us -> 27.8 us  [scatter(): ahead = lax.ppermute(ahead, 'dp', self.right)]
    all_gather x1 -> x0, waiting for transfers between devices: 10.5 us -> none  [gathered(): return lax.all_gather(own, 'dp', axis=0, axis_index_groups=same_core(n))]
    ppermute x12 -> x16, starting transfers between devices: 15.1 us -> 6.94 us  [scatter(): back = lax.ppermute(back, 'dp', self.left)]
    convert_element_type x11 -> x14, other arithmetic: 4.78 us -> 12.6 us  [add_low(): return (one.astype(F32) + two.astype(F32)).astype(BF16)]
    dot_general x8, matrix products: 28.8 us -> 21.8 us  [dot_nt(): lax.dot_general(a, b, (((1,), (1,)), ((), ())), preferred_element_type=F32)]
    ppermute x9 -> x12, waiting for transfers between devices: 34.5 us -> 41.5 us  [gather(): ahead = lax.ppermute(ahead, 'dp', self.right)]
    ppermute x17, starting transfers between devices: 49.8 us -> 42.9 us  [swap_core(): return lax.ppermute(block, 'dp', [(i, i ^ 1) for i in range(n)])]
    ppermute x9 -> x12, waiting for transfers between devices: 9.61 us -> 14.9 us  [gather(): back = lax.ppermute(back, 'dp', self.left)]
  transfers between devices with their start and end apart: 73 -> 87, of which waited for: 40 -> 41; matrix products, arithmetic and copies ran while one was open for 19% -> 24% of each run, Pallas kernels for 12% -> 8%
where the time goes in v4:
time: 505 us; the launch traced here: 496 us
  waiting for transfers between devices  150 us (30%)
  starting transfers between devices  99.5 us (20%)
  other arithmetic  80.9 us (16%)
  Pallas kernels  65.2 us (13%)
  matrix products  54 us (11%)
  local copies, waits for them, and re-layouts  42.3 us (8%)
    ppermute x17, starting transfers between devices, swap_core(): return lax.ppermute(block, 'dp', [(i, i ^ 1) for i in range(n)])  42.9 us
    ppermute x12, waiting for transfers between devices, gather(): ahead = lax.ppermute(ahead, 'dp', self.right)  41.5 us
    unnamed x290, local copies, waits for them, and re-layouts  34.7 us
    dot_general x8, matrix products, matmul(): return jnp.dot(a, b, preferred_element_type=F32)  28.1 us
    ppermute x16, waiting for transfers between devices, scatter(): ahead = lax.ppermute(ahead, 'dp', self.right)  27.8 us
    ppermute x16, waiting for transfers between devices, scatter(): back = lax.ppermute(back, 'dp', self.left)  26.8 us
    pallas_call x2, Pallas kernels, attend_back(): pl.pallas_call(attend_back_kernel, grid=(2, PAIRS), in_specs=[per_pair(le...  26 us
    ppermute x6, waiting for transfers between devices, swap_section(): return lax.ppermute(block, 'section', [(0, 1), (1, 0)])  22.1 us
  transfers between devices with their start and end apart: 87, of which 41 were waited for; matrix products, arithmetic and copies ran while one was open for 24% of the time, Pallas kernels for 8%

profile of v4, /device:TPU:1, one launch (start us, length us, event | category | flops | bytes accessed | tf_op | source)
XLA Modules:
  0.0 495.7 jit_solution(9676673430803308794)
XLA Ops:
  16.3 8.0 %collective-permute-done.3 = bf16[112,1536]{1,0:T(8,128)(2,1)S(1)} collective-permute-done((bf16[112,1536]{1,0:T(8,128)(2,1)S(1)}, bf16[112,1536]{1,0:T(8,128)(2,1)S(1)}, u32[]{:S(2)}, u32[]{:S(2)}) %collective-permute-start.3) | collective-permute-done | bytes 344096 | tf_op jit(solution)/shard_map/ppermute | solution.py:38
  32.9 4.4 collective-permute-done.6.refs_2_
  69.1 9.3 %shard_map.274 = (bf16[1024,1152]{1,0:T(8,128)(2,1)S(1)}, bf16[1024,384]{1,0:T(8,128)(2,1)S(1)}, f32[1024,384]{1,0:T(8,128)S(1)}) custom-call(f32[1024,1152]{1,0:T(8,128)S(1)} %convolution_add_fusion.1.joined_ref, f32[1024,256]{1,0:T(8,128)S(1)} %pad_maximum_fusion.4.table_ref, s32[1024,1]{1,0:T(8,128)S(1)} %bitcast.212), custom_call_target="tpu_custom_call" | custom-call | flops 20000000000 | bytes 12000000 | tf_op jit(solution)/shard_map/pallas_call | solution.py:387
  87.0 15.5 %collective-permute-done.18.refs_3_ = bf16[112,1536]{1,0:T(8,128)(2,1)S(1)} collective-permute-done((bf16[112,1536]{1,0:T(8,128)(2,1)S(1)}, bf16[112,1536]{1,0:T(8,128)(2,1)S(1)}, u32[]{:S(2)}, u32[]{:S(2)}) %collective-permute-start.18) | collective-permute-done | bytes 344096 | tf_op jit(solution)/shard_map/ppermute | solution.py:75
  105.7 11.8 %collective-permute-start.34 = (bf16[384,384]{1,0:T(8,128)(2,1)S(1)}, bf16[384,384]{1,0:T(8,128)(2,1)S(1)}, u32[]{:S(2)}, u32[]{:S(2)}) collective-permute-start(bf16[384,384]{1,0:T(8,128)(2,1)S(1)} %get-tuple-element.188), channel_id=1, source_target_pairs={{0,1},{1,0},{2,3},{3,2},{4,5},{5,4},{6,7},{7,6},{8,9},{9,8},{10,11... | collective-permute-start | bytes 884744 | tf_op jit(solution)/shard_map/ppermute | solution.py:34
  121.6 7.8 %collective-permute-start.44 = (bf16[512,768]{1,0:T(8,128)(2,1)}, bf16[512,768]{1,0:T(8,128)(2,1)}, u32[]{:S(2)}, u32[]{:S(2)}) collective-permute-start(bf16[512,768]{1,0:T(8,128)(2,1)} %get-tuple-element.295), channel_id=1, source_target_pairs={{0,1},{1,0},{2,3},{3,2},{4,5},{5,4},{6,7},{7,6},{8,9},{9,8},{10,11... | collective-permute-start | bytes 2359304 | tf_op jit(solution)/shard_map/ppermute | solution.py:34
  132.8 8.4 %collective-permute-done.26.refs_7_ = bf16[48,1536]{1,0:T(8,128)(2,1)S(1)} collective-permute-done((bf16[48,1536]{1,0:T(8,128)(2,1)S(1)}, bf16[48,1536]{1,0:T(8,128)(2,1)S(1)}, u32[]{:S(2)}, u32[]{:S(2)}) %collective-permute-start.26) | collective-permute-done | bytes 147488 | tf_op jit(solution)/shard_map/ppermute | solution.py:80
  144.9 6.9 %fusion.4 = (bf16[1024,1536]{1,0:T(8,128)(2,1)}, bf16[1024,1536]{1,0:T(8,128)(2,1)S(1)}) fusion(f32[1536]{0:T(1024)S(1)} %slice_reduce_fusion.1, bf16[1024,768]{1,0:T(8,128)(2,1)S(1)} %get-tuple-element.180.two_ref, bf16[768,1536]{1,0:T(8,128)(2,1)S(1)} %get-tuple-element.183), kind=kOutput, calls=%fused_computation.6 | convolution fusion | flops 2434793472 | bytes 10229760 | tf_op jit(solution)/shard_map/dot_general | solution.py:430
  151.7 4.8 collective-permute-done.31.refs_2_
  161.7 7.9 %collective-permute-done.32.refs_3_ = bf16[192,1536]{1,0:T(8,128)(2,1)S(1)} collective-permute-done((bf16[192,1536]{1,0:T(8,128)(2,1)S(1)}, bf16[192,1536]{1,0:T(8,128)(2,1)S(1)}, u32[]{:S(2)}, u32[]{:S(2)}) %collective-permute-start.32) | collective-permute-done | bytes 589856 | tf_op jit(solution)/shard_map/ppermute | solution.py:75
  181.3 9.1 %collective-permute-done.35.refs_5_ = bf16[192,1536]{1,0:T(8,128)(2,1)S(1)} collective-permute-done((bf16[192,1536]{1,0:T(8,128)(2,1)S(1)}, bf16[192,1536]{1,0:T(8,128)(2,1)S(1)}, u32[]{:S(2)}, u32[]{:S(2)}) %collective-permute-start.35) | collective-permute-done | bytes 589856 | tf_op jit(solution)/shard_map/ppermute | solution.py:75
  207.3 6.9 %fusion.9 = (bf16[1024,1536]{1,0:T(8,128)(2,1)S(1)}, bf16[1024,1536]{1,0:T(8,128)(2,1)}) fusion(f32[1536]{0:T(1024)S(1)} %slice_reduce_fusion, bf16[1024,768]{1,0:T(8,128)(2,1)S(1)} %get-tuple-element.203.two_ref, bf16[768,1536]{1,0:T(8,128)(2,1)S(1)} %get-tuple-element.206), kind=kOutput, calls=%fused_computation.11 | convolution fusion | flops 2434793472 | bytes 10229760 | tf_op jit(solution)/shard_map/dot_general | solution.py:430
  221.9 9.3 %shard_map.277 = (bf16[1024,1152]{1,0:T(8,128)(2,1)S(1)}, bf16[1024,384]{1,0:T(8,128)(2,1)S(1)}, f32[1024,384]{1,0:T(8,128)S(1)}) custom-call(f32[1024,1152]{1,0:T(8,128)S(1)} %convolution_add_fusion.joined_ref, f32[1024,256]{1,0:T(8,128)S(1)} %copy-done.23, s32[1024,1]{1,0:T(8,128)S(1)} %bitcast.213), custom_call_target="tpu_custom_call" | custom-call | flops 20000000000 | bytes 12000000 | tf_op jit(solution)/shard_map/pallas_call | solution.py:387
  231.3 13.1 %shard_map.279.fused_ref = bf16[1024,1152]{1,0:T(8,128)(2,1)S(1)} custom-call(bf16[1024,1152]{1,0:T(8,128)(2,1)S(1)} %get-tuple-element.211.qkv_ref, f32[1024,384]{1,0:T(8,128)S(1)} %get-tuple-element.212.lse_ref, bf16[1024,384]{1,0:T(8,128)(2,1)S(1)} %convolution_convert_fusion.1.dctx_ref, f32[1024,256]{1,0:T(8,128)S(1)} %copy-done.23, s32[1024,1]{1,0:T(8,128)S(1)} %bitcast.214), custom_call_target="tpu_custom_call" | custom-call | flops 30000001024 | bytes 12000000 | tf_op jit(solution)/shard_map/pallas_call | solution.py:405
  251.9 5.4 %fusion.96 = f32[1024,768]{1,0:T(8,128)S(1)} fusion(bf16[1024,1536]{1,0:T(8,128)(2,1)} %get-tuple-element.207.middle_ref, bf16[1536,768]{1,0:T(8,128)(2,1)} %copy-done.60), kind=kOutput, calls=%fused_computation.330 | convolution fusion | flops 2415919104 | bytes 8650752 | tf_op jit(solution)/shard_map/dot_general | solution.py:430
  257.4 5.7 %shard_map.280 = bf16[8,192,1536]{2,1,0:T(8,128)(2,1)S(1)} custom-call(bf16[1024,768]{1,0:T(8,128)(2,1)S(1)} %copy-done.12, bf16[1024,1536]{1,0:T(8,128)(2,1)S(1)} %multiply_convert_fusion.1.d_up_ref, bf16[1024,1536]{1,0:T(8,128)(2,1)S(1)} %copy-done.19, bf16[1024,768]{1,0:T(8,128)(2,1)S(1)} %copy-done.10), custom_call_target="tpu_custom_call" | custom-call | tf_op jit(solution)/shard_map/pallas_call | solution.py:670
  314.2 7.9 %collective-permute-done.54 = bf16[192,1536]{1,0:T(8,128)(2,1)S(1)} collective-permute-done((bf16[192,1536]{1,0:T(8,128)(2,1)S(1)}, bf16[192,1536]{1,0:T(8,128)(2,1)S(1)}, u32[]{:S(2)}, u32[]{:S(2)}) %collective-permute-start.54) | collective-permute-done | bytes 589856 | tf_op jit(solution)/shard_map/ppermute | solution.py:104
  327.5 5.7 %shard_map.282 = bf16[8,192,1536]{2,1,0:T(8,128)(2,1)S(1)} custom-call(bf16[1024,768]{1,0:T(8,128)(2,1)S(1)} %copy-done.9, bf16[1024,1536]{1,0:T(8,128)(2,1)S(1)} %multiply_convert_fusion.d_up_ref, bf16[1024,1536]{1,0:T(8,128)(2,1)S(1)} %copy-done.18, bf16[1024,768]{1,0:T(8,128)(2,1)S(1)} %pad_maximum_fusion.3.grad_ref), custom_call_target="tpu_custom_call" | custom-call | tf_op jit(solution)/shard_map/pallas_call | solution.py:670
  344.5 12.9 %shard_map.283.fused_ref = bf16[1024,1152]{1,0:T(8,128)(2,1)S(1)} custom-call(bf16[1024,1152]{1,0:T(8,128)(2,1)S(1)} %copy-done.67, f32[1024,384]{1,0:T(8,128)S(1)} %copy-done.69, bf16[1024,384]{1,0:T(8,128)(2,1)S(1)} %copy-done.65, f32[1024,256]{1,0:T(8,128)S(1)} %copy-done.24, s32[1024,1]{1,0:T(8,128)S(1)} %bitcast.215), custom_call_target="tpu_custom_call" | custom-call | flops 30000001024 | bytes 12000000 | tf_op jit(solution)/shard_map/pallas_call | solution.py:405
  372.9 7.4 %collective-permute-done.61 = bf16[112,1536]{1,0:T(8,128)(2,1)S(1)} collective-permute-done((bf16[112,1536]{1,0:T(8,128)(2,1)S(1)}, bf16[112,1536]{1,0:T(8,128)(2,1)S(1)}, u32[]{:S(2)}, u32[]{:S(2)}) %collective-permute-start.61) | collective-permute-done | bytes 344096 | tf_op jit(solution)/shard_map/ppermute | solution.py:104
  389.2 12.6 %collective-permute-done.67 = bf16[192,1536]{1,0:T(8,128)(2,1)S(1)} collective-permute-done((bf16[192,1536]{1,0:T(8,128)(2,1)S(1)}, bf16[192,1536]{1,0:T(8,128)(2,1)S(1)}, u32[]{:S(2)}, u32[]{:S(2)}) %collective-permute-start.67) | collective-permute-done | bytes 589856 | tf_op jit(solution)/shard_map/ppermute | solution.py:103
  439.9 9.8 %collective-permute-done.73 = bf16[48,1536]{1,0:T(8,128)(2,1)S(1)} collective-permute-done((bf16[48,1536]{1,0:T(8,128)(2,1)S(1)}, bf16[48,1536]{1,0:T(8,128)(2,1)S(1)}, u32[]{:S(2)}, u32[]{:S(2)}) %collective-permute-start.73) | collective-permute-done | bytes 147488 | tf_op jit(solution)/shard_map/ppermute | solution.py:95
  460.6 8.1 %collective-permute-done.85 = bf16[192,1536]{1,0:T(8,128)(2,1)S(1)} collective-permute-done((bf16[192,1536]{1,0:T(8,128)(2,1)S(1)}, bf16[192,1536]{1,0:T(8,128)(2,1)S(1)}, u32[]{:S(2)}, u32[]{:S(2)}) %collective-permute-start.85) | collective-permute-done | bytes 589856 | tf_op jit(solution)/shard_map/ppermute | solution.py:38
  484.8 5.0 %collective-permute-start.84 = (bf16[56,1536]{1,0:T(8,128)(2,1)S(1)}, bf16[56,1536]{1,0:T(8,128)(2,1)S(1)}, u32[]{:S(2)}, u32[]{:S(2)}) collective-permute-start(bf16[56,1536]{1,0:T(8,128)(2,1)S(1)} %select_convert_fusion.7), channel_id=1, source_target_pairs={{0,1},{1,0},{2,3},{3,2},{4,5},{5,4},{6,7},{7,6},{8,9},{9,8},{10,11... | collective-permute-start | bytes 516104 | tf_op jit(solution)/shard_map/ppermute | solution.py:34
  (646 shorter events, 288.5 us)
Async XLA Ops:
  29.3 18.9 %collective-permute-start.4 = (bf16[512,768]{1,0:T(8,128)(2,1)}, bf16[512,768]{1,0:T(8,128)(2,1)}, u32[]{:S(2)}, u32[]{:S(2)}) collective-permute-start(bf16[512,768]{1,0:T(8,128)(2,1)} %select_bitcast_fusion.2), channel_id=1, source_target_pairs={{0,1},{1,0},{2,3},{3,2},{4,5},{5,4},{6,7},{7,6},{8,9},{9,8},{10,11... | collective-permute-start | bytes 2359304 | tf_op jit(solution)/shard_map/ppermute | solution.py:34
  83.3 19.2 %collective-permute-start.20 = (bf16[192,1536]{1,0:T(8,128)(2,1)S(1)}, bf16[192,1536]{1,0:T(8,128)(2,1)S(1)}, u32[]{:S(2)}, u32[]{:S(2)}) collective-permute-start(bf16[192,1536]{1,0:T(8,128)(2,1)S(1)} %collective-permute-done.15.refs_1_), channel_id=1, source_target_pairs={{0,4},{1,5},{4,8},{5,9},{8,12},{9,13},{12,14},{13,15},{14,10},{15,... | collective-permute-start | bytes 1769480 | tf_op jit(solution)/shard_map/ppermute | solution.py:75
  84.5 18.0 %collective-permute-start.21 = (bf16[192,1536]{1,0:T(8,128)(2,1)S(1)}, bf16[192,1536]{1,0:T(8,128)(2,1)S(1)}, u32[]{:S(2)}, u32[]{:S(2)}) collective-permute-start(bf16[192,1536]{1,0:T(8,128)(2,1)S(1)} %collective-permute-done.16.refs_2_), channel_id=1, source_target_pairs={{0,2},{1,3},{4,0},{5,1},{8,4},{9,5},{12,8},{13,9},{14,12},{15,13},... | collective-permute-start | bytes 1769480 | tf_op jit(solution)/shard_map/ppermute | solution.py:76
  84.8 17.7 %collective-permute-start.18 = (bf16[112,1536]{1,0:T(8,128)(2,1)S(1)}, bf16[112,1536]{1,0:T(8,128)(2,1)S(1)}, u32[]{:S(2)}, u32[]{:S(2)}) collective-permute-start(bf16[112,1536]{1,0:T(8,128)(2,1)S(1)} %collective-permute-done.13.refs_1_), channel_id=1, source_target_pairs={{0,4},{1,5},{4,8},{5,9},{8,12},{9,13},{12,14},{13,15},{14,10},{15,... | collective-permute-start | bytes 1032200 | tf_op jit(solution)/shard_map/ppermute | solution.py:75
  102.5 26.9 %collective-permute-start.24 = (bf16[192,1536]{1,0:T(8,128)(2,1)S(1)}, bf16[192,1536]{1,0:T(8,128)(2,1)S(1)}, u32[]{:S(2)}, u32[]{:S(2)}) collective-permute-start(bf16[192,1536]{1,0:T(8,128)(2,1)S(1)} %collective-permute-done.20.refs_3_), channel_id=1, source_target_pairs={{0,4},{1,5},{4,8},{5,9},{8,12},{9,13},{12,14},{13,15},{14,10},{15,... | collective-permute-start | bytes 1769480 | tf_op jit(solution)/shard_map/ppermute | solution.py:75
  103.7 25.7 %collective-permute-start.25 = (bf16[192,1536]{1,0:T(8,128)(2,1)S(1)}, bf16[192,1536]{1,0:T(8,128)(2,1)S(1)}, u32[]{:S(2)}, u32[]{:S(2)}) collective-permute-start(bf16[192,1536]{1,0:T(8,128)(2,1)S(1)} %collective-permute-done.21.refs_4_), channel_id=1, source_target_pairs={{0,2},{1,3},{4,0},{5,1},{8,4},{9,5},{12,8},{13,9},{14,12},{15,13},... | collective-permute-start | bytes 1769480 | tf_op jit(solution)/shard_map/ppermute | solution.py:76
  104.2 17.5 %collective-permute-start.22 = (bf16[112,1536]{1,0:T(8,128)(2,1)S(1)}, bf16[112,1536]{1,0:T(8,128)(2,1)S(1)}, u32[]{:S(2)}, u32[]{:S(2)}) collective-permute-start(bf16[112,1536]{1,0:T(8,128)(2,1)S(1)} %collective-permute-done.18.refs_3_), channel_id=1, source_target_pairs={{0,4},{1,5},{4,8},{5,9},{8,12},{9,13},{12,14},{13,15},{14,10},{15,... | collective-permute-start | bytes 1032200 | tf_op jit(solution)/shard_map/ppermute | solution.py:75
  105.4 24.1 %collective-permute-start.23 = (bf16[112,1536]{1,0:T(8,128)(2,1)S(1)}, bf16[112,1536]{1,0:T(8,128)(2,1)S(1)}, u32[]{:S(2)}, u32[]{:S(2)}) collective-permute-start(bf16[112,1536]{1,0:T(8,128)(2,1)S(1)} %collective-permute-done.19.refs_4_), channel_id=1, source_target_pairs={{0,2},{1,3},{4,0},{5,1},{8,4},{9,5},{12,8},{13,9},{14,12},{15,13},... | collective-permute-start | bytes 1032200 | tf_op jit(solution)/shard_map/ppermute | solution.py:76
  105.7 26.8 %collective-permute-start.34 = (bf16[384,384]{1,0:T(8,128)(2,1)S(1)}, bf16[384,384]{1,0:T(8,128)(2,1)S(1)}, u32[]{:S(2)}, u32[]{:S(2)}) collective-permute-start(bf16[384,384]{1,0:T(8,128)(2,1)S(1)} %get-tuple-element.188), channel_id=1, source_target_pairs={{0,1},{1,0},{2,3},{3,2},{4,5},{5,4},{6,7},{7,6},{8,9},{9,8},{10,11... | collective-permute-start | bytes 884744 | tf_op jit(solution)/shard_map/ppermute | solution.py:34
  121.6 55.3 %collective-permute-start.44 = (bf16[512,768]{1,0:T(8,128)(2,1)}, bf16[512,768]{1,0:T(8,128)(2,1)}, u32[]{:S(2)}, u32[]{:S(2)}) collective-permute-start(bf16[512,768]{1,0:T(8,128)(2,1)} %get-tuple-element.295), channel_id=1, source_target_pairs={{0,1},{1,0},{2,3},{3,2},{4,5},{5,4},{6,7},{7,6},{8,9},{9,8},{10,11... | collective-permute-start | bytes 2359304 | tf_op jit(solution)/shard_map/ppermute | solution.py:34
  250.3 20.8 %collective-permute-start.45 = (bf16[384,384]{1,0:T(8,128)(2,1)}, bf16[384,384]{1,0:T(8,128)(2,1)}, u32[]{:S(2)}, u32[]{:S(2)}) collective-permute-start(bf16[384,384]{1,0:T(8,128)(2,1)} %broadcast_select_fusion.21), channel_id=1, source_target_pairs={{0,1},{1,0},{2,3},{3,2},{4,5},{5,4},{6,7},{7,6},{8,9},{9,8},{10,11... | collective-permute-start | bytes 884744 | tf_op jit(solution)/shard_map/ppermute | solution.py:34
  267.3 32.2 %collective-permute-start.42 = (bf16[512,768]{1,0:T(8,128)(2,1)}, bf16[512,768]{1,0:T(8,128)(2,1)}, u32[]{:S(2)}, u32[]{:S(2)}) collective-permute-start(bf16[512,768]{1,0:T(8,128)(2,1)} %select_convert_fusion.3), channel_id=1, source_target_pairs={{0,1},{1,0},{2,3},{3,2},{4,5},{5,4},{6,7},{7,6},{8,9},{9,8},{10,11... | collective-permute-start | bytes 2359304 | tf_op jit(solution)/shard_map/ppermute | solution.py:34
  302.2 132.0 %collective-permute-start.43 = (bf16[512,768]{1,0:T(8,128)(2,1)}, bf16[512,768]{1,0:T(8,128)(2,1)}, u32[]{:S(2)}, u32[]{:S(2)}) collective-permute-start(bf16[512,768]{1,0:T(8,128)(2,1)} %get-tuple-element.296), channel_id=1, source_target_pairs={{0,16},{16,0},{1,17},{17,1},{2,18},{18,2},{3,19},{19,3},{4,20},{20... | collective-permute-start | bytes 2359304 | tf_op jit(solution)/shard_map/ppermute | solution.py:38
  305.8 16.3 %collective-permute-start.54 = (bf16[192,1536]{1,0:T(8,128)(2,1)S(1)}, bf16[192,1536]{1,0:T(8,128)(2,1)S(1)}, u32[]{:S(2)}, u32[]{:S(2)}) collective-permute-start(bf16[192,1536]{1,0:T(8,128)(2,1)S(1)} %get-tuple-element.322), channel_id=1, source_target_pairs={{0,2},{1,3},{4,0},{5,1},{8,4},{9,5},{12,8},{13,9},{14,12},{15,13},... | collective-permute-start | bytes 1769480 | tf_op jit(solution)/shard_map/ppermute | solution.py:104
  336.5 24.5 %collective-permute-start.57 = (bf16[112,1536]{1,0:T(8,128)(2,1)}, bf16[112,1536]{1,0:T(8,128)(2,1)}, u32[]{:S(2)}, u32[]{:S(2)}) collective-permute-start(bf16[112,1536]{1,0:T(8,128)(2,1)} %pad_maximum_fusion.21), channel_id=1, source_target_pairs={{0,2},{1,3},{4,0},{5,1},{8,4},{9,5},{12,8},{13,9},{14,12},{15,13},... | collective-permute-start | bytes 1032200 | tf_op jit(solution)/shard_map/ppermute | solution.py:104
  337.5 26.1 %collective-permute-start.56 = (bf16[112,1536]{1,0:T(8,128)(2,1)}, bf16[112,1536]{1,0:T(8,128)(2,1)S(1)}, u32[]{:S(2)}, u32[]{:S(2)}) collective-permute-start(bf16[112,1536]{1,0:T(8,128)(2,1)} %pad_maximum_fusion.20), channel_id=1, source_target_pairs={{0,4},{1,5},{4,8},{5,9},{8,12},{9,13},{12,14},{13,15},{14,10},{15,... | collective-permute-start | bytes 1032200 | tf_op jit(solution)/shard_map/ppermute | solution.py:103
  341.6 22.1 %collective-permute-start.59 = (bf16[192,1536]{1,0:T(8,128)(2,1)}, bf16[192,1536]{1,0:T(8,128)(2,1)}, u32[]{:S(2)}, u32[]{:S(2)}) collective-permute-start(bf16[192,1536]{1,0:T(8,128)(2,1)} %get-tuple-element.320), channel_id=1, source_target_pairs={{0,2},{1,3},{4,0},{5,1},{8,4},{9,5},{12,8},{13,9},{14,12},{15,13},... | collective-permute-start | bytes 1769480 | tf_op jit(solution)/shard_map/ppermute | solution.py:104
  341.9 21.8 %collective-permute-start.58 = (bf16[192,1536]{1,0:T(8,128)(2,1)}, bf16[192,1536]{1,0:T(8,128)(2,1)}, u32[]{:S(2)}, u32[]{:S(2)}) collective-permute-start(bf16[192,1536]{1,0:T(8,128)(2,1)} %get-tuple-element.321), channel_id=1, source_target_pairs={{0,4},{1,5},{4,8},{5,9},{8,12},{9,13},{12,14},{13,15},{14,10},{15,... | collective-permute-start | bytes 1769480 | tf_op jit(solution)/shard_map/ppermute | solution.py:103
  383.3 18.6 %collective-permute-start.67 = (bf16[192,1536]{1,0:T(8,128)(2,1)S(1)}, bf16[192,1536]{1,0:T(8,128)(2,1)S(1)}, u32[]{:S(2)}, u32[]{:S(2)}) collective-permute-start(bf16[192,1536]{1,0:T(8,128)(2,1)S(1)} %pad_maximum_fusion.13), channel_id=1, source_target_pairs={{0,4},{1,5},{4,8},{5,9},{8,12},{9,13},{12,14},{13,15},{14,10},{15,... | collective-permute-start | bytes 1769480 | tf_op jit(solution)/shard_map/ppermute | solution.py:103
  383.9 18.8 %collective-permute-start.68 = (bf16[192,1536]{1,0:T(8,128)(2,1)S(1)}, bf16[192,1536]{1,0:T(8,128)(2,1)S(1)}, u32[]{:S(2)}, u32[]{:S(2)}) collective-permute-start(bf16[192,1536]{1,0:T(8,128)(2,1)S(1)} %pad_maximum_fusion.14), channel_id=1, source_target_pairs={{0,2},{1,3},{4,0},{5,1},{8,4},{9,5},{12,8},{13,9},{14,12},{15,13},... | collective-permute-start | bytes 1769480 | tf_op jit(solution)/shard_map/ppermute | solution.py:104
  432.7 18.0 %collective-permute-start.76 = (bf16[192,1536]{1,0:T(8,128)(2,1)S(1)}, bf16[192,1536]{1,0:T(8,128)(2,1)S(1)}, u32[]{:S(2)}, u32[]{:S(2)}) collective-permute-start(bf16[192,1536]{1,0:T(8,128)(2,1)S(1)} %get-tuple-element.310), channel_id=1, source_target_pairs={{0,2},{1,3},{4,0},{5,1},{8,4},{9,5},{12,8},{13,9},{14,12},{15,13},... | collective-permute-start | bytes 1769480 | tf_op jit(solution)/shard_map/ppermute | solution.py:104
  433.1 17.6 %collective-permute-start.75 = (bf16[192,1536]{1,0:T(8,128)(2,1)S(1)}, bf16[192,1536]{1,0:T(8,128)(2,1)S(1)}, u32[]{:S(2)}, u32[]{:S(2)}) collective-permute-start(bf16[192,1536]{1,0:T(8,128)(2,1)S(1)} %get-tuple-element.311), channel_id=1, source_target_pairs={{0,4},{1,5},{4,8},{5,9},{8,12},{9,13},{12,14},{13,15},{14,10},{15,... | collective-permute-start | bytes 1769480 | tf_op jit(solution)/shard_map/ppermute | solution.py:103
  438.6 17.2 %collective-permute-start.72 = (bf16[512,768]{1,0:T(8,128)(2,1)S(1)}, bf16[512,768]{1,0:T(8,128)(2,1)S(1)}, u32[]{:S(2)}, u32[]{:S(2)}) collective-permute-start(bf16[512,768]{1,0:T(8,128)(2,1)S(1)} %select_convert_fusion), channel_id=1, source_target_pairs={{0,16},{16,0},{1,17},{17,1},{2,18},{18,2},{3,19},{19,3},{4,20},{20... | collective-permute-start | bytes 2359304 | tf_op jit(solution)/shard_map/ppermute | solution.py:38
  472.4 17.4 %collective-permute-start.86 = (bf16[48,1536]{1,0:T(8,128)(2,1)S(1)}, bf16[48,1536]{1,0:T(8,128)(2,1)S(1)}, u32[]{:S(2)}, u32[]{:S(2)}) collective-permute-start(bf16[48,1536]{1,0:T(8,128)(2,1)S(1)} %select_convert_fusion.8), channel_id=1, source_target_pairs={{0,1},{1,0},{2,3},{3,2},{4,5},{5,4},{6,7},{7,6},{8,9},{9,8},{10,11... | collective-permute-start | bytes 442376 | tf_op jit(solution)/shard_map/ppermute | solution.py:34
  (198 other events, 1974.3 us)

commit v5 on v4

--- a/solution.py
+++ b/solution.py
@@ -245,16 +245,21 @@
     return pl.BlockSpec(memory_space=pltpu.SMEM)
 
 
-def whole(shape):
-    return pl.BlockSpec(shape, lambda i: (0,) * len(shape))
-
-
 def vmem():
     return pl.BlockSpec(memory_space=pltpu.VMEM)
 
 
 def pack_kernel(core_ref, wq_ref, wo_ref, wu_ref, wd_ref, *refs):
-    small_refs, (attn_keep, attn_send, mlp_keep, mlp_send, fold_ref, rows_ref) = refs[:-6], refs[-6:]
+    small = len(SMALL)
+    sources = (wq_ref, wo_ref, wu_ref, wd_ref, *refs[:small])
+    attn_keep, attn_send, mlp_keep, mlp_send, fold_ref, rows_ref = refs[small : small + 6]
+    held, sems = refs[small + 6 : -1], refs[-1]
+    copies = [pltpu.make_async_copy(s, h, sems.at[i]) for i, (s, h) in enumerate(zip(sources, held))]
+    for copy in copies:
+        copy.start()
+    for copy in copies:
+        copy.wait()
+    wq_ref, wo_ref, wu_ref, wd_ref, *small_refs = held
     r, chips, f = wq_ref.shape[1], D // wq_ref.shape[1] // 2, wd_ref.shape[1]
     rows_ref[...] = jnp.zeros_like(rows_ref)
     for i, ref in enumerate(small_refs):
@@ -435,20 +440,17 @@
     one = (normed * weights["g1"] + weights["b1"]).astype(BF16)
     two = (normed * weights["g2"] + weights["b2"]).astype(BF16)
     joined = matmul(one, weights["qkv"]) + weights["bqkv"]
-    one, two, joined = track.step((one, two, joined))
     qkv, ctx, lse = track.step(attend(joined, table, begin))
     return source, one, two, qkv, ctx, lse
 
 
-def forward_hidden(saved, weights, track):
+def forward_hidden(saved, weights):
     two, ctx = saved[2], saved[4]
     up = matmul(two, weights["up"]) + weights["bup"]
     phi = 0.5 * (1.0 + lax.erf(up * np.float32(0.5**0.5)))
     middle = (up * phi).astype(BF16)
     slope = (phi + up * jnp.exp(-0.5 * up * up) * np.float32((2 * np.pi) ** -0.5)).astype(BF16)
-    middle, slope = track.step((middle, slope))
     part = matmul(ctx, weights["out"]) + matmul(middle, weights["down"])
-    (part,) = track.step((part,))
     return part, (*saved, middle, slope)
 
 
@@ -461,9 +463,8 @@
     return d_fused, d_one
 
 
-def back_hidden(slope, grad, weights, track):
+def back_hidden(slope, grad, weights):
     d_up = (dot_nt(grad, weights["down"]) * slope.astype(F32)).astype(BF16)
-    (d_up,) = track.step((d_up,))
     return d_up, dot_nt(d_up, weights["up"])
 
 
@@ -523,11 +524,12 @@
             shapes = [(r + 8, LANES)] * 2 + [(r, LANES)] * 2 + [(u, LANES)]
             return pl.pallas_call(
                 pack_kernel,
-                grid=(1,),
-                in_specs=[smem()] + [whole(v.shape) for v in weights_in + vectors],
+                in_specs=[smem()] + [pl.BlockSpec(memory_space=pltpu.HBM)] * len(weights_in + vectors),
                 out_specs=[vmem()] * 5,
                 out_shape=[jax.ShapeDtypeStruct(shape, BF16) for shape in shapes],
-                scratch_shapes=[pltpu.VMEM((8, LANES), F32)],
+                scratch_shapes=[pltpu.VMEM((8, LANES), F32)]
+                + [pltpu.VMEM(v.shape, BF16) for v in weights_in + vectors]
+                + [pltpu.SemaphoreType.DMA((len(weights_in + vectors),))],
                 compiler_params=kernel_params(),
             )(core_scalar, *weights_in, *vectors)
         rows = jnp.concatenate([jnp.pad(v, ((0, 0), (0, LANES - v.shape[1]))) for v in vectors])
@@ -645,9 +647,10 @@
         track.push(0, ("attn", 1), ring.gather(attn_blocks[1]))
         track.push(0, ("mlp", 1), ring.gather(mlp_blocks[1]))
         track.push(1, ("mlp", 0), ring.gather(mlp_blocks[0]))
+        (both,) = track.step((both,))
     saved_0 = forward_attend(both, weights_0, table, begin, track)
     weights_0.update(mlp_weights(0))
-    part, saved_0 = forward_hidden(saved_0, weights_0, track)
+    part, saved_0 = forward_hidden(saved_0, weights_0)
     mid = (own_tokens.astype(F32) + summed(part) + weights_0["bout"]).astype(BF16)
     (mid,) = track.step((mid,))
     both = paired(mid)
@@ -729,31 +732,27 @@
     saved_1 = forward_attend(both, weights_1, table, begin, track)
     d_fused, d_one = back_attend(saved_1, grad, weights_1, table, begin, track)
     out_rows = out_rows_of(saved_1[4], grad)
-    (d_one, out_rows) = track.step((d_one, out_rows))
     weights_1.update(mlp_weights(1))
-    part, (source, one, two, _, _, _, middle, slope) = forward_hidden(saved_1, weights_1, track)
+    part, (source, one, two, _, _, _, middle, slope) = forward_hidden(saved_1, weights_1)
     last = (mid.astype(F32) + summed(part) + weights_1["bout"]).astype(BF16)
     kept_rows, got = pick(low_section, mid, last), swap_section(pick(low_section, last, mid))
     outputs = jnp.stack([pick(low_section, kept_rows, got), pick(low_section, got, kept_rows)])
-    d_up, d_two = back_hidden(slope, grad, weights_1, track)
+    d_up, d_two = back_hidden(slope, grad, weights_1)
     send_mlp(1, two, d_up, middle, grad)
-    (d_two,) = track.step((d_two,))
     part, sums = back_norms(source, d_one, d_two, weights_1)
     small = (*sums, sums_of(d_fused), None, sums_of(d_up))
+    send_attn(1, one, d_fused, out_rows, small, sums_of(cot_low))
     (part,) = track.step((part,))
-    send_attn(1, one, d_fused, out_rows, small, sums_of(cot_low))
     grad_1 = own_cot + summed(part)
     low_1 = grad_1.astype(BF16)
-    (low_1, grad_1) = track.step((low_1, grad_1))
 
     source, one, two, _, ctx, _, middle, slope = saved_0
     grad = paired(low_1)
-    d_up, d_two = back_hidden(slope, grad, weights_0, track)
+    d_up, d_two = back_hidden(slope, grad, weights_0)
     send_mlp(0, two, d_up, middle, grad)
     (d_two,) = track.step((d_two,))
     out_rows = out_rows_of(ctx, grad)
     d_fused, d_one = back_attend(saved_0, grad, weights_0, table, begin, track)
-    (d_one,) = track.step((d_one,))
     part, sums = back_norms(source, d_one, d_two, weights_0)
     small = (*sums, sums_of(d_fused), None, sums_of(d_up))
     send_attn(0, one, d_fused, out_rows, small, sums_of(low_1))

time: 505 us -> 530 us (1.050)
  local copies, waits for them, and re-layouts: 42.3 us -> 65.2 us
  waiting for transfers between devices: 150 us -> 169 us
  other arithmetic: 80.9 us -> 67.9 us
  starting transfers between devices: 99.5 us -> 93.3 us
    ppermute x16, waiting for transfers between devices: 27.8 us -> 54.6 us  [scatter(): ahead = lax.ppermute(ahead, 'dp', self.right)]
    ppermute x4, waiting for transfers between devices: 11.1 us -> 29.4 us  [gather(): ahead = lax.ppermute(ahead[:cut], 'dp', self.right)]
    ppermute x16, waiting for transfers between devices: 26.8 us -> 11.4 us  [scatter(): back = lax.ppermute(back, 'dp', self.left)]
    unnamed x290 -> x314, local copies, waits for them, and re-layouts: 34.7 us -> 46.2 us
    dot_general x8, matrix products: 21.8 us -> 30.4 us  [dot_nt(): lax.dot_general(a, b, (((1,), (1,)), ((), ())), preferred_element_type=F32)]
    ppermute x12, waiting for transfers between devices: 14.9 us -> 6.86 us  [gather(): back = lax.ppermute(back, 'dp', self.left)]
    dot_general x8, matrix products: 28.1 us -> 22.2 us  [matmul(): return jnp.dot(a, b, preferred_element_type=F32)]
    ppermute x12, waiting for transfers between devices: 41.5 us -> 36 us  [gather(): ahead = lax.ppermute(ahead, 'dp', self.right)]
  transfers between devices with their start and end apart: 87 -> 87, of which waited for: 41 -> 32; matrix products, arithmetic and copies ran while one was open for 24% -> 19% of each run, Pallas kernels for 8% -> 11%
where the time goes in v5:
time: 530 us; the launch traced here: 520 us
  waiting for transfers between devices  169 us (32%)
  starting transfers between devices  93.3 us (18%)
  other arithmetic  67.9 us (13%)
  Pallas kernels  66.2 us (12%)
  local copies, waits for them, and re-layouts  65.2 us (12%)
  matrix products  55.1 us (10%)
    ppermute x16, waiting for transfers between devices, scatter(): ahead = lax.ppermute(ahead, 'dp', self.right)  54.6 us
    unnamed x314, local copies, waits for them, and re-layouts  46.2 us
    ppermute x17, starting transfers between devices, swap_core(): return lax.ppermute(block, 'dp', [(i, i ^ 1) for i in range(n)])  38.2 us
    ppermute x12, waiting for transfers between devices, gather(): ahead = lax.ppermute(ahead, 'dp', self.right)  36 us
    dot_general x8, matrix products, dot_nt(): lax.dot_general(a, b, (((1,), (1,)), ((), ())), preferred_element_type=F32)  30.4 us
    ppermute x4, waiting for transfers between devices, gather(): ahead = lax.ppermute(ahead[:cut], 'dp', self.right)  29.4 us
    ppermute x6, waiting for transfers between devices, swap_section(): return lax.ppermute(block, 'section', [(0, 1), (1, 0)])  25.7 us
    pallas_call x2, Pallas kernels, attend_back(): pl.pallas_call(attend_back_kernel, grid=(2, PAIRS), in_specs=[per_pair(le...  25.3 us
  transfers between devices with their start and end apart: 87, of which 32 were waited for; matrix products, arithmetic and copies ran while one was open for 19% of the time, Pallas kernels for 11%

profile of v5, /device:TPU:1, one launch (start us, length us, event | category | flops | bytes accessed | tf_op | source)
XLA Modules:
  0.0 519.6 jit_solution(11184634394830550698)
XLA Ops:
  17.0 8.0 %collective-permute-done.3 = bf16[112,1536]{1,0:T(8,128)(2,1)S(1)} collective-permute-done((bf16[112,1536]{1,0:T(8,128)(2,1)S(1)}, bf16[112,1536]{1,0:T(8,128)(2,1)S(1)}, u32[]{:S(2)}, u32[]{:S(2)}) %collective-permute-start.3) | collective-permute-done | bytes 344096 | tf_op jit(solution)/shard_map/ppermute | solution.py:38
  57.1 20.5 %collective-permute-done.15.refs_7_ = bf16[48,1536]{1,0:T(8,128)(2,1)S(1)} collective-permute-done((bf16[48,1536]{1,0:T(8,128)(2,1)S(1)}, bf16[48,1536]{1,0:T(8,128)(2,1)S(1)}, u32[]{:S(2)}, u32[]{:S(2)}) %collective-permute-start.15) | collective-permute-done | bytes 147488 | tf_op jit(solution)/shard_map/ppermute | solution.py:80
  83.5 9.3 %shard_map.274 = (bf16[1024,1152]{1,0:T(8,128)(2,1)S(1)}, bf16[1024,384]{1,0:T(8,128)(2,1)S(1)}, f32[1024,384]{1,0:T(8,128)S(1)}) custom-call(f32[1024,1152]{1,0:T(8,128)S(1)} %convolution_add_fusion.1.joined_ref, f32[1024,256]{1,0:T(8,128)S(1)} %pad_maximum_fusion.4.table_ref, s32[1024,1]{1,0:T(8,128)S(1)} %bitcast.214), custom_call_target="tpu_custom_call" | custom-call | flops 20000000000 | bytes 12000000 | tf_op jit(solution)/shard_map/pallas_call | solution.py:392
  98.5 15.5 %collective-permute-done.18.refs_3_ = bf16[112,1536]{1,0:T(8,128)(2,1)S(1)} collective-permute-done((bf16[112,1536]{1,0:T(8,128)(2,1)S(1)}, bf16[112,1536]{1,0:T(8,128)(2,1)S(1)}, u32[]{:S(2)}, u32[]{:S(2)}) %collective-permute-start.18) | collective-permute-done | bytes 344096 | tf_op jit(solution)/shard_map/ppermute | solution.py:75
  117.4 6.6 %collective-permute-start.32 = (bf16[384,384]{1,0:T(8,128)(2,1)S(1)}, bf16[384,384]{1,0:T(8,128)(2,1)S(1)}, u32[]{:S(2)}, u32[]{:S(2)}) collective-permute-start(bf16[384,384]{1,0:T(8,128)(2,1)S(1)} %get-tuple-element.169), channel_id=1, source_target_pairs={{0,1},{1,0},{2,3},{3,2},{4,5},{5,4},{6,7},{7,6},{8,9},{9,8},{10,11... | collective-permute-start | bytes 884744 | tf_op jit(solution)/shard_map/ppermute | solution.py:34
  127.0 6.4 %collective-permute-done.22.refs_5_ = bf16[112,1536]{1,0:T(8,128)(2,1)S(1)} collective-permute-done((bf16[112,1536]{1,0:T(8,128)(2,1)S(1)}, bf16[112,1536]{1,0:T(8,128)(2,1)S(1)}, u32[]{:S(2)}, u32[]{:S(2)}) %collective-permute-start.22) | collective-permute-done | bytes 344096 | tf_op jit(solution)/shard_map/ppermute | solution.py:75
  142.1 8.0 %collective-permute-done.26.refs_7_ = bf16[48,1536]{1,0:T(8,128)(2,1)S(1)} collective-permute-done((bf16[48,1536]{1,0:T(8,128)(2,1)S(1)}, bf16[48,1536]{1,0:T(8,128)(2,1)S(1)}, u32[]{:S(2)}, u32[]{:S(2)}) %collective-permute-start.26) | collective-permute-done | bytes 147488 | tf_op jit(solution)/shard_map/ppermute | solution.py:80
  151.4 5.4 %multiply_convert_fusion.3 = (bf16[1024,1536]{1,0:T(8,128)(2,1)S(1)}, f32[1024,1536]{1,0:T(8,128)}) fusion(f32[1536]{0:T(1024)S(1)} %slice_reduce_fusion.1, bf16[1024,768]{1,0:T(8,128)(2,1)S(1)} %get-tuple-element.324.two_ref, bf16[768,1536]{1,0:T(8,128)(2,1)S(1)} %get-tuple-element.172), kind=kOutput, calls=%fused_computation.18 | convolution fusion | flops 2425356288 | bytes 13375488 | tf_op jit(solution)/shard_map/dot_general | solution.py:435
  171.9 9.3 %collective-permute-done.30.refs_1_ = bf16[192,1536]{1,0:T(8,128)(2,1)S(1)} collective-permute-done((bf16[192,1536]{1,0:T(8,128)(2,1)S(1)}, bf16[192,1536]{1,0:T(8,128)(2,1)S(1)}, u32[]{:S(2)}, u32[]{:S(2)}) %collective-permute-start.30) | collective-permute-done | bytes 589856 | tf_op jit(solution)/shard_map/ppermute | solution.py:75
  197.3 9.3 %shard_map.277 = (bf16[1024,1152]{1,0:T(8,128)(2,1)S(1)}, bf16[1024,384]{1,0:T(8,128)(2,1)S(1)}, f32[1024,384]{1,0:T(8,128)S(1)}) custom-call(f32[1024,1152]{1,0:T(8,128)S(1)} %convolution_add_fusion.joined_ref, f32[1024,256]{1,0:T(8,128)S(1)} %pad_maximum_fusion.4.table_ref, s32[1024,1]{1,0:T(8,128)S(1)} %bitcast.215), custom_call_target="tpu_custom_call" | custom-call | flops 20000000000 | bytes 12000000 | tf_op jit(solution)/shard_map/pallas_call | solution.py:392
  210.6 12.7 %shard_map.278.fused_ref = bf16[1024,1152]{1,0:T(8,128)(2,1)S(1)} custom-call(bf16[1024,1152]{1,0:T(8,128)(2,1)S(1)} %get-tuple-element.187.qkv_ref, f32[1024,384]{1,0:T(8,128)S(1)} %get-tuple-element.188.lse_ref, bf16[1024,384]{1,0:T(8,128)(2,1)S(1)} %convolution_convert_fusion.1.dctx_ref, f32[1024,256]{1,0:T(8,128)S(1)} %copy-done.27, s32[1024,1]{1,0:T(8,128)S(1)} %bitcast.216), custom_call_target="tpu_custom_call" | custom-call | flops 30000001024 | bytes 12000000 | tf_op jit(solution)/shard_map/pallas_call | solution.py:410
  256.3 5.9 %fusion.87 = (f32[1024]{0:T(1024)S(1)}, f32[1024]{0:T(1024)S(1)}, f32[1024,768]{1,0:T(8,128)}, f32[768]{0:T(1024)S(1)}, f32[768]{0:T(1024)S(1)}, /*index=5*/f32[768]{0:T(1024)S(1)}, f32[768]{0:T(1024)S(1)}) fusion(f32[1024]{0:T(1024)S(1)} %copy-done.131, f32[1024]{0:T(1024)S(1)} %copy-done.125, bf16[512,768]{1,0:T(8,128)(2,1)S(1)} %copy-done.90, ...), kind=kOutput, calls=%fused_computation.321 | convolution fusion | flops 1826089984 | bytes 12027904 | tf_op jit(solution)/shard_map/dot_general | solution.py:177
  269.2 5.7 %shard_map.281 = bf16[8,192,1536]{2,1,0:T(8,128)(2,1)S(1)} custom-call(bf16[1024,768]{1,0:T(8,128)(2,1)S(1)} %copy-done.11, bf16[1024,1536]{1,0:T(8,128)(2,1)S(1)} %copy-done.21, bf16[1024,1536]{1,0:T(8,128)(2,1)S(1)} %copy-done.18, bf16[1024,768]{1,0:T(8,128)(2,1)S(1)} %copy-done.9), custom_call_target="tpu_custom_call" | custom-call | tf_op jit(solution)/shard_map/pallas_call | solution.py:673
  299.9 6.8 %convert_reduce_fusion = (f32[1536]{0:T(1024)S(1)}, bf16[1024,1536]{1,0:T(8,128)(2,1)S(1)}) fusion(f32[1024,1536]{1,0:T(8,128)} %get-tuple-element.380, f32[1536]{0:T(1024)S(1)} %copy-done.138, bf16[1536,768]{1,0:T(8,128)(2,1)S(1)} %copy-done.69, bf16[512,768]{1,0:T(8,128)(2,1)S(1)} %get-tuple-element.327, bf16[512,768]{1,0:T(8,128)(2,1)S(1)} %get-tuple-element.326), kind=kOutput, calls=%fused_computation.12 | convolution fusion | flops 2442656256 | bytes 13381632 | tf_op jit(solution)/shard_map/dot_general | solution.py:177
  313.6 5.7 %shard_map.284 = bf16[8,192,1536]{2,1,0:T(8,128)(2,1)S(1)} custom-call(bf16[1024,768]{1,0:T(8,128)(2,1)S(1)} %copy-done.8, bf16[1024,1536]{1,0:T(8,128)(2,1)S(1)} %get-tuple-element.386.d_up_ref, bf16[1024,1536]{1,0:T(8,128)(2,1)S(1)} %copy-done.17, bf16[1024,768]{1,0:T(8,128)(2,1)S(1)} %pad_maximum_fusion.3.grad_ref), custom_call_target="tpu_custom_call" | custom-call | tf_op jit(solution)/shard_map/pallas_call | solution.py:673
  341.1 12.7 %shard_map.282.fused_ref = bf16[1024,1152]{1,0:T(8,128)(2,1)S(1)} custom-call(bf16[1024,1152]{1,0:T(8,128)(2,1)S(1)} %copy-done.78, f32[1024,384]{1,0:T(8,128)S(1)} %copy-done.80, bf16[1024,384]{1,0:T(8,128)(2,1)S(1)} %copy-done.76, f32[1024,256]{1,0:T(8,128)S(1)} %copy-done.28, s32[1024,1]{1,0:T(8,128)S(1)} %bitcast.217), custom_call_target="tpu_custom_call" | custom-call | flops 30000001024 | bytes 12000000 | tf_op jit(solution)/shard_map/pallas_call | solution.py:410
  385.3 7.0 %collective-permute-done.56 = bf16[112,1536]{1,0:T(8,128)(2,1)} collective-permute-done((bf16[112,1536]{1,0:T(8,128)(2,1)}, bf16[112,1536]{1,0:T(8,128)(2,1)}, u32[]{:S(2)}, u32[]{:S(2)}) %collective-permute-start.56) | collective-permute-done | bytes 344096 | tf_op jit(solution)/shard_map/ppermute | solution.py:103
  399.0 16.3 %collective-permute-done.63 = bf16[112,1536]{1,0:T(8,128)(2,1)S(1)} collective-permute-done((bf16[112,1536]{1,0:T(8,128)(2,1)S(1)}, bf16[112,1536]{1,0:T(8,128)(2,1)S(1)}, u32[]{:S(2)}, u32[]{:S(2)}) %collective-permute-start.63) | collective-permute-done | bytes 344096 | tf_op jit(solution)/shard_map/ppermute | solution.py:103
  431.0 5.6 %collective-permute-start.43 = (bf16[512,768]{1,0:T(8,128)(2,1)S(1)}, bf16[512,768]{1,0:T(8,128)(2,1)S(1)}, u32[]{:S(2)}, u32[]{:S(2)}) collective-permute-start(bf16[512,768]{1,0:T(8,128)(2,1)S(1)} %select_convert_fusion.3), channel_id=1, source_target_pairs={{0,1},{1,0},{2,3},{3,2},{4,5},{5,4},{6,7},{7,6},{8,9},{9,8},{10,11... | collective-permute-start | bytes 2359304 | tf_op jit(solution)/shard_map/ppermute | solution.py:34
  436.6 8.7 %collective-permute-done.72 = bf16[112,1536]{1,0:T(8,128)(2,1)S(1)} collective-permute-done((bf16[112,1536]{1,0:T(8,128)(2,1)S(1)}, bf16[112,1536]{1,0:T(8,128)(2,1)S(1)}, u32[]{:S(2)}, u32[]{:S(2)}) %collective-permute-start.72) | collective-permute-done | bytes 344096 | tf_op jit(solution)/shard_map/ppermute | solution.py:104
  450.5 14.0 %collective-permute-done.75 = bf16[112,1536]{1,0:T(8,128)(2,1)S(1)} collective-permute-done((bf16[112,1536]{1,0:T(8,128)(2,1)S(1)}, bf16[112,1536]{1,0:T(8,128)(2,1)S(1)}, u32[]{:S(2)}, u32[]{:S(2)}) %collective-permute-start.75) | collective-permute-done | bytes 344096 | tf_op jit(solution)/shard_map/ppermute | solution.py:103
  469.7 14.2 %collective-permute-done.79 = bf16[112,1536]{1,0:T(8,128)(2,1)S(1)} collective-permute-done((bf16[112,1536]{1,0:T(8,128)(2,1)S(1)}, bf16[112,1536]{1,0:T(8,128)(2,1)S(1)}, u32[]{:S(2)}, u32[]{:S(2)}) %collective-permute-start.79) | collective-permute-done | bytes 344096 | tf_op jit(solution)/shard_map/ppermute | solution.py:103
  490.8 8.1 %collective-permute-start.84 = (bf16[56,1536]{1,0:T(8,128)(2,1)S(1)}, bf16[56,1536]{1,0:T(8,128)(2,1)S(1)}, u32[]{:S(2)}, u32[]{:S(2)}) collective-permute-start(bf16[56,1536]{1,0:T(8,128)(2,1)S(1)} %select_convert_fusion.7), channel_id=1, source_target_pairs={{0,1},{1,0},{2,3},{3,2},{4,5},{5,4},{6,7},{7,6},{8,9},{9,8},{10,11... | collective-permute-start | bytes 516104 | tf_op jit(solution)/shard_map/ppermute | solution.py:34
  502.6 11.7 %collective-permute-done.85 = bf16[192,1536]{1,0:T(8,128)(2,1)S(1)} collective-permute-done((bf16[192,1536]{1,0:T(8,128)(2,1)S(1)}, bf16[192,1536]{1,0:T(8,128)(2,1)S(1)}, u32[]{:S(2)}, u32[]{:S(2)}) %collective-permute-start.85) | collective-permute-done | bytes 589856 | tf_op jit(solution)/shard_map/ppermute | solution.py:38
  (669 shorter events, 282.7 us)
Async XLA Ops:
  50.5 45.0 %collective-permute-start.7 = (bf16[192,1536]{1,0:T(8,128)(2,1)S(1)}, bf16[192,1536]{1,0:T(8,128)(2,1)S(1)}, u32[]{:S(2)}, u32[]{:S(2)}) collective-permute-start(bf16[192,1536]{1,0:T(8,128)(2,1)S(1)} %get-tuple-element.135.refs_0_), channel_id=1, source_target_pairs={{0,4},{1,5},{4,8},{5,9},{8,12},{9,13},{12,14},{13,15},{14,10},{15,... | collective-permute-start | bytes 1769480 | tf_op jit(solution)/shard_map/ppermute | solution.py:75
  51.8 43.7 %collective-permute-start.8 = (bf16[192,1536]{1,0:T(8,128)(2,1)S(1)}, bf16[192,1536]{1,0:T(8,128)(2,1)S(1)}, u32[]{:S(2)}, u32[]{:S(2)}) collective-permute-start(bf16[192,1536]{1,0:T(8,128)(2,1)S(1)} %get-tuple-element.135.refs_0_), channel_id=1, source_target_pairs={{0,2},{1,3},{4,0},{5,1},{8,4},{9,5},{12,8},{13,9},{14,12},{15,13},... | collective-permute-start | bytes 1769480 | tf_op jit(solution)/shard_map/ppermute | solution.py:76
  52.3 43.2 %collective-permute-start.5 = (bf16[112,1536]{1,0:T(8,128)(2,1)S(1)}, bf16[112,1536]{1,0:T(8,128)(2,1)S(1)}, u32[]{:S(2)}, u32[]{:S(2)}) collective-permute-start(bf16[112,1536]{1,0:T(8,128)(2,1)S(1)} %get-tuple-element.134.refs_0_), channel_id=1, source_target_pairs={{0,4},{1,5},{4,8},{5,9},{8,12},{9,13},{12,14},{13,15},{14,10},{15,... | collective-permute-start | bytes 1032200 | tf_op jit(solution)/shard_map/ppermute | solution.py:75
  55.5 23.2 %collective-permute-start.16 = (bf16[64,1536]{1,0:T(8,128)(2,1)S(1)}, bf16[64,1536]{1,0:T(8,128)(2,1)S(1)}, u32[]{:S(2)}, u32[]{:S(2)}) collective-permute-start(bf16[64,1536]{1,0:T(8,128)(2,1)S(1)} %slice.396), channel_id=1, source_target_pairs={{0,2},{1,3},{4,0},{5,1},{8,4},{9,5},{12,8},{13,9},{14,12},{15,13},... | collective-permute-start | bytes 589832 | tf_op jit(solution)/shard_map/ppermute | solution.py:81
  55.8 21.9 %collective-permute-start.15 = (bf16[48,1536]{1,0:T(8,128)(2,1)S(1)}, bf16[48,1536]{1,0:T(8,128)(2,1)S(1)}, u32[]{:S(2)}, u32[]{:S(2)}) collective-permute-start(bf16[48,1536]{1,0:T(8,128)(2,1)S(1)} %slice.395), channel_id=1, source_target_pairs={{0,4},{1,5},{4,8},{5,9},{8,12},{9,13},{12,14},{13,15},{14,10},{15,... | collective-permute-start | bytes 442376 | tf_op jit(solution)/shard_map/ppermute | solution.py:80
  114.3 24.5 %collective-permute-start.24 = (bf16[192,1536]{1,0:T(8,128)(2,1)S(1)}, bf16[192,1536]{1,0:T(8,128)(2,1)S(1)}, u32[]{:S(2)}, u32[]{:S(2)}) collective-permute-start(bf16[192,1536]{1,0:T(8,128)(2,1)S(1)} %collective-permute-done.20.refs_3_), channel_id=1, source_target_pairs={{0,4},{1,5},{4,8},{5,9},{8,12},{9,13},{12,14},{13,15},{14,10},{15,... | collective-permute-start | bytes 1769480 | tf_op jit(solution)/shard_map/ppermute | solution.py:75
  115.8 22.9 %collective-permute-start.25 = (bf16[192,1536]{1,0:T(8,128)(2,1)S(1)}, bf16[192,1536]{1,0:T(8,128)(2,1)S(1)}, u32[]{:S(2)}, u32[]{:S(2)}) collective-permute-start(bf16[192,1536]{1,0:T(8,128)(2,1)S(1)} %collective-permute-done.21.refs_4_), channel_id=1, source_target_pairs={{0,2},{1,3},{4,0},{5,1},{8,4},{9,5},{12,8},{13,9},{14,12},{15,13},... | collective-permute-start | bytes 1769480 | tf_op jit(solution)/shard_map/ppermute | solution.py:76
  117.3 21.5 %collective-permute-start.23 = (bf16[112,1536]{1,0:T(8,128)(2,1)S(1)}, bf16[112,1536]{1,0:T(8,128)(2,1)S(1)}, u32[]{:S(2)}, u32[]{:S(2)}) collective-permute-start(bf16[112,1536]{1,0:T(8,128)(2,1)S(1)} %collective-permute-done.19.refs_4_), channel_id=1, source_target_pairs={{0,2},{1,3},{4,0},{5,1},{8,4},{9,5},{12,8},{13,9},{14,12},{15,13},... | collective-permute-start | bytes 1032200 | tf_op jit(solution)/shard_map/ppermute | solution.py:76
  117.4 24.3 %collective-permute-start.32 = (bf16[384,384]{1,0:T(8,128)(2,1)S(1)}, bf16[384,384]{1,0:T(8,128)(2,1)S(1)}, u32[]{:S(2)}, u32[]{:S(2)}) collective-permute-start(bf16[384,384]{1,0:T(8,128)(2,1)S(1)} %get-tuple-element.169), channel_id=1, source_target_pairs={{0,1},{1,0},{2,3},{3,2},{4,5},{5,4},{6,7},{7,6},{8,9},{9,8},{10,11... | collective-permute-start | bytes 884744 | tf_op jit(solution)/shard_map/ppermute | solution.py:34
  133.4 34.4 %collective-permute-start.40 = (bf16[512,768]{1,0:T(8,128)(2,1)}, bf16[512,768]{1,0:T(8,128)(2,1)}, u32[]{:S(2)}, u32[]{:S(2)}) collective-permute-start(bf16[512,768]{1,0:T(8,128)(2,1)} %get-tuple-element.270), channel_id=1, source_target_pairs={{0,1},{1,0},{2,3},{3,2},{4,5},{5,4},{6,7},{7,6},{8,9},{9,8},{10,11... | collective-permute-start | bytes 2359304 | tf_op jit(solution)/shard_map/ppermute | solution.py:34
  295.0 26.7 %collective-permute-start.48 = (bf16[96,1536]{1,0:T(8,128)(2,1)}, bf16[96,1536]{1,0:T(8,128)(2,1)S(1)}, u32[]{:S(2)}, u32[]{:S(2)}) collective-permute-start(bf16[96,1536]{1,0:T(8,128)(2,1)} %get-tuple-element.198), channel_id=1, source_target_pairs={{0,4},{1,5},{4,8},{5,9},{8,12},{9,13},{12,14},{13,15},{14,10},{15,... | collective-permute-start | bytes 884744 | tf_op jit(solution)/shard_map/ppermute | solution.py:95
  296.1 25.5 %collective-permute-start.49 = (bf16[96,1536]{1,0:T(8,128)(2,1)}, bf16[96,1536]{1,0:T(8,128)(2,1)S(1)}, u32[]{:S(2)}, u32[]{:S(2)}) collective-permute-start(bf16[96,1536]{1,0:T(8,128)(2,1)} %get-tuple-element.199), channel_id=1, source_target_pairs={{0,2},{1,3},{4,0},{5,1},{8,4},{9,5},{12,8},{13,9},{14,12},{15,13},... | collective-permute-start | bytes 884744 | tf_op jit(solution)/shard_map/ppermute | solution.py:96
  296.5 25.2 %collective-permute-start.47 = (bf16[64,1536]{1,0:T(8,128)(2,1)}, bf16[64,1536]{1,0:T(8,128)(2,1)}, u32[]{:S(2)}, u32[]{:S(2)}) collective-permute-start(bf16[64,1536]{1,0:T(8,128)(2,1)} %get-tuple-element.197), channel_id=1, source_target_pairs={{0,2},{1,3},{4,0},{5,1},{8,4},{9,5},{12,8},{13,9},{14,12},{15,13},... | collective-permute-start | bytes 589832 | tf_op jit(solution)/shard_map/ppermute | solution.py:96
  296.6 25.0 %collective-permute-start.46 = (bf16[48,1536]{1,0:T(8,128)(2,1)}, bf16[48,1536]{1,0:T(8,128)(2,1)}, u32[]{:S(2)}, u32[]{:S(2)}) collective-permute-start(bf16[48,1536]{1,0:T(8,128)(2,1)} %get-tuple-element.196), channel_id=1, source_target_pairs={{0,4},{1,5},{4,8},{5,9},{8,12},{9,13},{12,14},{13,15},{14,10},{15,... | collective-permute-start | bytes 442376 | tf_op jit(solution)/shard_map/ppermute | solution.py:95
  323.8 36.1 %collective-permute-start.55 = (bf16[192,1536]{1,0:T(8,128)(2,1)}, bf16[192,1536]{1,0:T(8,128)(2,1)}, u32[]{:S(2)}, u32[]{:S(2)}) collective-permute-start(bf16[192,1536]{1,0:T(8,128)(2,1)} %pad_maximum_fusion.11), channel_id=1, source_target_pairs={{0,2},{1,3},{4,0},{5,1},{8,4},{9,5},{12,8},{13,9},{14,12},{15,13},... | collective-permute-start | bytes 1769480 | tf_op jit(solution)/shard_map/ppermute | solution.py:104
  324.9 35.1 %collective-permute-start.54 = (bf16[192,1536]{1,0:T(8,128)(2,1)}, bf16[192,1536]{1,0:T(8,128)(2,1)}, u32[]{:S(2)}, u32[]{:S(2)}) collective-permute-start(bf16[192,1536]{1,0:T(8,128)(2,1)} %pad_maximum_fusion.10), channel_id=1, source_target_pairs={{0,4},{1,5},{4,8},{5,9},{8,12},{9,13},{12,14},{13,15},{14,10},{15,... | collective-permute-start | bytes 1769480 | tf_op jit(solution)/shard_map/ppermute | solution.py:103
  327.9 32.0 %collective-permute-start.53 = (bf16[112,1536]{1,0:T(8,128)(2,1)}, bf16[112,1536]{1,0:T(8,128)(2,1)}, u32[]{:S(2)}, u32[]{:S(2)}) collective-permute-start(bf16[112,1536]{1,0:T(8,128)(2,1)} %pad_maximum_fusion.21), channel_id=1, source_target_pairs={{0,2},{1,3},{4,0},{5,1},{8,4},{9,5},{12,8},{13,9},{14,12},{15,13},... | collective-permute-start | bytes 1032200 | tf_op jit(solution)/shard_map/ppermute | solution.py:104
  329.8 30.1 %collective-permute-start.52 = (bf16[112,1536]{1,0:T(8,128)(2,1)}, bf16[112,1536]{1,0:T(8,128)(2,1)}, u32[]{:S(2)}, u32[]{:S(2)}) collective-permute-start(bf16[112,1536]{1,0:T(8,128)(2,1)} %pad_maximum_fusion.20), channel_id=1, source_target_pairs={{0,4},{1,5},{4,8},{5,9},{8,12},{9,13},{12,14},{13,15},{14,10},{15,... | collective-permute-start | bytes 1032200 | tf_op jit(solution)/shard_map/ppermute | solution.py:103
  333.3 24.5 %collective-permute-start.62 = (bf16[384,384]{1,0:T(8,128)(2,1)}, bf16[384,384]{1,0:T(8,128)(2,1)}, u32[]{:S(2)}, u32[]{:S(2)}) collective-permute-start(bf16[384,384]{1,0:T(8,128)(2,1)} %broadcast_select_fusion.17), channel_id=1, source_target_pairs={{0,1},{1,0},{2,3},{3,2},{4,5},{5,4},{6,7},{7,6},{8,9},{9,8},{10,11... | collective-permute-start | bytes 884744 | tf_op jit(solution)/shard_map/ppermute | solution.py:34
  370.1 23.0 %collective-permute-start.58 = (bf16[192,1536]{1,0:T(8,128)(2,1)}, bf16[192,1536]{1,0:T(8,128)(2,1)}, u32[]{:S(2)}, u32[]{:S(2)}) collective-permute-start(bf16[192,1536]{1,0:T(8,128)(2,1)} %get-tuple-element.295), channel_id=1, source_target_pairs={{0,4},{1,5},{4,8},{5,9},{8,12},{9,13},{12,14},{13,15},{14,10},{15,... | collective-permute-start | bytes 1769480 | tf_op jit(solution)/shard_map/ppermute | solution.py:103
  371.3 21.9 %collective-permute-start.59 = (bf16[192,1536]{1,0:T(8,128)(2,1)}, bf16[192,1536]{1,0:T(8,128)(2,1)}, u32[]{:S(2)}, u32[]{:S(2)}) collective-permute-start(bf16[192,1536]{1,0:T(8,128)(2,1)} %get-tuple-element.294), channel_id=1, source_target_pairs={{0,2},{1,3},{4,0},{5,1},{8,4},{9,5},{12,8},{13,9},{14,12},{15,13},... | collective-permute-start | bytes 1769480 | tf_op jit(solution)/shard_map/ppermute | solution.py:104
  394.7 21.4 %collective-permute-start.65 = (bf16[192,1536]{1,0:T(8,128)(2,1)S(1)}, bf16[192,1536]{1,0:T(8,128)(2,1)S(1)}, u32[]{:S(2)}, u32[]{:S(2)}) collective-permute-start(bf16[192,1536]{1,0:T(8,128)(2,1)S(1)} %get-tuple-element.293), channel_id=1, source_target_pairs={{0,4},{1,5},{4,8},{5,9},{8,12},{9,13},{12,14},{13,15},{14,10},{15,... | collective-permute-start | bytes 1769480 | tf_op jit(solution)/shard_map/ppermute | solution.py:103
  395.7 20.3 %collective-permute-start.66 = (bf16[192,1536]{1,0:T(8,128)(2,1)S(1)}, bf16[192,1536]{1,0:T(8,128)(2,1)S(1)}, u32[]{:S(2)}, u32[]{:S(2)}) collective-permute-start(bf16[192,1536]{1,0:T(8,128)(2,1)S(1)} %get-tuple-element.292), channel_id=1, source_target_pairs={{0,2},{1,3},{4,0},{5,1},{8,4},{9,5},{12,8},{13,9},{14,12},{15,13},... | collective-permute-start | bytes 1769480 | tf_op jit(solution)/shard_map/ppermute | solution.py:104
  464.5 19.8 %collective-permute-start.61 = (bf16[512,768]{1,0:T(8,128)(2,1)S(1)}, bf16[512,768]{1,0:T(8,128)(2,1)S(1)}, u32[]{:S(2)}, u32[]{:S(2)}) collective-permute-start(bf16[512,768]{1,0:T(8,128)(2,1)S(1)} %select_convert_fusion), channel_id=1, source_target_pairs={{0,16},{16,0},{1,17},{17,1},{2,18},{18,2},{3,19},{19,3},{4,20},{20... | collective-permute-start | bytes 2359304 | tf_op jit(solution)/shard_map/ppermute | solution.py:38
  (210 other events, 2340.7 us)

commit v6 on v4

--- a/solution.py
+++ b/solution.py
@@ -430,30 +430,28 @@
     return jnp.dot(a, b, preferred_element_type=F32)
 
 
-def forward_attend(source, weights, table, begin, track):
+def norms(source, weights):
     normed, scale = normalized(source.astype(F32))
     one = (normed * weights["g1"] + weights["b1"]).astype(BF16)
-    two = (normed * weights["g2"] + weights["b2"]).astype(BF16)
-    joined = matmul(one, weights["qkv"]) + weights["bqkv"]
-    one, two, joined = track.step((one, two, joined))
-    qkv, ctx, lse = track.step(attend(joined, table, begin))
-    return source, one, two, qkv, ctx, lse
-
-
-def forward_hidden(saved, weights, track):
-    two, ctx = saved[2], saved[4]
+    return one, (normed * weights["g2"] + weights["b2"]).astype(BF16)
+
+
+def joined_of(one, weights):
+    return matmul(one, weights["qkv"]) + weights["bqkv"]
+
+
+def hidden(two, weights):
     up = matmul(two, weights["up"]) + weights["bup"]
     phi = 0.5 * (1.0 + lax.erf(up * np.float32(0.5**0.5)))
-    middle = (up * phi).astype(BF16)
-    slope = (phi + up * jnp.exp(-0.5 * up * up) * np.float32((2 * np.pi) ** -0.5)).astype(BF16)
-    middle, slope = track.step((middle, slope))
-    part = matmul(ctx, weights["out"]) + matmul(middle, weights["down"])
-    (part,) = track.step((part,))
-    return part, (*saved, middle, slope)
-
-
-def back_attend(saved, grad, weights, table, begin, track):
-    qkv, lse = saved[3], saved[5]
+    slope = phi + up * jnp.exp(-0.5 * up * up) * np.float32((2 * np.pi) ** -0.5)
+    return (up * phi).astype(BF16), slope.astype(BF16)
+
+
+def branch_part(ctx, middle, weights):
+    return matmul(ctx, weights["out"]) + matmul(middle, weights["down"])
+
+
+def back_attend(qkv, lse, grad, weights, table, begin, track):
     d_ctx = dot_nt(grad, weights["out"]).astype(BF16)
     d_fused = attend_back(qkv, lse, d_ctx, table, begin)
     (d_fused,) = track.step((d_fused,))
@@ -461,9 +459,8 @@
     return d_fused, d_one
 
 
-def back_hidden(slope, grad, weights, track):
+def back_hidden(slope, grad, weights):
     d_up = (dot_nt(grad, weights["down"]) * slope.astype(F32)).astype(BF16)
-    (d_up,) = track.step((d_up,))
     return d_up, dot_nt(d_up, weights["up"])
 
 
@@ -645,13 +642,18 @@
         track.push(0, ("attn", 1), ring.gather(attn_blocks[1]))
         track.push(0, ("mlp", 1), ring.gather(mlp_blocks[1]))
         track.push(1, ("mlp", 0), ring.gather(mlp_blocks[0]))
-    saved_0 = forward_attend(both, weights_0, table, begin, track)
+    source_0 = both
+    one_0, two_0 = norms(both, weights_0)
+    one_0, two_0, joined = track.step((one_0, two_0, joined_of(one_0, weights_0)))
+    qkv_0, ctx_0, lse_0 = track.step(attend(joined, table, begin))
     weights_0.update(mlp_weights(0))
-    part, saved_0 = forward_hidden(saved_0, weights_0, track)
+    middle_0, slope_0 = track.step(hidden(two_0, weights_0))
+    (part,) = track.step((branch_part(ctx_0, middle_0, weights_0),))
     mid = (own_tokens.astype(F32) + summed(part) + weights_0["bout"]).astype(BF16)
     (mid,) = track.step((mid,))
-    both = paired(mid)
+    source_1 = paired(mid)
     weights_1 = attn_weights(1)
+
     def reduce_group(name, group):
         if ring is None:
             total = lax.psum_scatter(group, "dp", scatter_dimension=0, axis_index_groups=same_core(n))
@@ -726,19 +728,16 @@
         return jnp.sum(rows.astype(F32), axis=0)
 
     grad = paired(cot_low)
-    saved_1 = forward_attend(both, weights_1, table, begin, track)
-    d_fused, d_one = back_attend(saved_1, grad, weights_1, table, begin, track)
-    out_rows = out_rows_of(saved_1[4], grad)
-    (d_one, out_rows) = track.step((d_one, out_rows))
+    one, two = norms(source_1, weights_1)
     weights_1.update(mlp_weights(1))
-    part, (source, one, two, _, _, _, middle, slope) = forward_hidden(saved_1, weights_1, track)
-    last = (mid.astype(F32) + summed(part) + weights_1["bout"]).astype(BF16)
-    kept_rows, got = pick(low_section, mid, last), swap_section(pick(low_section, last, mid))
-    outputs = jnp.stack([pick(low_section, kept_rows, got), pick(low_section, got, kept_rows)])
-    d_up, d_two = back_hidden(slope, grad, weights_1, track)
+    middle, slope = hidden(two, weights_1)
+    d_up, d_two = back_hidden(slope, grad, weights_1)
     send_mlp(1, two, d_up, middle, grad)
-    (d_two,) = track.step((d_two,))
-    part, sums = back_norms(source, d_one, d_two, weights_1)
+    (one, d_two) = track.step((one, d_two))
+    qkv, ctx, lse = track.step(attend(joined_of(one, weights_1), table, begin))
+    d_fused, d_one = back_attend(qkv, lse, grad, weights_1, table, begin, track)
+    out_rows = out_rows_of(ctx, grad)
+    part, sums = back_norms(source_1, d_one, d_two, weights_1)
     small = (*sums, sums_of(d_fused), None, sums_of(d_up))
     (part,) = track.step((part,))
     send_attn(1, one, d_fused, out_rows, small, sums_of(cot_low))
@@ -746,19 +745,22 @@
     low_1 = grad_1.astype(BF16)
     (low_1, grad_1) = track.step((low_1, grad_1))
 
-    source, one, two, _, ctx, _, middle, slope = saved_0
+    last = (mid.astype(F32) + summed(branch_part(ctx, middle, weights_1)) + weights_1["bout"]).astype(BF16)
+    kept_out, got_out = pick(low_section, mid, last), swap_section(pick(low_section, last, mid))
+
     grad = paired(low_1)
-    d_up, d_two = back_hidden(slope, grad, weights_0, track)
-    send_mlp(0, two, d_up, middle, grad)
+    d_up, d_two = back_hidden(slope_0, grad, weights_0)
+    send_mlp(0, two_0, d_up, middle_0, grad)
     (d_two,) = track.step((d_two,))
-    out_rows = out_rows_of(ctx, grad)
-    d_fused, d_one = back_attend(saved_0, grad, weights_0, table, begin, track)
-    (d_one,) = track.step((d_one,))
-    part, sums = back_norms(source, d_one, d_two, weights_0)
+    out_rows = out_rows_of(ctx_0, grad)
+    d_fused, d_one = back_attend(qkv_0, lse_0, grad, weights_0, table, begin, track)
+    part, sums = back_norms(source_0, d_one, d_two, weights_0)
     small = (*sums, sums_of(d_fused), None, sums_of(d_up))
-    send_attn(0, one, d_fused, out_rows, small, sums_of(low_1))
+    (part, got_out) = track.step((part, got_out))
+    send_attn(0, one_0, d_fused, out_rows, small, sums_of(low_1))
     grad_0 = low_1.astype(F32) + summed(part)
     (grad_0,) = track.step((grad_0,))
+    outputs = jnp.stack([pick(low_section, kept_out, got_out), pick(low_section, got_out, kept_out)])
     sent = swap_section(pick(low_section, grad_1, grad_0).astype(BF16)).astype(F32)
     kept_rows = pick(low_section, grad_0, grad_1)
     in_grads = jnp.stack([pick(low_section, kept_rows, sent), pick(low_section, sent, kept_rows)])

time: 505 us -> 515 us (1.020)
  waiting for transfers between devices: 150 us -> 159 us
  other arithmetic: 80.9 us -> 74 us
  starting transfers between devices: 99.5 us -> 106 us
  matrix products: 54 us -> 59.3 us
    ppermute x16, waiting for transfers between devices: 27.8 us -> 53.7 us  [scatter(): ahead = lax.ppermute(ahead, 'dp', self.right)]
    ppermute x16, waiting for transfers between devices: 26.8 us -> 9.15 us  [scatter(): back = lax.ppermute(back, 'dp', self.left)]
    ppermute x16, starting transfers between devices: 6.94 us -> 20.1 us  [scatter(): back = lax.ppermute(back, 'dp', self.left)]
    ppermute x16, starting transfers between devices: 17.4 us -> 4.94 us  [scatter(): ahead = lax.ppermute(ahead, 'dp', self.right)]
    dot_general x8, matrix products: 21.8 us -> 31.5 us  [dot_nt(): lax.dot_general(a, b, (((1,), (1,)), ((), ())), preferred_element_type=F32)]
    ppermute x17, starting transfers between devices: 42.9 us -> 48.7 us  [swap_core(): return lax.ppermute(block, 'dp', [(i, i ^ 1) for i in range(n)])]
    unnamed x290 -> x278, local copies, waits for them, and re-layouts: 34.7 us -> 30.2 us
  transfers between devices with their start and end apart: 87 -> 87, of which waited for: 41 -> 40; matrix products, arithmetic and copies ran while one was open for 24% -> 21% of each run, Pallas kernels for 8% -> 10%
where the time goes in v6:
time: 515 us; the launch traced here: 506 us
  waiting for transfers between devices  159 us (31%)
  starting transfers between devices  106 us (21%)
  other arithmetic  74 us (14%)
  Pallas kernels  64.9 us (13%)
  matrix products  59.3 us (12%)
  local copies, waits for them, and re-layouts  39.4 us (8%)
    ppermute x16, waiting for transfers between devices, scatter(): ahead = lax.ppermute(ahead, 'dp', self.right)  53.7 us
    ppermute x17, starting transfers between devices, swap_core(): return lax.ppermute(block, 'dp', [(i, i ^ 1) for i in range(n)])  48.7 us
    ppermute x12, waiting for transfers between devices, gather(): ahead = lax.ppermute(ahead, 'dp', self.right)  43.9 us
    dot_general x8, matrix products, dot_nt(): lax.dot_general(a, b, (((1,), (1,)), ((), ())), preferred_element_type=F32)  31.5 us
    unnamed x278, local copies, waits for them, and re-layouts  30.2 us
    pallas_call x2, Pallas kernels, attend_back(): pl.pallas_call(attend_back_kernel, grid=(2, PAIRS), in_specs=[per_pair(le...  25.4 us
    dot_general x8, matrix products, matmul(): return jnp.dot(a, b, preferred_element_type=F32)  25 us
    ppermute x6, waiting for transfers between devices, swap_section(): return lax.ppermute(block, 'section', [(0, 1), (1, 0)])  23.3 us
  transfers between devices with their start and end apart: 87, of which 40 were waited for; matrix products, arithmetic and copies ran while one was open for 21% of the time, Pallas kernels for 10%

profile of v6, /device:TPU:1, one launch (start us, length us, event | category | flops | bytes accessed | tf_op | source)
XLA Modules:
  0.0 505.7 jit_solution(11197116455556181795)
XLA Ops:
  16.3 8.0 %collective-permute-done.3 = bf16[112,1536]{1,0:T(8,128)(2,1)S(1)} collective-permute-done((bf16[112,1536]{1,0:T(8,128)(2,1)S(1)}, bf16[112,1536]{1,0:T(8,128)(2,1)S(1)}, u32[]{:S(2)}, u32[]{:S(2)}) %collective-permute-start.3) | collective-permute-done | bytes 344096 | tf_op jit(solution)/shard_map/ppermute | solution.py:38
  68.2 9.3 %shard_map.274 = (bf16[1024,1152]{1,0:T(8,128)(2,1)S(1)}, bf16[1024,384]{1,0:T(8,128)(2,1)S(1)}, f32[1024,384]{1,0:T(8,128)S(1)}) custom-call(f32[1024,1152]{1,0:T(8,128)S(1)} %convolution_add_fusion.1.joined_ref, f32[1024,256]{1,0:T(8,128)S(1)} %pad_maximum_fusion.4.table_ref, s32[1024,1]{1,0:T(8,128)S(1)} %bitcast.212), custom_call_target="tpu_custom_call" | custom-call | flops 20000000000 | bytes 12000000 | tf_op jit(solution)/shard_map/pallas_call | solution.py:387
  88.1 13.3 %collective-permute-done.18.refs_3_ = bf16[112,1536]{1,0:T(8,128)(2,1)S(1)} collective-permute-done((bf16[112,1536]{1,0:T(8,128)(2,1)S(1)}, bf16[112,1536]{1,0:T(8,128)(2,1)S(1)}, u32[]{:S(2)}, u32[]{:S(2)}) %collective-permute-start.18) | collective-permute-done | bytes 344096 | tf_op jit(solution)/shard_map/ppermute | solution.py:75
  105.1 12.1 %collective-permute-start.34 = (bf16[384,384]{1,0:T(8,128)(2,1)S(1)}, bf16[384,384]{1,0:T(8,128)(2,1)S(1)}, u32[]{:S(2)}, u32[]{:S(2)}) collective-permute-start(bf16[384,384]{1,0:T(8,128)(2,1)S(1)} %get-tuple-element.186), channel_id=1, source_target_pairs={{0,1},{1,0},{2,3},{3,2},{4,5},{5,4},{6,7},{7,6},{8,9},{9,8},{10,11... | collective-permute-start | bytes 884744 | tf_op jit(solution)/shard_map/ppermute | solution.py:34
  119.8 8.6 %collective-permute-start.39 = (bf16[512,768]{1,0:T(8,128)(2,1)}, bf16[512,768]{1,0:T(8,128)(2,1)}, u32[]{:S(2)}, u32[]{:S(2)}) collective-permute-start(bf16[512,768]{1,0:T(8,128)(2,1)} %get-tuple-element.293), channel_id=1, source_target_pairs={{0,1},{1,0},{2,3},{3,2},{4,5},{5,4},{6,7},{7,6},{8,9},{9,8},{10,11... | collective-permute-start | bytes 2359304 | tf_op jit(solution)/shard_map/ppermute | solution.py:34
  131.8 7.1 %collective-permute-done.26.refs_7_ = bf16[48,1536]{1,0:T(8,128)(2,1)S(1)} collective-permute-done((bf16[48,1536]{1,0:T(8,128)(2,1)S(1)}, bf16[48,1536]{1,0:T(8,128)(2,1)S(1)}, u32[]{:S(2)}, u32[]{:S(2)}) %collective-permute-start.26) | collective-permute-done | bytes 147488 | tf_op jit(solution)/shard_map/ppermute | solution.py:80
  143.6 6.9 %fusion.4 = (bf16[1024,1536]{1,0:T(8,128)(2,1)}, bf16[1024,1536]{1,0:T(8,128)(2,1)S(1)}) fusion(f32[1536]{0:T(1024)S(1)} %slice_reduce_fusion.1, bf16[1024,768]{1,0:T(8,128)(2,1)S(1)} %get-tuple-element.178.two_ref, bf16[768,1536]{1,0:T(8,128)(2,1)S(1)} %get-tuple-element.181), kind=kOutput, calls=%fused_computation.6 | convolution fusion | flops 2434793472 | bytes 10229760 | tf_op jit(solution)/shard_map/dot_general | solution.py:430
  160.2 6.3 %collective-permute-done.32.refs_3_ = bf16[192,1536]{1,0:T(8,128)(2,1)S(1)} collective-permute-done((bf16[192,1536]{1,0:T(8,128)(2,1)S(1)}, bf16[192,1536]{1,0:T(8,128)(2,1)S(1)}, u32[]{:S(2)}, u32[]{:S(2)}) %collective-permute-start.32) | collective-permute-done | bytes 589856 | tf_op jit(solution)/shard_map/ppermute | solution.py:75
  178.8 9.1 %collective-permute-done.35.refs_5_ = bf16[192,1536]{1,0:T(8,128)(2,1)S(1)} collective-permute-done((bf16[192,1536]{1,0:T(8,128)(2,1)}, bf16[192,1536]{1,0:T(8,128)(2,1)S(1)}, u32[]{:S(2)}, u32[]{:S(2)}) %collective-permute-start.35) | collective-permute-done | bytes 589856 | tf_op jit(solution)/shard_map/ppermute | solution.py:75
  223.1 5.7 %shard_map.278 = bf16[8,192,1536]{2,1,0:T(8,128)(2,1)S(1)} custom-call(bf16[1024,768]{1,0:T(8,128)(2,1)S(1)} %get-tuple-element.346.two_ref, bf16[1024,1536]{1,0:T(8,128)(2,1)S(1)} %get-tuple-element.407.d_up_ref, bf16[1024,1536]{1,0:T(8,128)(2,1)S(1)} %get-tuple-element.404.middle_ref, bf16[1024,768]{1,0:T(8,128)(2,1)S(1)} %pad_maximum_fusion.2.grad_ref), custom_call_target="tpu_custom_call" | custom-call | tf_op jit(solution)/shard_map/pallas_call | solution.py:672
  234.2 9.3 %shard_map.279 = (bf16[1024,1152]{1,0:T(8,128)(2,1)S(1)}, bf16[1024,384]{1,0:T(8,128)(2,1)S(1)}, f32[1024,384]{1,0:T(8,128)S(1)}) custom-call(f32[1024,1152]{1,0:T(8,128)S(1)} %convolution_add_fusion.joined_ref, f32[1024,256]{1,0:T(8,128)S(1)} %pad_maximum_fusion.4.table_ref, s32[1024,1]{1,0:T(8,128)S(1)} %bitcast.213), custom_call_target="tpu_custom_call" | custom-call | flops 20000000000 | bytes 12000000 | tf_op jit(solution)/shard_map/pallas_call | solution.py:387
  266.2 12.7 %shard_map.280.fused_ref = bf16[1024,1152]{1,0:T(8,128)(2,1)S(1)} custom-call(bf16[1024,1152]{1,0:T(8,128)(2,1)S(1)} %copy-done.61, f32[1024,384]{1,0:T(8,128)S(1)} %copy-done.65, bf16[1024,384]{1,0:T(8,128)(2,1)S(1)} %copy-done.57, f32[1024,256]{1,0:T(8,128)S(1)} %pad_maximum_fusion.4.table_ref, s32[1024,1]{1,0:T(8,128)S(1)} %bitcast.214), custom_call_target="tpu_custom_call" | custom-call | flops 30000001024 | bytes 12000000 | tf_op jit(solution)/shard_map/pallas_call | solution.py:405
  281.6 5.9 %fusion.87 = (f32[1024]{0:T(1024)S(1)}, f32[1024]{0:T(1024)S(1)}, f32[1024,768]{1,0:T(8,128)}, f32[768]{0:T(1024)S(1)}, f32[768]{0:T(1024)S(1)}, /*index=5*/f32[768]{0:T(1024)S(1)}, f32[768]{0:T(1024)S(1)}) fusion(f32[1024]{0:T(1024)S(1)} %add_rsqrt_fusion, f32[1024]{0:T(1024)S(1)} %broadcast_multiply_fusion.4, bf16[512,768]{1,0:T(8,128)(2,1)S(1)} %copy-done.77, ...), kind=kOutput, calls=%fused_computation.321 | convolution fusion | flops 1826089984 | bytes 12027904 | tf_op jit(solution)/shard_map/dot_general | solution.py:177
  299.2 6.1 %collective-permute-done.49 = bf16[192,1536]{1,0:T(8,128)(2,1)} collective-permute-done((bf16[192,1536]{1,0:T(8,128)(2,1)}, bf16[192,1536]{1,0:T(8,128)(2,1)}, u32[]{:S(2)}, u32[]{:S(2)}) %collective-permute-start.49) | collective-permute-done | bytes 589856 | tf_op jit(solution)/shard_map/ppermute | solution.py:103
  313.4 10.7 %collective-permute-done.51 = bf16[192,1536]{1,0:T(8,128)(2,1)} collective-permute-done((bf16[192,1536]{1,0:T(8,128)(2,1)S(1)}, bf16[192,1536]{1,0:T(8,128)(2,1)}, u32[]{:S(2)}, u32[]{:S(2)}) %collective-permute-start.51) | collective-permute-done | bytes 589856 | tf_op jit(solution)/shard_map/ppermute | solution.py:103
  342.5 5.7 %shard_map.282 = bf16[8,192,1536]{2,1,0:T(8,128)(2,1)S(1)} custom-call(bf16[1024,768]{1,0:T(8,128)(2,1)S(1)} %copy-done.8, bf16[1024,1536]{1,0:T(8,128)(2,1)S(1)} %get-tuple-element.409.d_up_ref, bf16[1024,1536]{1,0:T(8,128)(2,1)S(1)} %copy-done.14, bf16[1024,768]{1,0:T(8,128)(2,1)S(1)} %pad_maximum_fusion.3.grad_ref), custom_call_target="tpu_custom_call" | custom-call | tf_op jit(solution)/shard_map/pallas_call | solution.py:672
  356.5 12.7 %shard_map.283.fused_ref = bf16[1024,1152]{1,0:T(8,128)(2,1)S(1)} custom-call(bf16[1024,1152]{1,0:T(8,128)(2,1)S(1)} %copy-done.59, f32[1024,384]{1,0:T(8,128)S(1)} %copy-done.63, bf16[1024,384]{1,0:T(8,128)(2,1)S(1)} %convolution_convert_fusion.dctx_ref, f32[1024,256]{1,0:T(8,128)S(1)} %copy-done.16, s32[1024,1]{1,0:T(8,128)S(1)} %bitcast.215), custom_call_target="tpu_custom_call" | custom-call | flops 30000001024 | bytes 12000000 | tf_op jit(solution)/shard_map/pallas_call | solution.py:405
  373.3 6.4 %collective-permute-done.60 = bf16[96,1536]{1,0:T(8,128)(2,1)S(1)} collective-permute-done((bf16[96,1536]{1,0:T(8,128)(2,1)}, bf16[96,1536]{1,0:T(8,128)(2,1)S(1)}, u32[]{:S(2)}, u32[]{:S(2)}) %collective-permute-start.60) | collective-permute-done | bytes 294944 | tf_op jit(solution)/shard_map/ppermute | solution.py:96
  379.7 6.1 %fusion.99 = f32[1024,768]{1,0:T(8,128)} fusion(bf16[1024,1152]{1,0:T(8,128)(2,1)} %copy-done.2, bf16[768,1152]{1,0:T(8,128)(2,1)} %copy-done.54), kind=kOutput, calls=%fused_computation.333 | convolution fusion | flops 1811939328 | bytes 7274496 | tf_op jit(solution)/shard_map/dot_general | solution.py:177
  401.8 10.2 %collective-permute-done.61 = bf16[112,1536]{1,0:T(8,128)(2,1)} collective-permute-done((bf16[112,1536]{1,0:T(8,128)(2,1)}, bf16[112,1536]{1,0:T(8,128)(2,1)}, u32[]{:S(2)}, u32[]{:S(2)}) %collective-permute-start.61) | collective-permute-done | bytes 344096 | tf_op jit(solution)/shard_map/ppermute | solution.py:103
  425.4 12.7 %collective-permute-done.66 = bf16[112,1536]{1,0:T(8,128)(2,1)S(1)} collective-permute-done((bf16[112,1536]{1,0:T(8,128)(2,1)S(1)}, bf16[112,1536]{1,0:T(8,128)(2,1)S(1)}, u32[]{:S(2)}, u32[]{:S(2)}) %collective-permute-start.66) | collective-permute-done | bytes 344096 | tf_op jit(solution)/shard_map/ppermute | solution.py:103
  449.8 6.8 %collective-permute-done.73 = bf16[48,1536]{1,0:T(8,128)(2,1)S(1)} collective-permute-done((bf16[48,1536]{1,0:T(8,128)(2,1)S(1)}, bf16[48,1536]{1,0:T(8,128)(2,1)S(1)}, u32[]{:S(2)}, u32[]{:S(2)}) %collective-permute-start.73) | collective-permute-done | bytes 147488 | tf_op jit(solution)/shard_map/ppermute | solution.py:95
  471.1 7.0 %collective-permute-done.85 = bf16[192,1536]{1,0:T(8,128)(2,1)S(1)} collective-permute-done((bf16[192,1536]{1,0:T(8,128)(2,1)S(1)}, bf16[192,1536]{1,0:T(8,128)(2,1)S(1)}, u32[]{:S(2)}, u32[]{:S(2)}) %collective-permute-start.85) | collective-permute-done | bytes 589856 | tf_op jit(solution)/shard_map/ppermute | solution.py:38
  494.6 5.5 %collective-permute-start.84 = (bf16[56,1536]{1,0:T(8,128)(2,1)S(1)}, bf16[56,1536]{1,0:T(8,128)(2,1)S(1)}, u32[]{:S(2)}, u32[]{:S(2)}) collective-permute-start(bf16[56,1536]{1,0:T(8,128)(2,1)S(1)} %select_convert_fusion.7), channel_id=1, source_target_pairs={{0,1},{1,0},{2,3},{3,2},{4,5},{5,4},{6,7},{7,6},{8,9},{9,8},{10,11... | collective-permute-start | bytes 516104 | tf_op jit(solution)/shard_map/ppermute | solution.py:34
  (631 shorter events, 298.5 us)
Async XLA Ops:
  29.3 19.8 %collective-permute-start.4 = (bf16[512,768]{1,0:T(8,128)(2,1)}, bf16[512,768]{1,0:T(8,128)(2,1)}, u32[]{:S(2)}, u32[]{:S(2)}) collective-permute-start(bf16[512,768]{1,0:T(8,128)(2,1)} %select_bitcast_fusion.2), channel_id=1, source_target_pairs={{0,1},{1,0},{2,3},{3,2},{4,5},{5,4},{6,7},{7,6},{8,9},{9,8},{10,11... | collective-permute-start | bytes 2359304 | tf_op jit(solution)/shard_map/ppermute | solution.py:34
  65.2 18.5 %collective-permute-start.15 = (bf16[192,1536]{1,0:T(8,128)(2,1)S(1)}, bf16[192,1536]{1,0:T(8,128)(2,1)S(1)}, u32[]{:S(2)}, u32[]{:S(2)}) collective-permute-start(bf16[192,1536]{1,0:T(8,128)(2,1)S(1)} %get-tuple-element.157.refs_0_), channel_id=1, source_target_pairs={{0,4},{1,5},{4,8},{5,9},{8,12},{9,13},{12,14},{13,15},{14,10},{15,... | collective-permute-start | bytes 1769480 | tf_op jit(solution)/shard_map/ppermute | solution.py:75
  83.7 18.2 %collective-permute-start.20 = (bf16[192,1536]{1,0:T(8,128)(2,1)S(1)}, bf16[192,1536]{1,0:T(8,128)(2,1)S(1)}, u32[]{:S(2)}, u32[]{:S(2)}) collective-permute-start(bf16[192,1536]{1,0:T(8,128)(2,1)S(1)} %collective-permute-done.15.refs_1_), channel_id=1, source_target_pairs={{0,4},{1,5},{4,8},{5,9},{8,12},{9,13},{12,14},{13,15},{14,10},{15,... | collective-permute-start | bytes 1769480 | tf_op jit(solution)/shard_map/ppermute | solution.py:75
  101.9 26.5 %collective-permute-start.24 = (bf16[192,1536]{1,0:T(8,128)(2,1)S(1)}, bf16[192,1536]{1,0:T(8,128)(2,1)S(1)}, u32[]{:S(2)}, u32[]{:S(2)}) collective-permute-start(bf16[192,1536]{1,0:T(8,128)(2,1)S(1)} %collective-permute-done.20.refs_3_), channel_id=1, source_target_pairs={{0,4},{1,5},{4,8},{5,9},{8,12},{9,13},{12,14},{13,15},{14,10},{15,... | collective-permute-start | bytes 1769480 | tf_op jit(solution)/shard_map/ppermute | solution.py:75
  103.1 25.3 %collective-permute-start.25 = (bf16[192,1536]{1,0:T(8,128)(2,1)S(1)}, bf16[192,1536]{1,0:T(8,128)(2,1)S(1)}, u32[]{:S(2)}, u32[]{:S(2)}) collective-permute-start(bf16[192,1536]{1,0:T(8,128)(2,1)S(1)} %collective-permute-done.21.refs_4_), channel_id=1, source_target_pairs={{0,2},{1,3},{4,0},{5,1},{8,4},{9,5},{12,8},{13,9},{14,12},{15,13},... | collective-permute-start | bytes 1769480 | tf_op jit(solution)/shard_map/ppermute | solution.py:76
  104.8 23.6 %collective-permute-start.23 = (bf16[112,1536]{1,0:T(8,128)(2,1)S(1)}, bf16[112,1536]{1,0:T(8,128)(2,1)S(1)}, u32[]{:S(2)}, u32[]{:S(2)}) collective-permute-start(bf16[112,1536]{1,0:T(8,128)(2,1)S(1)} %collective-permute-done.19.refs_4_), channel_id=1, source_target_pairs={{0,2},{1,3},{4,0},{5,1},{8,4},{9,5},{12,8},{13,9},{14,12},{15,13},... | collective-permute-start | bytes 1032200 | tf_op jit(solution)/shard_map/ppermute | solution.py:76
  105.1 25.9 %collective-permute-start.34 = (bf16[384,384]{1,0:T(8,128)(2,1)S(1)}, bf16[384,384]{1,0:T(8,128)(2,1)S(1)}, u32[]{:S(2)}, u32[]{:S(2)}) collective-permute-start(bf16[384,384]{1,0:T(8,128)(2,1)S(1)} %get-tuple-element.186), channel_id=1, source_target_pairs={{0,1},{1,0},{2,3},{3,2},{4,5},{5,4},{6,7},{7,6},{8,9},{9,8},{10,11... | collective-permute-start | bytes 884744 | tf_op jit(solution)/shard_map/ppermute | solution.py:34
  119.8 54.8 %collective-permute-start.39 = (bf16[512,768]{1,0:T(8,128)(2,1)}, bf16[512,768]{1,0:T(8,128)(2,1)}, u32[]{:S(2)}, u32[]{:S(2)}) collective-permute-start(bf16[512,768]{1,0:T(8,128)(2,1)} %get-tuple-element.293), channel_id=1, source_target_pairs={{0,1},{1,0},{2,3},{3,2},{4,5},{5,4},{6,7},{7,6},{8,9},{9,8},{10,11... | collective-permute-start | bytes 2359304 | tf_op jit(solution)/shard_map/ppermute | solution.py:34
  259.0 66.4 %collective-permute-start.45 = (bf16[512,768]{1,0:T(8,128)(2,1)}, bf16[512,768]{1,0:T(8,128)(2,1)}, u32[]{:S(2)}, u32[]{:S(2)}) collective-permute-start(bf16[512,768]{1,0:T(8,128)(2,1)} %select_convert_fusion.3), channel_id=1, source_target_pairs={{0,1},{1,0},{2,3},{3,2},{4,5},{5,4},{6,7},{7,6},{8,9},{9,8},{10,11... | collective-permute-start | bytes 2359304 | tf_op jit(solution)/shard_map/ppermute | solution.py:34
  329.2 72.7 %collective-permute-start.65 = (bf16[512,768]{1,0:T(8,128)(2,1)}, bf16[512,768]{1,0:T(8,128)(2,1)}, u32[]{:S(2)}, u32[]{:S(2)}) collective-permute-start(bf16[512,768]{1,0:T(8,128)(2,1)} %get-tuple-element.286), channel_id=1, source_target_pairs={{0,16},{16,0},{1,17},{17,1},{2,18},{18,2},{3,19},{19,3},{4,20},{20... | collective-permute-start | bytes 2359304 | tf_op jit(solution)/shard_map/ppermute | solution.py:38
  329.4 21.3 %collective-permute-start.55 = (bf16[64,1536]{1,0:T(8,128)(2,1)S(1)}, bf16[64,1536]{1,0:T(8,128)(2,1)S(1)}, u32[]{:S(2)}, u32[]{:S(2)}) collective-permute-start(bf16[64,1536]{1,0:T(8,128)(2,1)S(1)} %copy-done.112), channel_id=1, source_target_pairs={{0,2},{1,3},{4,0},{5,1},{8,4},{9,5},{12,8},{13,9},{14,12},{15,13},... | collective-permute-start | bytes 589832 | tf_op jit(solution)/shard_map/ppermute | solution.py:96
  330.6 20.1 %collective-permute-start.54 = (bf16[48,1536]{1,0:T(8,128)(2,1)S(1)}, bf16[48,1536]{1,0:T(8,128)(2,1)S(1)}, u32[]{:S(2)}, u32[]{:S(2)}) collective-permute-start(bf16[48,1536]{1,0:T(8,128)(2,1)S(1)} %copy-done.113), channel_id=1, source_target_pairs={{0,4},{1,5},{4,8},{5,9},{8,12},{9,13},{12,14},{13,15},{14,10},{15,... | collective-permute-start | bytes 442376 | tf_op jit(solution)/shard_map/ppermute | solution.py:95
  351.6 28.2 %collective-permute-start.58 = (bf16[112,1536]{1,0:T(8,128)(2,1)}, bf16[112,1536]{1,0:T(8,128)(2,1)}, u32[]{:S(2)}, u32[]{:S(2)}) collective-permute-start(bf16[112,1536]{1,0:T(8,128)(2,1)} %pad_maximum_fusion.21), channel_id=1, source_target_pairs={{0,2},{1,3},{4,0},{5,1},{8,4},{9,5},{12,8},{13,9},{14,12},{15,13},... | collective-permute-start | bytes 1032200 | tf_op jit(solution)/shard_map/ppermute | solution.py:104
  353.6 26.2 %collective-permute-start.57 = (bf16[112,1536]{1,0:T(8,128)(2,1)}, bf16[112,1536]{1,0:T(8,128)(2,1)}, u32[]{:S(2)}, u32[]{:S(2)}) collective-permute-start(bf16[112,1536]{1,0:T(8,128)(2,1)} %pad_maximum_fusion.20), channel_id=1, source_target_pairs={{0,4},{1,5},{4,8},{5,9},{8,12},{9,13},{12,14},{13,15},{14,10},{15,... | collective-permute-start | bytes 1032200 | tf_op jit(solution)/shard_map/ppermute | solution.py:103
  353.8 19.5 %collective-permute-start.59 = (bf16[96,1536]{1,0:T(8,128)(2,1)}, bf16[96,1536]{1,0:T(8,128)(2,1)}, u32[]{:S(2)}, u32[]{:S(2)}) collective-permute-start(bf16[96,1536]{1,0:T(8,128)(2,1)} %get-tuple-element.227), channel_id=1, source_target_pairs={{0,4},{1,5},{4,8},{5,9},{8,12},{9,13},{12,14},{13,15},{14,10},{15,... | collective-permute-start | bytes 884744 | tf_op jit(solution)/shard_map/ppermute | solution.py:95
  388.5 23.6 %collective-permute-start.64 = (bf16[192,1536]{1,0:T(8,128)(2,1)}, bf16[192,1536]{1,0:T(8,128)(2,1)}, u32[]{:S(2)}, u32[]{:S(2)}) collective-permute-start(bf16[192,1536]{1,0:T(8,128)(2,1)} %pad_maximum_fusion.13), channel_id=1, source_target_pairs={{0,2},{1,3},{4,0},{5,1},{8,4},{9,5},{12,8},{13,9},{14,12},{15,13},... | collective-permute-start | bytes 1769480 | tf_op jit(solution)/shard_map/ppermute | solution.py:104
  390.6 21.4 %collective-permute-start.63 = (bf16[192,1536]{1,0:T(8,128)(2,1)}, bf16[192,1536]{1,0:T(8,128)(2,1)}, u32[]{:S(2)}, u32[]{:S(2)}) collective-permute-start(bf16[192,1536]{1,0:T(8,128)(2,1)} %pad_maximum_fusion.12), channel_id=1, source_target_pairs={{0,4},{1,5},{4,8},{5,9},{8,12},{9,13},{12,14},{13,15},{14,10},{15,... | collective-permute-start | bytes 1769480 | tf_op jit(solution)/shard_map/ppermute | solution.py:103
  392.9 19.2 %collective-permute-start.61 = (bf16[112,1536]{1,0:T(8,128)(2,1)}, bf16[112,1536]{1,0:T(8,128)(2,1)}, u32[]{:S(2)}, u32[]{:S(2)}) collective-permute-start(bf16[112,1536]{1,0:T(8,128)(2,1)} %get-tuple-element.338), channel_id=1, source_target_pairs={{0,4},{1,5},{4,8},{5,9},{8,12},{9,13},{12,14},{13,15},{14,10},{15,... | collective-permute-start | bytes 1032200 | tf_op jit(solution)/shard_map/ppermute | solution.py:103
  393.0 19.0 %collective-permute-start.62 = (bf16[112,1536]{1,0:T(8,128)(2,1)}, bf16[112,1536]{1,0:T(8,128)(2,1)}, u32[]{:S(2)}, u32[]{:S(2)}) collective-permute-start(bf16[112,1536]{1,0:T(8,128)(2,1)} %get-tuple-element.337), channel_id=1, source_target_pairs={{0,2},{1,3},{4,0},{5,1},{8,4},{9,5},{12,8},{13,9},{14,12},{15,13},... | collective-permute-start | bytes 1032200 | tf_op jit(solution)/shard_map/ppermute | solution.py:104
  415.9 22.2 %collective-permute-start.68 = (bf16[192,1536]{1,0:T(8,128)(2,1)S(1)}, bf16[192,1536]{1,0:T(8,128)(2,1)S(1)}, u32[]{:S(2)}, u32[]{:S(2)}) collective-permute-start(bf16[192,1536]{1,0:T(8,128)(2,1)S(1)} %get-tuple-element.308), channel_id=1, source_target_pairs={{0,4},{1,5},{4,8},{5,9},{8,12},{9,13},{12,14},{13,15},{14,10},{15,... | collective-permute-start | bytes 1769480 | tf_op jit(solution)/shard_map/ppermute | solution.py:103
  416.1 22.0 %collective-permute-start.69 = (bf16[192,1536]{1,0:T(8,128)(2,1)S(1)}, bf16[192,1536]{1,0:T(8,128)(2,1)S(1)}, u32[]{:S(2)}, u32[]{:S(2)}) collective-permute-start(bf16[192,1536]{1,0:T(8,128)(2,1)S(1)} %get-tuple-element.307), channel_id=1, source_target_pairs={{0,2},{1,3},{4,0},{5,1},{8,4},{9,5},{12,8},{13,9},{14,12},{15,13},... | collective-permute-start | bytes 1769480 | tf_op jit(solution)/shard_map/ppermute | solution.py:104
  418.6 19.5 %collective-permute-start.66 = (bf16[112,1536]{1,0:T(8,128)(2,1)S(1)}, bf16[112,1536]{1,0:T(8,128)(2,1)S(1)}, u32[]{:S(2)}, u32[]{:S(2)}) collective-permute-start(bf16[112,1536]{1,0:T(8,128)(2,1)S(1)} %get-tuple-element.336), channel_id=1, source_target_pairs={{0,4},{1,5},{4,8},{5,9},{8,12},{9,13},{12,14},{13,15},{14,10},{15,... | collective-permute-start | bytes 1032200 | tf_op jit(solution)/shard_map/ppermute | solution.py:103
  418.8 19.3 %collective-permute-start.67 = (bf16[112,1536]{1,0:T(8,128)(2,1)S(1)}, bf16[112,1536]{1,0:T(8,128)(2,1)S(1)}, u32[]{:S(2)}, u32[]{:S(2)}) collective-permute-start(bf16[112,1536]{1,0:T(8,128)(2,1)S(1)} %get-tuple-element.335), channel_id=1, source_target_pairs={{0,2},{1,3},{4,0},{5,1},{8,4},{9,5},{12,8},{13,9},{14,12},{15,13},... | collective-permute-start | bytes 1032200 | tf_op jit(solution)/shard_map/ppermute | solution.py:104
  459.8 18.2 %collective-permute-start.85 = (bf16[192,1536]{1,0:T(8,128)(2,1)S(1)}, bf16[192,1536]{1,0:T(8,128)(2,1)S(1)}, u32[]{:S(2)}, u32[]{:S(2)}) collective-permute-start(bf16[192,1536]{1,0:T(8,128)(2,1)S(1)} %select_convert_fusion.5), channel_id=1, source_target_pairs={{0,16},{16,0},{1,17},{17,1},{2,18},{18,2},{3,19},{19,3},{4,20},{20... | collective-permute-start | bytes 1769480 | tf_op jit(solution)/shard_map/ppermute | solution.py:38
  (192 other events, 2152.9 us)

commit v7 on v6

--- a/solution.py
+++ b/solution.py
@@ -369,6 +369,10 @@
         out_ref[i, u:, :] = row_ref[...].astype(BF16)
 
 
+def small_cost():
+    return pl.CostEstimate(flops=1000, bytes_accessed=1000, transcendentals=0)
+
+
 def kernel_params():
     return pltpu.CompilerParams(vmem_limit_bytes=40 * 1024 * 1024)
 
@@ -395,7 +399,7 @@
             jax.ShapeDtypeStruct((tokens, HALF), F32),
         ],
         compiler_params=kernel_params(),
-        cost_estimate=pl.CostEstimate(flops=20_000_000_000, bytes_accessed=12_000_000, transcendentals=3_000_000),
+        cost_estimate=small_cost(),
     )(joined, table, begin)
 
 
@@ -415,7 +419,7 @@
         out_specs=per_pair(length, 3 * PAIR),
         out_shape=jax.ShapeDtypeStruct((tokens, QKVH), BF16),
         compiler_params=kernel_params(),
-        cost_estimate=pl.CostEstimate(flops=30_000_000_000, bytes_accessed=12_000_000, transcendentals=3_000_000),
+        cost_estimate=small_cost(),
     )(qkv, lse, dctx, table, begin)
 
 
@@ -526,6 +530,7 @@
                 out_shape=[jax.ShapeDtypeStruct(shape, BF16) for shape in shapes],
                 scratch_shapes=[pltpu.VMEM((8, LANES), F32)],
                 compiler_params=kernel_params(),
+                cost_estimate=small_cost(),
             )(core_scalar, *weights_in, *vectors)
         rows = jnp.concatenate([jnp.pad(v, ((0, 0), (0, LANES - v.shape[1]))) for v in vectors])
         attn, hidden = [], []
@@ -591,6 +596,7 @@
                     pltpu.VMEM((2, 1, FFH), F32),
                 ],
                 compiler_params=kernel_params(),
+                cost_estimate=small_cost(),
             )(place, *track.finish(("attn", layer)))
             widths = (D, D, D, D, QKVH, D, FFH)
             found = [vec[i, :w] for i, w in enumerate(widths)]
@@ -611,6 +617,7 @@
                 out_specs=[vmem()] * 2,
                 out_shape=[jax.ShapeDtypeStruct((D, FFH), BF16), jax.ShapeDtypeStruct((FFH, D), BF16)],
                 compiler_params=kernel_params(),
+                cost_estimate=small_cost(),
             )(place, *track.finish(("mlp", layer)))
         return {"up": up, "down": down}
 
@@ -681,6 +688,7 @@
                 out_specs=pl.BlockSpec((chips // 2, 2 * u, LANES), lambda g: (g, 0, 0)),
                 out_shape=jax.ShapeDtypeStruct((chips, 2 * u, LANES), BF16),
                 compiler_params=kernel_params(),
+                cost_estimate=small_cost(),
             )(two, d_up, middle, grad)
         reduce_group(("d_mlp", layer), group)
 
@@ -714,6 +722,7 @@
                 out_shape=jax.ShapeDtypeStruct((chips, u + PAD, LANES), BF16),
                 scratch_shapes=[pltpu.VMEM((PAD, LANES), F32)],
                 compiler_params=kernel_params(),
+                cost_estimate=small_cost(),
             )(one, d_fused, out_rows, unit, bq, bu)
         reduce_group(("d_attn", layer), group)
 

time: 515 us -> 513 us (level)
  starting transfers between devices: 106 us -> 100 us
    unnamed x278 -> x280, local copies, waits for them, and re-layouts: 30.2 us -> 26.5 us
  transfers between devices with their start and end apart: 87 -> 87, of which waited for: 40 -> 39; matrix products, arithmetic and copies ran while one was open for 21% -> 21% of each run, Pallas kernels for 10% -> 10%
where the time goes in v7:
time: 513 us; the launch traced here: 504 us
  waiting for transfers between devices  164 us (32%)
  starting transfers between devices  100 us (19%)
  other arithmetic  75.4 us (15%)
  Pallas kernels  65.8 us (13%)
  matrix products  59.9 us (12%)
  local copies, waits for them, and re-layouts  34.9 us (7%)
    ppermute x16, waiting for transfers between devices, scatter(): ahead = lax.ppermute(ahead, 'dp', self.right)  57.8 us
    ppermute x12, waiting for transfers between devices, gather(): ahead = lax.ppermute(ahead, 'dp', self.right)  46.7 us
    ppermute x17, starting transfers between devices, swap_core(): return lax.ppermute(block, 'dp', [(i, i ^ 1) for i in range(n)])  45.7 us
    dot_general x8, matrix products, dot_nt(): lax.dot_general(a, b, (((1,), (1,)), ((), ())), preferred_element_type=F32)  30.8 us
    unnamed x280, local copies, waits for them, and re-layouts  26.5 us
    dot_general x8, matrix products, matmul(): return jnp.dot(a, b, preferred_element_type=F32)  26.1 us
    pallas_call x2, Pallas kernels, attend_back(): pl.pallas_call(attend_back_kernel, grid=(2, PAIRS), in_specs=[per_pair(le...  25.4 us
    ppermute x6, waiting for transfers between devices, swap_section(): return lax.ppermute(block, 'section', [(0, 1), (1, 0)])  20.7 us
  transfers between devices with their start and end apart: 87, of which 39 were waited for; matrix products, arithmetic and copies ran while one was open for 21% of the time, Pallas kernels for 10%

profile of v7, /device:TPU:1, one launch (start us, length us, event | category | flops | bytes accessed | tf_op | source)
XLA Modules:
  0.0 503.7 jit_solution(258416969429932520)
XLA Ops:
  16.1 7.1 %collective-permute-done.3 = bf16[112,1536]{1,0:T(8,128)(2,1)S(1)} collective-permute-done((bf16[112,1536]{1,0:T(8,128)(2,1)S(1)}, bf16[112,1536]{1,0:T(8,128)(2,1)S(1)}, u32[]{:S(2)}, u32[]{:S(2)}) %collective-permute-start.3) | collective-permute-done | bytes 344096 | tf_op jit(solution)/shard_map/ppermute | solution.py:38
  27.8 7.6 %collective-permute-done.5.refs_1_ = bf16[112,1536]{1,0:T(8,128)(2,1)S(1)} collective-permute-done((bf16[112,1536]{1,0:T(8,128)(2,1)S(1)}, bf16[112,1536]{1,0:T(8,128)(2,1)S(1)}, u32[]{:S(2)}, u32[]{:S(2)}) %collective-permute-start.5) | collective-permute-done | bytes 344096 | tf_op jit(solution)/shard_map/ppermute | solution.py:75
  39.1 5.8 %collective-permute-done.7.refs_3_ = bf16[112,1536]{1,0:T(8,128)(2,1)S(1)} collective-permute-done((bf16[112,1536]{1,0:T(8,128)(2,1)S(1)}, bf16[112,1536]{1,0:T(8,128)(2,1)S(1)}, u32[]{:S(2)}, u32[]{:S(2)}) %collective-permute-start.7) | collective-permute-done | bytes 344096 | tf_op jit(solution)/shard_map/ppermute | solution.py:75
  73.7 9.3 %shard_map.274 = (bf16[1024,1152]{1,0:T(8,128)(2,1)S(1)}, bf16[1024,384]{1,0:T(8,128)(2,1)S(1)}, f32[1024,384]{1,0:T(8,128)S(1)}) custom-call(f32[1024,1152]{1,0:T(8,128)S(1)} %copy-done.12, f32[1024,256]{1,0:T(8,128)S(1)} %pad_maximum_fusion.4.table_ref, s32[1024,1]{1,0:T(8,128)S(1)} %bitcast.212), custom_call_target="tpu_custom_call" | custom-call | flops 1000 | bytes 1000 | tf_op jit(solution)/shard_map/pallas_call | solution.py:391
  89.3 14.0 %collective-permute-done.18.refs_3_ = bf16[112,1536]{1,0:T(8,128)(2,1)S(1)} collective-permute-done((bf16[112,1536]{1,0:T(8,128)(2,1)S(1)}, bf16[112,1536]{1,0:T(8,128)(2,1)S(1)}, u32[]{:S(2)}, u32[]{:S(2)}) %collective-permute-start.18) | collective-permute-done | bytes 344096 | tf_op jit(solution)/shard_map/ppermute | solution.py:75
  108.0 11.1 %collective-permute-start.34 = (bf16[384,384]{1,0:T(8,128)(2,1)S(1)}, bf16[384,384]{1,0:T(8,128)(2,1)S(1)}, u32[]{:S(2)}, u32[]{:S(2)}) collective-permute-start(bf16[384,384]{1,0:T(8,128)(2,1)S(1)} %copy-done.73), channel_id=1, source_target_pairs={{0,1},{1,0},{2,3},{3,2},{4,5},{5,4},{6,7},{7,6},{8,9},{9,8},{10,11... | collective-permute-start | bytes 884744 | tf_op jit(solution)/shard_map/ppermute | solution.py:34
  121.6 7.9 %collective-permute-start.39 = (bf16[512,768]{1,0:T(8,128)(2,1)}, bf16[512,768]{1,0:T(8,128)(2,1)}, u32[]{:S(2)}, u32[]{:S(2)}) collective-permute-start(bf16[512,768]{1,0:T(8,128)(2,1)} %get-tuple-element.293), channel_id=1, source_target_pairs={{0,1},{1,0},{2,3},{3,2},{4,5},{5,4},{6,7},{7,6},{8,9},{9,8},{10,11... | collective-permute-start | bytes 2359304 | tf_op jit(solution)/shard_map/ppermute | solution.py:34
  132.9 7.4 %collective-permute-done.26.refs_7_ = bf16[48,1536]{1,0:T(8,128)(2,1)S(1)} collective-permute-done((bf16[48,1536]{1,0:T(8,128)(2,1)S(1)}, bf16[48,1536]{1,0:T(8,128)(2,1)S(1)}, u32[]{:S(2)}, u32[]{:S(2)}) %collective-permute-start.26) | collective-permute-done | bytes 147488 | tf_op jit(solution)/shard_map/ppermute | solution.py:80
  145.9 6.9 %fusion.4 = (bf16[1024,1536]{1,0:T(8,128)(2,1)}, bf16[1024,1536]{1,0:T(8,128)(2,1)S(1)}) fusion(f32[1536]{0:T(1024)S(1)} %slice_reduce_fusion.1, bf16[1024,768]{1,0:T(8,128)(2,1)S(1)} %get-tuple-element.178.two_ref, bf16[768,1536]{1,0:T(8,128)(2,1)S(1)} %get-tuple-element.181), kind=kOutput, calls=%fused_computation.6 | convolution fusion | flops 2434793472 | bytes 10229760 | tf_op jit(solution)/shard_map/dot_general | solution.py:434
  161.4 6.3 %collective-permute-done.32.refs_3_ = bf16[192,1536]{1,0:T(8,128)(2,1)} collective-permute-done((bf16[192,1536]{1,0:T(8,128)(2,1)S(1)}, bf16[192,1536]{1,0:T(8,128)(2,1)}, u32[]{:S(2)}, u32[]{:S(2)}) %collective-permute-start.32) | collective-permute-done | bytes 589856 | tf_op jit(solution)/shard_map/ppermute | solution.py:75
  180.9 9.0 %collective-permute-done.35.refs_5_ = bf16[192,1536]{1,0:T(8,128)(2,1)S(1)} collective-permute-done((bf16[192,1536]{1,0:T(8,128)(2,1)}, bf16[192,1536]{1,0:T(8,128)(2,1)S(1)}, u32[]{:S(2)}, u32[]{:S(2)}) %collective-permute-start.35) | collective-permute-done | bytes 589856 | tf_op jit(solution)/shard_map/ppermute | solution.py:75
  220.4 5.7 %shard_map.278 = bf16[8,192,1536]{2,1,0:T(8,128)(2,1)S(1)} custom-call(bf16[1024,768]{1,0:T(8,128)(2,1)S(1)} %get-tuple-element.346.two_ref, bf16[1024,1536]{1,0:T(8,128)(2,1)S(1)} %get-tuple-element.407.d_up_ref, bf16[1024,1536]{1,0:T(8,128)(2,1)S(1)} %get-tuple-element.404.middle_ref, bf16[1024,768]{1,0:T(8,128)(2,1)S(1)} %pad_maximum_fusion.2.grad_ref), custom_call_target="tpu_custom_call" | custom-call | flops 1000 | bytes 1000 | tf_op jit(solution)/shard_map/pallas_call | solution.py:679
  233.7 9.3 %shard_map.279 = (bf16[1024,1152]{1,0:T(8,128)(2,1)S(1)}, bf16[1024,384]{1,0:T(8,128)(2,1)S(1)}, f32[1024,384]{1,0:T(8,128)S(1)}) custom-call(f32[1024,1152]{1,0:T(8,128)S(1)} %convolution_add_fusion.joined_ref, f32[1024,256]{1,0:T(8,128)S(1)} %pad_maximum_fusion.4.table_ref, s32[1024,1]{1,0:T(8,128)S(1)} %bitcast.213), custom_call_target="tpu_custom_call" | custom-call | flops 1000 | bytes 1000 | tf_op jit(solution)/shard_map/pallas_call | solution.py:391
  265.4 12.7 %shard_map.280.fused_ref = bf16[1024,1152]{1,0:T(8,128)(2,1)S(1)} custom-call(bf16[1024,1152]{1,0:T(8,128)(2,1)S(1)} %copy-done.21, f32[1024,384]{1,0:T(8,128)S(1)} %copy-done.25, bf16[1024,384]{1,0:T(8,128)(2,1)S(1)} %copy-done.30, f32[1024,256]{1,0:T(8,128)S(1)} %pad_maximum_fusion.4.table_ref, s32[1024,1]{1,0:T(8,128)S(1)} %bitcast.214), custom_call_target="tpu_custom_call" | custom-call | flops 1000 | bytes 1000 | tf_op jit(solution)/shard_map/pallas_call | solution.py:409
  280.2 5.9 %fusion.87 = (f32[1024]{0:T(1024)S(1)}, f32[1024]{0:T(1024)S(1)}, f32[1024,768]{1,0:T(8,128)}, f32[768]{0:T(1024)S(1)}, f32[768]{0:T(1024)S(1)}, /*index=5*/f32[768]{0:T(1024)S(1)}, f32[768]{0:T(1024)S(1)}) fusion(f32[1024]{0:T(1024)S(1)} %add_rsqrt_fusion, f32[1024]{0:T(1024)S(1)} %broadcast_multiply_fusion.4, bf16[512,768]{1,0:T(8,128)(2,1)S(1)} %copy-done.85, ...), kind=kOutput, calls=%fused_computation.321 | convolution fusion | flops 1826089984 | bytes 12027904 | tf_op jit(solution)/shard_map/dot_general | solution.py:177
  297.2 6.4 %collective-permute-done.49 = bf16[192,1536]{1,0:T(8,128)(2,1)} collective-permute-done((bf16[192,1536]{1,0:T(8,128)(2,1)}, bf16[192,1536]{1,0:T(8,128)(2,1)}, u32[]{:S(2)}, u32[]{:S(2)}) %collective-permute-start.49) | collective-permute-done | bytes 589856 | tf_op jit(solution)/shard_map/ppermute | solution.py:103
  310.2 11.6 %collective-permute-done.51 = bf16[192,1536]{1,0:T(8,128)(2,1)S(1)} collective-permute-done((bf16[192,1536]{1,0:T(8,128)(2,1)S(1)}, bf16[192,1536]{1,0:T(8,128)(2,1)S(1)}, u32[]{:S(2)}, u32[]{:S(2)}) %collective-permute-start.51) | collective-permute-done | bytes 589856 | tf_op jit(solution)/shard_map/ppermute | solution.py:103
  340.6 5.7 %shard_map.282 = bf16[8,192,1536]{2,1,0:T(8,128)(2,1)S(1)} custom-call(bf16[1024,768]{1,0:T(8,128)(2,1)S(1)} %copy-done.7, bf16[1024,1536]{1,0:T(8,128)(2,1)S(1)} %get-tuple-element.409.d_up_ref, bf16[1024,1536]{1,0:T(8,128)(2,1)S(1)} %copy-done.14, bf16[1024,768]{1,0:T(8,128)(2,1)S(1)} %pad_maximum_fusion.3.grad_ref), custom_call_target="tpu_custom_call" | custom-call | flops 1000 | bytes 1000 | tf_op jit(solution)/shard_map/pallas_call | solution.py:679
  356.5 12.7 %shard_map.283.fused_ref = bf16[1024,1152]{1,0:T(8,128)(2,1)S(1)} custom-call(bf16[1024,1152]{1,0:T(8,128)(2,1)S(1)} %copy-done.19, f32[1024,384]{1,0:T(8,128)S(1)} %copy-done.23, bf16[1024,384]{1,0:T(8,128)(2,1)S(1)} %convolution_convert_fusion.dctx_ref, f32[1024,256]{1,0:T(8,128)S(1)} %pad_maximum_fusion.4.table_ref, s32[1024,1]{1,0:T(8,128)S(1)} %bitcast.215), custom_call_target="tpu_custom_call" | custom-call | flops 1000 | bytes 1000 | tf_op jit(solution)/shard_map/pallas_call | solution.py:409
  372.1 6.3 %collective-permute-done.60 = bf16[96,1536]{1,0:T(8,128)(2,1)S(1)} collective-permute-done((bf16[96,1536]{1,0:T(8,128)(2,1)}, bf16[96,1536]{1,0:T(8,128)(2,1)S(1)}, u32[]{:S(2)}, u32[]{:S(2)}) %collective-permute-start.60) | collective-permute-done | bytes 294944 | tf_op jit(solution)/shard_map/ppermute | solution.py:96
  399.9 9.9 %collective-permute-done.61 = bf16[112,1536]{1,0:T(8,128)(2,1)S(1)} collective-permute-done((bf16[112,1536]{1,0:T(8,128)(2,1)}, bf16[112,1536]{1,0:T(8,128)(2,1)S(1)}, u32[]{:S(2)}, u32[]{:S(2)}) %collective-permute-start.61) | collective-permute-done | bytes 344096 | tf_op jit(solution)/shard_map/ppermute | solution.py:103
  422.2 13.7 %collective-permute-done.66 = bf16[112,1536]{1,0:T(8,128)(2,1)S(1)} collective-permute-done((bf16[112,1536]{1,0:T(8,128)(2,1)S(1)}, bf16[112,1536]{1,0:T(8,128)(2,1)S(1)}, u32[]{:S(2)}, u32[]{:S(2)}) %collective-permute-start.66) | collective-permute-done | bytes 344096 | tf_op jit(solution)/shard_map/ppermute | solution.py:103
  444.9 9.4 %collective-permute-done.73 = bf16[48,1536]{1,0:T(8,128)(2,1)S(1)} collective-permute-done((bf16[48,1536]{1,0:T(8,128)(2,1)S(1)}, bf16[48,1536]{1,0:T(8,128)(2,1)S(1)}, u32[]{:S(2)}, u32[]{:S(2)}) %collective-permute-start.73) | collective-permute-done | bytes 147488 | tf_op jit(solution)/shard_map/ppermute | solution.py:95
  467.5 6.6 %collective-permute-done.85 = bf16[192,1536]{1,0:T(8,128)(2,1)S(1)} collective-permute-done((bf16[192,1536]{1,0:T(8,128)(2,1)S(1)}, bf16[192,1536]{1,0:T(8,128)(2,1)S(1)}, u32[]{:S(2)}, u32[]{:S(2)}) %collective-permute-start.85) | collective-permute-done | bytes 589856 | tf_op jit(solution)/shard_map/ppermute | solution.py:38
  (633 shorter events, 292.1 us)
Async XLA Ops:
  16.1 21.7 %collective-permute-start.1 = (bf16[192,1536]{1,0:T(8,128)(2,1)}, bf16[192,1536]{1,0:T(8,128)(2,1)S(1)}, u32[]{:S(2)}, u32[]{:S(2)}) collective-permute-start(bf16[192,1536]{1,0:T(8,128)(2,1)} %pad_maximum_fusion.6), channel_id=1, source_target_pairs={{0,16},{16,0},{1,17},{17,1},{2,18},{18,2},{3,19},{19,3},{4,20},{20... | collective-permute-start | bytes 1769480 | tf_op jit(solution)/shard_map/ppermute | solution.py:38
  27.0 20.3 %collective-permute-start.4 = (bf16[512,768]{1,0:T(8,128)(2,1)S(1)}, bf16[512,768]{1,0:T(8,128)(2,1)S(1)}, u32[]{:S(2)}, u32[]{:S(2)}) collective-permute-start(bf16[512,768]{1,0:T(8,128)(2,1)S(1)} %select_bitcast_fusion.2), channel_id=1, source_target_pairs={{0,1},{1,0},{2,3},{3,2},{4,5},{5,4},{6,7},{7,6},{8,9},{9,8},{10,11... | collective-permute-start | bytes 2359304 | tf_op jit(solution)/shard_map/ppermute | solution.py:34
  66.1 18.8 %collective-permute-start.15 = (bf16[192,1536]{1,0:T(8,128)(2,1)}, bf16[192,1536]{1,0:T(8,128)(2,1)}, u32[]{:S(2)}, u32[]{:S(2)}) collective-permute-start(bf16[192,1536]{1,0:T(8,128)(2,1)} %get-tuple-element.157.refs_0_), channel_id=1, source_target_pairs={{0,4},{1,5},{4,8},{5,9},{8,12},{9,13},{12,14},{13,15},{14,10},{15,... | collective-permute-start | bytes 1769480 | tf_op jit(solution)/shard_map/ppermute | solution.py:75
  103.4 26.1 %collective-permute-start.24 = (bf16[192,1536]{1,0:T(8,128)(2,1)S(1)}, bf16[192,1536]{1,0:T(8,128)(2,1)S(1)}, u32[]{:S(2)}, u32[]{:S(2)}) collective-permute-start(bf16[192,1536]{1,0:T(8,128)(2,1)S(1)} %collective-permute-done.20.refs_3_), channel_id=1, source_target_pairs={{0,4},{1,5},{4,8},{5,9},{8,12},{9,13},{12,14},{13,15},{14,10},{15,... | collective-permute-start | bytes 1769480 | tf_op jit(solution)/shard_map/ppermute | solution.py:75
  104.4 25.1 %collective-permute-start.25 = (bf16[192,1536]{1,0:T(8,128)(2,1)S(1)}, bf16[192,1536]{1,0:T(8,128)(2,1)S(1)}, u32[]{:S(2)}, u32[]{:S(2)}) collective-permute-start(bf16[192,1536]{1,0:T(8,128)(2,1)S(1)} %collective-permute-done.21.refs_4_), channel_id=1, source_target_pairs={{0,2},{1,3},{4,0},{5,1},{8,4},{9,5},{12,8},{13,9},{14,12},{15,13},... | collective-permute-start | bytes 1769480 | tf_op jit(solution)/shard_map/ppermute | solution.py:76
  106.9 22.7 %collective-permute-start.23 = (bf16[112,1536]{1,0:T(8,128)(2,1)S(1)}, bf16[112,1536]{1,0:T(8,128)(2,1)S(1)}, u32[]{:S(2)}, u32[]{:S(2)}) collective-permute-start(bf16[112,1536]{1,0:T(8,128)(2,1)S(1)} %collective-permute-done.19.refs_4_), channel_id=1, source_target_pairs={{0,2},{1,3},{4,0},{5,1},{8,4},{9,5},{12,8},{13,9},{14,12},{15,13},... | collective-permute-start | bytes 1032200 | tf_op jit(solution)/shard_map/ppermute | solution.py:76
  108.0 24.4 %collective-permute-start.34 = (bf16[384,384]{1,0:T(8,128)(2,1)S(1)}, bf16[384,384]{1,0:T(8,128)(2,1)S(1)}, u32[]{:S(2)}, u32[]{:S(2)}) collective-permute-start(bf16[384,384]{1,0:T(8,128)(2,1)S(1)} %copy-done.73), channel_id=1, source_target_pairs={{0,1},{1,0},{2,3},{3,2},{4,5},{5,4},{6,7},{7,6},{8,9},{9,8},{10,11... | collective-permute-start | bytes 884744 | tf_op jit(solution)/shard_map/ppermute | solution.py:34
  121.6 54.6 %collective-permute-start.39 = (bf16[512,768]{1,0:T(8,128)(2,1)}, bf16[512,768]{1,0:T(8,128)(2,1)}, u32[]{:S(2)}, u32[]{:S(2)}) collective-permute-start(bf16[512,768]{1,0:T(8,128)(2,1)} %get-tuple-element.293), channel_id=1, source_target_pairs={{0,1},{1,0},{2,3},{3,2},{4,5},{5,4},{6,7},{7,6},{8,9},{9,8},{10,11... | collective-permute-start | bytes 2359304 | tf_op jit(solution)/shard_map/ppermute | solution.py:34
  259.2 19.9 %collective-permute-start.47 = (bf16[192,1536]{1,0:T(8,128)(2,1)S(1)}, bf16[192,1536]{1,0:T(8,128)(2,1)S(1)}, u32[]{:S(2)}, u32[]{:S(2)}) collective-permute-start(bf16[192,1536]{1,0:T(8,128)(2,1)S(1)} %pad_maximum_fusion.10), channel_id=1, source_target_pairs={{0,2},{1,3},{4,0},{5,1},{8,4},{9,5},{12,8},{13,9},{14,12},{15,13},... | collective-permute-start | bytes 1769480 | tf_op jit(solution)/shard_map/ppermute | solution.py:104
  265.1 58.9 %collective-permute-start.45 = (bf16[512,768]{1,0:T(8,128)(2,1)}, bf16[512,768]{1,0:T(8,128)(2,1)}, u32[]{:S(2)}, u32[]{:S(2)}) collective-permute-start(bf16[512,768]{1,0:T(8,128)(2,1)} %select_convert_fusion.3), channel_id=1, source_target_pairs={{0,1},{1,0},{2,3},{3,2},{4,5},{5,4},{6,7},{7,6},{8,9},{9,8},{10,11... | collective-permute-start | bytes 2359304 | tf_op jit(solution)/shard_map/ppermute | solution.py:34
  327.6 72.3 %collective-permute-start.65 = (bf16[512,768]{1,0:T(8,128)(2,1)}, bf16[512,768]{1,0:T(8,128)(2,1)}, u32[]{:S(2)}, u32[]{:S(2)}) collective-permute-start(bf16[512,768]{1,0:T(8,128)(2,1)} %get-tuple-element.286), channel_id=1, source_target_pairs={{0,16},{16,0},{1,17},{17,1},{2,18},{18,2},{3,19},{19,3},{4,20},{20... | collective-permute-start | bytes 2359304 | tf_op jit(solution)/shard_map/ppermute | solution.py:38
  328.8 20.0 %collective-permute-start.55 = (bf16[64,1536]{1,0:T(8,128)(2,1)S(1)}, bf16[64,1536]{1,0:T(8,128)(2,1)S(1)}, u32[]{:S(2)}, u32[]{:S(2)}) collective-permute-start(bf16[64,1536]{1,0:T(8,128)(2,1)S(1)} %get-tuple-element.222), channel_id=1, source_target_pairs={{0,2},{1,3},{4,0},{5,1},{8,4},{9,5},{12,8},{13,9},{14,12},{15,13},... | collective-permute-start | bytes 589832 | tf_op jit(solution)/shard_map/ppermute | solution.py:96
  330.0 18.8 %collective-permute-start.54 = (bf16[48,1536]{1,0:T(8,128)(2,1)S(1)}, bf16[48,1536]{1,0:T(8,128)(2,1)S(1)}, u32[]{:S(2)}, u32[]{:S(2)}) collective-permute-start(bf16[48,1536]{1,0:T(8,128)(2,1)S(1)} %get-tuple-element.221), channel_id=1, source_target_pairs={{0,4},{1,5},{4,8},{5,9},{8,12},{9,13},{12,14},{13,15},{14,10},{15,... | collective-permute-start | bytes 442376 | tf_op jit(solution)/shard_map/ppermute | solution.py:95
  350.7 27.7 %collective-permute-start.58 = (bf16[112,1536]{1,0:T(8,128)(2,1)}, bf16[112,1536]{1,0:T(8,128)(2,1)}, u32[]{:S(2)}, u32[]{:S(2)}) collective-permute-start(bf16[112,1536]{1,0:T(8,128)(2,1)} %pad_maximum_fusion.21), channel_id=1, source_target_pairs={{0,2},{1,3},{4,0},{5,1},{8,4},{9,5},{12,8},{13,9},{14,12},{15,13},... | collective-permute-start | bytes 1032200 | tf_op jit(solution)/shard_map/ppermute | solution.py:104
  353.6 24.8 %collective-permute-start.57 = (bf16[112,1536]{1,0:T(8,128)(2,1)}, bf16[112,1536]{1,0:T(8,128)(2,1)}, u32[]{:S(2)}, u32[]{:S(2)}) collective-permute-start(bf16[112,1536]{1,0:T(8,128)(2,1)} %pad_maximum_fusion.20), channel_id=1, source_target_pairs={{0,4},{1,5},{4,8},{5,9},{8,12},{9,13},{12,14},{13,15},{14,10},{15,... | collective-permute-start | bytes 1032200 | tf_op jit(solution)/shard_map/ppermute | solution.py:103
  386.4 23.5 %collective-permute-start.64 = (bf16[192,1536]{1,0:T(8,128)(2,1)}, bf16[192,1536]{1,0:T(8,128)(2,1)}, u32[]{:S(2)}, u32[]{:S(2)}) collective-permute-start(bf16[192,1536]{1,0:T(8,128)(2,1)} %pad_maximum_fusion.13), channel_id=1, source_target_pairs={{0,2},{1,3},{4,0},{5,1},{8,4},{9,5},{12,8},{13,9},{14,12},{15,13},... | collective-permute-start | bytes 1769480 | tf_op jit(solution)/shard_map/ppermute | solution.py:104
  388.5 21.3 %collective-permute-start.63 = (bf16[192,1536]{1,0:T(8,128)(2,1)}, bf16[192,1536]{1,0:T(8,128)(2,1)}, u32[]{:S(2)}, u32[]{:S(2)}) collective-permute-start(bf16[192,1536]{1,0:T(8,128)(2,1)} %pad_maximum_fusion.12), channel_id=1, source_target_pairs={{0,4},{1,5},{4,8},{5,9},{8,12},{9,13},{12,14},{13,15},{14,10},{15,... | collective-permute-start | bytes 1769480 | tf_op jit(solution)/shard_map/ppermute | solution.py:103
  391.0 18.8 %collective-permute-start.61 = (bf16[112,1536]{1,0:T(8,128)(2,1)}, bf16[112,1536]{1,0:T(8,128)(2,1)S(1)}, u32[]{:S(2)}, u32[]{:S(2)}) collective-permute-start(bf16[112,1536]{1,0:T(8,128)(2,1)} %get-tuple-element.338), channel_id=1, source_target_pairs={{0,4},{1,5},{4,8},{5,9},{8,12},{9,13},{12,14},{13,15},{14,10},{15,... | collective-permute-start | bytes 1032200 | tf_op jit(solution)/shard_map/ppermute | solution.py:103
  391.2 18.7 %collective-permute-start.62 = (bf16[112,1536]{1,0:T(8,128)(2,1)}, bf16[112,1536]{1,0:T(8,128)(2,1)}, u32[]{:S(2)}, u32[]{:S(2)}) collective-permute-start(bf16[112,1536]{1,0:T(8,128)(2,1)} %get-tuple-element.337), channel_id=1, source_target_pairs={{0,2},{1,3},{4,0},{5,1},{8,4},{9,5},{12,8},{13,9},{14,12},{15,13},... | collective-permute-start | bytes 1032200 | tf_op jit(solution)/shard_map/ppermute | solution.py:104
  413.6 22.2 %collective-permute-start.68 = (bf16[192,1536]{1,0:T(8,128)(2,1)S(1)}, bf16[192,1536]{1,0:T(8,128)(2,1)S(1)}, u32[]{:S(2)}, u32[]{:S(2)}) collective-permute-start(bf16[192,1536]{1,0:T(8,128)(2,1)S(1)} %get-tuple-element.308), channel_id=1, source_target_pairs={{0,4},{1,5},{4,8},{5,9},{8,12},{9,13},{12,14},{13,15},{14,10},{15,... | collective-permute-start | bytes 1769480 | tf_op jit(solution)/shard_map/ppermute | solution.py:103
  413.9 22.0 %collective-permute-start.69 = (bf16[192,1536]{1,0:T(8,128)(2,1)S(1)}, bf16[192,1536]{1,0:T(8,128)(2,1)S(1)}, u32[]{:S(2)}, u32[]{:S(2)}) collective-permute-start(bf16[192,1536]{1,0:T(8,128)(2,1)S(1)} %get-tuple-element.307), channel_id=1, source_target_pairs={{0,2},{1,3},{4,0},{5,1},{8,4},{9,5},{12,8},{13,9},{14,12},{15,13},... | collective-permute-start | bytes 1769480 | tf_op jit(solution)/shard_map/ppermute | solution.py:104
  416.5 19.3 %collective-permute-start.66 = (bf16[112,1536]{1,0:T(8,128)(2,1)S(1)}, bf16[112,1536]{1,0:T(8,128)(2,1)S(1)}, u32[]{:S(2)}, u32[]{:S(2)}) collective-permute-start(bf16[112,1536]{1,0:T(8,128)(2,1)S(1)} %get-tuple-element.336), channel_id=1, source_target_pairs={{0,4},{1,5},{4,8},{5,9},{8,12},{9,13},{12,14},{13,15},{14,10},{15,... | collective-permute-start | bytes 1032200 | tf_op jit(solution)/shard_map/ppermute | solution.py:103
  416.8 19.1 %collective-permute-start.67 = (bf16[112,1536]{1,0:T(8,128)(2,1)S(1)}, bf16[112,1536]{1,0:T(8,128)(2,1)S(1)}, u32[]{:S(2)}, u32[]{:S(2)}) collective-permute-start(bf16[112,1536]{1,0:T(8,128)(2,1)S(1)} %get-tuple-element.335), channel_id=1, source_target_pairs={{0,2},{1,3},{4,0},{5,1},{8,4},{9,5},{12,8},{13,9},{14,12},{15,13},... | collective-permute-start | bytes 1032200 | tf_op jit(solution)/shard_map/ppermute | solution.py:104
  478.2 19.5 %collective-permute-start.86 = (bf16[48,1536]{1,0:T(8,128)(2,1)S(1)}, bf16[48,1536]{1,0:T(8,128)(2,1)S(1)}, u32[]{:S(2)}, u32[]{:S(2)}) collective-permute-start(bf16[48,1536]{1,0:T(8,128)(2,1)S(1)} %select_convert_fusion.8), channel_id=1, source_target_pairs={{0,1},{1,0},{2,3},{3,2},{4,5},{5,4},{6,7},{7,6},{8,9},{9,8},{10,11... | collective-permute-start | bytes 442376 | tf_op jit(solution)/shard_map/ppermute | solution.py:34
  (193 other events, 2260.2 us)
